TPU v7x, 256 devices: a whole 4x4x8 slice. The times are simulated.
256 devices in a mesh: chan: 16 (over z, core), ctx: 16 (over x, y).
Axes of the slice: x: 4, y: 4, z: 8, core: 2. Of those that a mesh axis runs over, the one named last changes fastest.
Arguments:
- saved_input: float32 [2, 256, 131072], P(None, 'chan', 'ctx'), may hold values from -6 to 6
- out_grad: float32 [2, 256, 131072], P(None, 'chan', 'ctx'), may hold values from -6 to 6
- filters: float32 [2, 131072], P(None, 'ctx'), may hold values from -0.015625 to 0.015625
Outputs:
- input_grad: bfloat16 [2, 256, 131072], P(None, 'chan', 'ctx')
- filter_grad: float32 [2, 131072], P(None, 'ctx')
All inputs are finite; a program needn't handle non-finite values.
Results may differ from a plain program's by a relative error of at most 0.001.
Values sent between devices are 32-bit elements; how exact they have to be, the bound alone decides.
No kernel may reach another device: no remote copies, remote signals or barrier semaphores. Data moves between devices by JAX's collectives and lax.ppermute only.
A program may use at most 128 MiB of HBM per device.

v0:
```python
import math

import jax
import jax.numpy as jnp
from jax import lax
from jax.sharding import PartitionSpec as P

RADIX = 32


precise = lax.Precision.HIGHEST


def split_up(array, dim, size):
    before, after = (array.shape[:dim], array.shape[dim + 1 :])
    return jnp.moveaxis(array.reshape(*before, size, -1, *after), dim, 0)


def piece_ends(length, count):
    turn = length // count
    if turn >= 8:
        turn -= turn % 8
    return [turn * k for k in range(1, count)]


def joined_along(tiles, dim):
    shape = list(tiles.shape[1:])
    shape[dim] *= tiles.shape[0]
    return jnp.moveaxis(tiles, 0, dim).reshape(shape)


def exchange_in_pieces(array, axis, pieces, split_dim, concat_dim):
    tiles = split_up(array, split_dim, lax.axis_size(axis))
    cut = max(range(1, max(2, tiles.ndim - 1)), key=lambda d: tiles.shape[d])
    done = []
    for share in jnp.split(tiles, piece_ends(tiles.shape[cut], pieces), axis=cut):
        if share.size:
            done.append(lax.all_to_all(share, axis, split_axis=0, concat_axis=0, tiled=True))
    return joined_along(jnp.concatenate(done, axis=cut), concat_dim)


def copy_for_each(array, axis):
    size = lax.axis_size(axis)
    return lax.all_to_all(
        jnp.broadcast_to(array[None], (size, *array.shape)), axis, 0, 0, tiled=True
    )


def of_everyone(array, axis):
    everything = copy_for_each(array, axis)
    return jnp.sum(everything, axis=0)


def dft_tables(length, sign_value):
    positions = jnp.arange(length, dtype=jnp.int32)
    phases = positions[:, None] * positions[None, :] % length
    angles = 2.0 * math.pi / length * phases.astype(jnp.float32)
    return (jnp.cos(angles), sign_value * jnp.sin(angles))


def rotate(values, angles):
    cosine = jnp.cos(angles)
    sine_part = jnp.sin(angles)
    real_part = values[0] * cosine - values[1] * sine_part
    imag_part = values[0] * sine_part + values[1] * cosine
    return jnp.stack([real_part, imag_part])


def inner_angles(first_factor, second_factor, sign_value):
    period = first_factor * second_factor
    lefts = jnp.arange(first_factor, dtype=jnp.int32)[:, None]
    rights = jnp.arange(second_factor, dtype=jnp.int32)[None, :]
    phases = lefts * rights % period
    return sign_value * 2.0 * math.pi / period * phases.astype(jnp.float32)


def slot_frequency(slots, devices):
    owner = slots // 2
    parity = slots % 2
    return jnp.where(
        owner == 0, parity * devices, jnp.where(parity == 0, owner, 2 * devices - owner)
    )


def paired_angles(device, devices, tokens, sign_value):
    frequency = slot_frequency(2 * device + jnp.arange(2, dtype=jnp.int32), devices)[:, None]
    offsets = jnp.arange(tokens, dtype=jnp.int32)[None, :]
    period = 2 * devices * tokens
    phases = offsets * frequency % period
    return sign_value * 2.0 * math.pi / period * phases.astype(jnp.float32)


def complex_apply(form, cosine, sine_part, real_part, imag_part):
    new_real = jnp.einsum(form, real_part, cosine, precision=precise) - jnp.einsum(
        form, imag_part, sine_part, precision=precise
    )
    new_imag = jnp.einsum(form, real_part, sine_part, precision=precise) + jnp.einsum(
        form, imag_part, cosine, precision=precise
    )
    return jnp.stack([new_real, new_imag])


def local_forward(values, first_factor, second_factor):
    cosine, sine_part = dft_tables(first_factor, -1.0)
    sectioned = complex_apply("rpab,ak->rpbk", cosine, sine_part, values[0], values[1])
    sectioned = rotate(sectioned, inner_angles(first_factor, second_factor, -1.0).T)
    cosine, sine_part = dft_tables(second_factor, -1.0)
    return complex_apply("rpbk,bm->rpkm", cosine, sine_part, sectioned[0], sectioned[1])


def local_inverse(values, first_factor, second_factor):
    cosine, sine_part = dft_tables(second_factor, 1.0)
    sectioned = complex_apply("rpkm,mb->rpkb", cosine, sine_part, values[0], values[1])
    sectioned = rotate(sectioned, inner_angles(first_factor, second_factor, 1.0))
    cosine, sine_part = dft_tables(first_factor, 1.0)
    result = complex_apply("rpkb,ka->rpba", cosine, sine_part, sectioned[0], sectioned[1])
    return jnp.swapaxes(result, -1, -2)


def paired_kernel(devices):
    blocks = jnp.arange(devices, dtype=jnp.int32)[:, None]
    frequencies = slot_frequency(jnp.arange(2 * devices, dtype=jnp.int32), devices)[None, :]
    angles = math.pi / devices * (blocks * frequencies % (2 * devices)).astype(jnp.float32)
    cosine = jnp.cos(angles)
    sine_part = jnp.sin(angles)
    return jnp.stack(
        [jnp.stack([cosine, -sine_part], axis=1), jnp.stack([sine_part, cosine], axis=1)], axis=0
    )


def paired_back_kernel(devices):
    frequencies = slot_frequency(jnp.arange(2 * devices, dtype=jnp.int32), devices)[:, None]
    blocks = jnp.arange(devices, dtype=jnp.int32)[None, :]
    angles = math.pi / devices * (frequencies * blocks % (2 * devices)).astype(jnp.float32)
    cosine = jnp.cos(angles)
    sine_part = jnp.sin(angles)
    return jnp.stack(
        [jnp.stack([cosine, sine_part], axis=1), jnp.stack([-sine_part, cosine], axis=1)], axis=0
    )


def mirror_spectra(values, device, first_factor):
    flipped = jnp.flip(values, axis=(3, 4))
    swapped = flipped[:, :, ::-1]
    lowest = flipped[:, :, 0]
    moved = jnp.concatenate(
        [jnp.roll(lowest[:, :, first_factor - 1 :], 1, axis=3), lowest[:, :, : first_factor - 1]],
        axis=2,
    )
    own = jnp.stack([moved, flipped[:, :, 1]], axis=2)
    return jnp.where(device == 0, own, swapped)


def local(saved_input, out_grad, filters):
    batch_size, channels, tokens = saved_input.shape
    groups = filters.shape[0]
    devices = lax.axis_size("ctx")
    device = lax.axis_index("ctx")
    first_factor = RADIX
    second_factor = tokens // RADIX
    row_count = batch_size * channels
    half_rows = row_count // 2
    real_rows = jnp.concatenate([saved_input.reshape(row_count, tokens), filters[0::2]], axis=0)
    imag_rows = jnp.concatenate([out_grad.reshape(row_count, tokens), filters[1::2]], axis=0)
    packed_rows = row_count + groups // 2
    packed = jnp.stack([real_rows, imag_rows]).reshape(2, packed_rows, 1, tokens)
    columns = exchange_in_pieces(packed, "ctx", 2, 3, 2)
    mixed_part = jnp.einsum("cpxj,cxdu->dpuj", columns, paired_kernel(devices), precision=precise)
    values = lax.all_to_all(mixed_part, "ctx", split_axis=2, concat_axis=3, tiled=True)
    forward_turns = paired_angles(device, devices, tokens, -1.0)
    inverse_turns = paired_angles(device, devices, tokens, 1.0)
    values = rotate(values, forward_turns)
    rows_now = values.shape[1]
    values = local_forward(
        values.reshape(2, rows_now, 2, first_factor, second_factor), first_factor, second_factor
    )
    mirror = mirror_spectra(values, device, first_factor)
    first_part = jnp.stack([(values[0] + mirror[0]) * 0.5, (values[1] - mirror[1]) * 0.5])
    second_part = jnp.stack([(values[1] + mirror[1]) * 0.5, (mirror[0] - values[0]) * 0.5])
    filter_both = jnp.stack([first_part[:, row_count:], second_part[:, row_count:]], axis=2)
    filter_both = filter_both.reshape(2, groups, 2, first_factor, second_factor)
    values = jnp.concatenate(
        [first_part[:, :row_count], second_part[:, :row_count], filter_both], axis=1
    )
    per_filter = channels // groups
    spectrum_shape = (2, batch_size, per_filter, groups, 2, first_factor, second_factor)
    in_spec = values[:, :row_count].reshape(spectrum_shape)
    grad_spec = values[:, row_count : 2 * row_count].reshape(spectrum_shape)
    filter_spec = values[:, 2 * row_count :].reshape(
        2, 1, 1, groups, 2, first_factor, second_factor
    )
    input_spec = jnp.stack(
        [
            filter_spec[0] * grad_spec[0] + filter_spec[1] * grad_spec[1],
            filter_spec[0] * grad_spec[1] - filter_spec[1] * grad_spec[0],
        ]
    ).reshape(2, row_count, 2, first_factor, second_factor)
    filter_part = jnp.stack(
        [
            jnp.sum(in_spec[0] * grad_spec[0] + in_spec[1] * grad_spec[1], axis=(0, 1)),
            jnp.sum(in_spec[0] * grad_spec[1] - in_spec[1] * grad_spec[0], axis=(0, 1)),
        ]
    )
    joined = jnp.concatenate([input_spec, filter_part], axis=1)
    left_rows = jnp.concatenate([joined[:, :half_rows], joined[:, row_count::2]], axis=1)
    right_rows = jnp.concatenate(
        [joined[:, half_rows:row_count], joined[:, row_count + 1 :: 2]], axis=1
    )
    joined = jnp.stack([left_rows[0] - right_rows[1], left_rows[1] + right_rows[0]])
    rows_back = joined.shape[1]
    values = local_inverse(joined, first_factor, second_factor).reshape(2, rows_back, 2, tokens)
    values = rotate(values, inverse_turns)
    columns = exchange_in_pieces(values, "ctx", 2, 3, 2)
    restored = jnp.einsum(
        "cpuj,cudx->dpxj", columns, paired_back_kernel(devices), precision=precise
    )
    both_parts = lax.all_to_all(restored, "ctx", split_axis=2, concat_axis=3, tiled=True).reshape(
        2, rows_back, tokens
    )
    input_rows = jnp.concatenate([both_parts[0, :half_rows], both_parts[1, :half_rows]], axis=0)
    filter_rows = jnp.stack([both_parts[0, half_rows:], both_parts[1, half_rows:]], axis=1).reshape(
        groups, tokens
    )
    signal = jnp.concatenate([input_rows, filter_rows], axis=0)
    signal = signal * (1.0 / (2 * devices * tokens))
    input_grad = signal[:row_count].reshape(batch_size, channels, tokens).astype(jnp.bfloat16)
    filter_grad = signal[row_count:]
    filter_grad = of_everyone(filter_grad, "chan")
    norm_factor = float(tokens * devices * batch_size * per_filter * lax.axis_size("chan")) ** (
        -0.5
    )
    return (input_grad, filter_grad * norm_factor)


def solution(mesh):
    placed = (P(None, "chan", "ctx"), P(None, "chan", "ctx"), P(None, "ctx"))
    return jax.shard_map(
        local,
        mesh=mesh,
        in_specs=placed,
        out_specs=(P(None, "chan", "ctx"), P(None, "ctx")),
        check_vma=False,
    )
```

profile of v0, /device:TPU:1, one launch (start us, length us, event | category | flops | bytes accessed | tf_op | source)
XLA Modules:
  0.0 345.4 jit_solution(11764776496755780933)
XLA Ops:
  1.8 1.8 copy.157
  4.6 1.8 copy.124
  6.3 7.6 %all-to-all-start = ((f32[16,2,16,1,512]{4,1,2,3,0:T(2,128)}), f32[16,2,16,1,512]{4,1,2,3,0:T(2,128)S(1)}, u32[]{:S(2)}, u32[]{:S(2)}) async-start(f32[16,2,16,1,512]{4,1,2,3,0:T(2,128)} %copy.124), calls=%async_computation | async-start | bytes 2097152 | tf_op jit(solution)/shard_map/all_to_all | solution.py:38
  14.0 1.9 copy.125
  15.9 13.5 %all-to-all-done = f32[16,2,16,1,512]{4,1,2,3,0:T(2,128)S(1)} async-done(((f32[16,2,16,1,512]{4,1,2,3,0:T(2,128)}), f32[16,2,16,1,512]{4,1,2,3,0:T(2,128)S(1)}, u32[]{:S(2)}, u32[]{:S(2)}) %all-to-all-start) | async-done | bytes 1048608 | tf_op jit(solution)/shard_map/all_to_all | solution.py:38
  29.4 4.5 %all-to-all-start.1 = ((f32[16,2,17,1,512]{4,1,2,3,0:T(2,128)}), f32[16,2,17,1,512]{4,1,2,3,0:T(2,128)S(1)}, u32[]{:S(2)}, u32[]{:S(2)}) async-start(f32[16,2,17,1,512]{4,1,2,3,0:T(2,128)} %copy.125), calls=%async_computation.1 | async-start | bytes 2228224 | tf_op jit(solution)/shard_map/all_to_all | solution.py:38
  34.6 14.4 %all-to-all-done.1 = f32[16,2,17,1,512]{4,1,2,3,0:T(2,128)S(1)} async-done(((f32[16,2,17,1,512]{4,1,2,3,0:T(2,128)}), f32[16,2,17,1,512]{4,1,2,3,0:T(2,128)S(1)}, u32[]{:S(2)}, u32[]{:S(2)}) %all-to-all-start.1) | async-done | bytes 1114144 | tf_op jit(solution)/shard_map/all_to_all | solution.py:38
  49.2 3.7 %convolution_bitcast_fusion = f32[2,33,32,512]{3,2,1,0:T(8,128)S(1)} fusion(f32[16,2,17,1,512]{4,0,1,2,3:T(8,128)S(1)} %copy.127, f32[16,2,16,1,512]{4,0,1,2,3:T(8,128)S(1)} %copy.126, f32[1,16,2,32]{3,1,0,2:T(8,128)S(1)} %get-tuple-element.40, f32[1,16,2,32]{3,1,0,2:T(8,128)S(1)} %get-tuple-element.39), kind=kOutput, calls=%fused_computation.17 | convolution fusion | flops 415778816 | bytes 6496256 | tf_op jit(solution)/shard_map/cpxj,cxdu->dpuj/dot_general | solution.py:168
  52.9 5.4 %copy.128 = f32[2,33,32,512]{3,0,1,2:T(2,128)} copy(f32[2,33,32,512]{3,2,1,0:T(8,128)S(1)} %convolution_bitcast_fusion) | data formatting | bytes 8650752 | tf_op jit(solution)/shard_map/cpxj,cxdu->dpuj/transpose | solution.py:168
  58.3 5.5 %all-to-all-start.2 = ((f32[2,33,32,512]{3,0,1,2:T(2,128)}), f32[2,33,32,512]{3,0,1,2:T(2,128)}, u32[]{:S(2)}, u32[]{:S(2)}) async-start(f32[2,33,32,512]{3,0,1,2:T(2,128)} %copy.128), calls=%async_computation.2 | async-start | bytes 8650752 | tf_op jit(solution)/shard_map/all_to_all | solution.py:169
  64.8 50.8 %all-to-all-done.2 = f32[2,33,32,512]{3,0,1,2:T(2,128)} async-done(((f32[2,33,32,512]{3,0,1,2:T(2,128)}), f32[2,33,32,512]{3,0,1,2:T(2,128)}, u32[]{:S(2)}, u32[]{:S(2)}) %all-to-all-start.2) | async-done | bytes 4325408 | tf_op jit(solution)/shard_map/all_to_all | solution.py:169
  115.6 8.6 %fusion.209 = (f32[1,33,2,16,512]{4,0,1,2,3:T(1,128)S(1)}, f32[1,33,2,16,512]{4,0,1,2,3:T(1,128)}) fusion(f32[2,33,2,16,512]{4,0,1,2,3:T(2,128)} %bitcast.18), kind=kLoop, calls=%fused_computation.304 | loop fusion | bytes 8650752 | tf_op jit(solution)/shard_map/slice | solution.py:64
  124.3 1.8 copy.129
  126.0 2.3 squeeze.18
  128.3 3.4 copy.130
  131.7 3.2 squeeze.19
  134.9 4.0 %fusion.20 = f32[33,2,256,32]{2,3,1,0:T(8,128)S(1)} fusion(f32[33,2,32,256]{3,2,1,0:T(8,128)} %squeeze.19, f32[33,2,32,256]{3,2,1,0:T(8,128)S(1)} %squeeze.18, f32[2,32,256]{2,1,0:T(8,128)S(1)} %get-tuple-element.36, f32[2,32,256]{2,1,0:T(8,128)S(1)} %get-tuple-element.35), kind=kOutput, calls=%fused_computation.71 | convolution fusion | flops 209254400 | bytes 6619136 | tf_op jit(solution)/shard_map/rpab,ak->rpbk/dot_general | solution.py:94
  139.0 2.3 fusion.19
  141.3 2.3 convolution_subtract_fusion
  143.6 2.3 convolution_add_fusion
  145.9 3.4 fusion.18
  149.3 2.9 fusion.17
  152.3 3.0 convolution_subtract_fusion.1
  155.2 2.9 convolution_add_fusion.1
  158.2 2.6 fusion.2
  160.9 5.3 %slice.166 = f32[2,33,1,32,256]{4,3,1,0,2:T(8,128)} reverse(f32[2,33,1,32,256]{4,3,1,0,2:T(8,128)} %get-tuple-element.19), dimensions={3,4} | reverse | bytes 4325376 | tf_op jit(solution)/shard_map/slice | solution.py:145
  168.4 4.1 %pad_maximum_fusion = f32[2,33,2,32,256]{4,3,2,1,0:T(8,128)} fusion(f32[1,33,2,32,256]{4,3,2,1,0:T(8,128)} %bitcast.204, f32[1,33,2,32,256]{4,3,2,1,0:T(8,128)S(1)} %bitcast.202), kind=kLoop, calls=%fused_computation.2 | loop fusion | flops 1081344 | bytes 8650752 | tf_op jit(solution)/shard_map/stack | solution.py:100
  172.4 5.3 %slice.171 = f32[2,33,1,32,256]{4,3,2,1,0:T(8,128)} reverse(f32[2,33,1,32,256]{4,3,2,1,0:T(8,128)} %get-tuple-element.20), dimensions={3,4} | reverse | bytes 4325376 | tf_op jit(solution)/shard_map/slice | solution.py:150
  177.7 9.5 %rev.5 = f32[2,33,2,32,256]{4,3,2,1,0:T(8,128)} reverse(f32[2,33,2,32,256]{4,3,2,1,0:T(8,128)} %pad_maximum_fusion), dimensions={2,3,4} | reverse | bytes 8650752 | tf_op jit(solution)/shard_map/rev | solution.py:144
  187.3 2.0 maximum_bitcast_fusion.6
  190.1 4.7 %maximum_select_fusion = f32[2,33,2,32,256]{4,3,2,1,0:T(8,128)} fusion(f32[2,33,2,32,256]{4,3,2,1,0:T(8,128)S(1)} %copy-done.4, f32[2,33,1,32,256]{4,3,2,1,0:T(8,128)} %slice.171, f32[2,33,1,32,256]{4,3,2,1,0:T(8,128)S(1)} %maximum_bitcast_fusion.6, pred[]{:T(512)S(6)} %eq.97), kind=kLoop, calls=%fused_computation.5 | loop fusion | flops 2162688 | bytes 12976129 | tf_op jit(solution)/shard_map/jit(_where)/select_n | solution.py:151
  194.9 6.4 %fusion.13 = (f32[1,33,2,32,256]{4,3,2,1,0:T(8,128)}, f32[1,33,2,32,256]{4,3,2,0,1:T(8,128)S(1)}, f32[1,33,2,32,256]{4,3,2,1,0:T(8,128)S(1)}, f32[1,33,2,32,256]...) fusion(f32[33,2,32,256]{3,2,1,0:T(8,128)S(1)} %copy-done.2, ...), kind=kLoop, calls=%fused_computation.64 | loop fusion | flops 4325376 | bytes 21626880 | tf_op jit(solution)/shard_map/stack | solution.py:179
  205.8 7.4 %multiply_subtract_fusion.2 = (f32[1,32,2,32,256]{4,3,2,1,0:T(8,128)}, f32[1,32,2,32,256]{4,3,2,1,0:T(8,128)}, f32[1,32,2,32,256]{4,3,2,1,0:T(8,128)S(1)}, f32[1,32,2,32,256]{4,3,2,1,0:T(8,128)}) fusion(f32[1,33,2,32,256]{4,3,2,1,0:T(8,128)S(1)} %get-tuple-element.10, f32[1,33,2,32,256]{4,3,2,1,0:T(8,128)S(1)} %get-tuple-element.16, ...), kind=kLoop, calls=%fused_computation.37 | loop fusion | flops 6291456 | bytes 20971520 | tf_op jit(solution)/shard_map/sub | solution.py:201
  218.8 2.0 fusion.30
  220.8 2.0 fusion.26
  222.9 2.3 convolution_subtract_fusion.2
  225.2 2.0 convolution_add_fusion.2
  234.0 1.8 copy.134
  235.8 6.0 %all-to-all-start.3 = ((f32[16,2,8,2,512]{4,3,2,1,0:T(2,128)}), f32[16,2,8,2,512]{4,3,2,1,0:T(2,128)S(1)}, u32[]{:S(2)}, u32[]{:S(2)}) async-start(f32[16,2,8,2,512]{4,3,2,1,0:T(2,128)} %copy.134), calls=%async_computation.3 | async-start | bytes 2097152 | tf_op jit(solution)/shard_map/all_to_all | solution.py:38
  241.9 1.9 copy.135
  243.8 10.2 %all-to-all-done.3 = f32[16,2,8,2,512]{4,3,2,1,0:T(2,128)S(1)} async-done(((f32[16,2,8,2,512]{4,3,2,1,0:T(2,128)}), f32[16,2,8,2,512]{4,3,2,1,0:T(2,128)S(1)}, u32[]{:S(2)}, u32[]{:S(2)}) %all-to-all-start.3) | async-done | bytes 1048608 | tf_op jit(solution)/shard_map/all_to_all | solution.py:38
  254.0 4.4 %all-to-all-start.4 = ((f32[16,2,9,2,512]{4,3,2,1,0:T(2,128)}), f32[16,2,9,2,512]{4,3,2,1,0:T(2,128)S(1)}, u32[]{:S(2)}, u32[]{:S(2)}) async-start(f32[16,2,9,2,512]{4,3,2,1,0:T(2,128)} %copy.135), calls=%async_computation.4 | async-start | bytes 2359296 | tf_op jit(solution)/shard_map/all_to_all | solution.py:38
  258.6 12.7 %all-to-all-done.4 = f32[16,2,9,2,512]{4,3,2,1,0:T(2,128)S(1)} async-done(((f32[16,2,9,2,512]{4,3,2,1,0:T(2,128)}), f32[16,2,9,2,512]{4,3,2,1,0:T(2,128)S(1)}, u32[]{:S(2)}, u32[]{:S(2)}) %all-to-all-start.4) | async-done | bytes 1179680 | tf_op jit(solution)/shard_map/all_to_all | solution.py:38
  272.3 2.6 copy.136
  274.9 3.0 reshape.661
  280.0 16.2 %all_to_all.49 = f32[2,17,16,512]{3,0,1,2:T(2,128)S(1)} all-to-all(f32[2,17,16,512]{3,0,1,2:T(2,128)S(1)} %copy.137), channel_id=1, replica_groups=mesh['chan'=16,'ctx'=16] {'ctx'}, dimensions={2} | all-to-all | bytes 2228224 | tf_op jit(solution)/shard_map/all_to_all | solution.py:217
  300.2 15.7 %all-to-all-start.6 = ((f32[16,2,8192]{2,1,0:T(2,128)}), f32[16,2,8192]{2,1,0:T(2,128)S(1)}, u32[]{:S(2)}, u32[]{:S(2)}) async-start(f32[16,2,8192]{2,1,0:T(2,128)} %broadcast_in_dim.2), calls=%async_computation.6 | async-start | bytes 2097152 | tf_op jit(solution)/shard_map/all_to_all | solution.py:44
  316.8 27.1 %all-to-all-done.6 = f32[16,2,8192]{2,1,0:T(2,128)S(1)} async-done(((f32[16,2,8192]{2,1,0:T(2,128)}), f32[16,2,8192]{2,1,0:T(2,128)S(1)}, u32[]{:S(2)}, u32[]{:S(2)}) %all-to-all-start.6) | async-done | bytes 1048608 | tf_op jit(solution)/shard_map/all_to_all | solution.py:44
  (77 shorter events, 32.9 us)
Async XLA Ops:
  0.6 3.0 copy-start.7
  6.3 23.1 %all-to-all-start = ((f32[16,2,16,1,512]{4,1,2,3,0:T(2,128)}), f32[16,2,16,1,512]{4,1,2,3,0:T(2,128)S(1)}, u32[]{:S(2)}, u32[]{:S(2)}) async-start(f32[16,2,16,1,512]{4,1,2,3,0:T(2,128)} %copy.124), calls=%async_computation | async-start | bytes 2097152 | tf_op jit(solution)/shard_map/all_to_all | solution.py:38
  29.4 19.6 %all-to-all-start.1 = ((f32[16,2,17,1,512]{4,1,2,3,0:T(2,128)}), f32[16,2,17,1,512]{4,1,2,3,0:T(2,128)S(1)}, u32[]{:S(2)}, u32[]{:S(2)}) async-start(f32[16,2,17,1,512]{4,1,2,3,0:T(2,128)} %copy.125), calls=%async_computation.1 | async-start | bytes 2228224 | tf_op jit(solution)/shard_map/all_to_all | solution.py:38
  58.3 57.3 %all-to-all-start.2 = ((f32[2,33,32,512]{3,0,1,2:T(2,128)}), f32[2,33,32,512]{3,0,1,2:T(2,128)}, u32[]{:S(2)}, u32[]{:S(2)}) async-start(f32[2,33,32,512]{3,0,1,2:T(2,128)} %copy.128), calls=%async_computation.2 | async-start | bytes 8650752 | tf_op jit(solution)/shard_map/all_to_all | solution.py:169
  134.9 4.0 %copy-start = (f32[33,2,32,256]{3,2,1,0:T(8,128)S(1)}, f32[33,2,32,256]{3,2,1,0:T(8,128)}, u32[]{:S(2)}) copy-start(f32[33,2,32,256]{3,2,1,0:T(8,128)} %squeeze.19) | copy-start | bytes 6488068
  158.1 2.7 copy-start.1
  187.2 2.9 copy-start.4
  190.1 4.7 %copy-start.2 = (f32[33,2,32,256]{3,2,1,0:T(8,128)S(1)}, f32[33,2,32,256]{3,2,1,0:T(8,128)}, u32[]{:S(2)}) copy-start(f32[33,2,32,256]{3,2,1,0:T(8,128)} %copy-done.1) | copy-start | bytes 6488068
  202.2 3.2 copy-start.5
  202.2 3.6 %copy-start.6 = (f32[1,33,2,32,256]{4,3,2,1,0:T(8,128)S(1)}, f32[1,33,2,32,256]{4,3,2,1,0:T(8,128)}, u32[]{:S(2)}) copy-start(f32[1,33,2,32,256]{4,3,2,1,0:T(8,128)} %get-tuple-element.18) | copy-start | bytes 6488068
  216.7 1.9 copy-start.3
  235.8 18.2 %all-to-all-start.3 = ((f32[16,2,8,2,512]{4,3,2,1,0:T(2,128)}), f32[16,2,8,2,512]{4,3,2,1,0:T(2,128)S(1)}, u32[]{:S(2)}, u32[]{:S(2)}) async-start(f32[16,2,8,2,512]{4,3,2,1,0:T(2,128)} %copy.134), calls=%async_computation.3 | async-start | bytes 2097152 | tf_op jit(solution)/shard_map/all_to_all | solution.py:38
  254.0 17.3 %all-to-all-start.4 = ((f32[16,2,9,2,512]{4,3,2,1,0:T(2,128)}), f32[16,2,9,2,512]{4,3,2,1,0:T(2,128)S(1)}, u32[]{:S(2)}, u32[]{:S(2)}) async-start(f32[16,2,9,2,512]{4,3,2,1,0:T(2,128)} %copy.135), calls=%async_computation.4 | async-start | bytes 2359296 | tf_op jit(solution)/shard_map/all_to_all | solution.py:38
  300.2 43.7 %all-to-all-start.6 = ((f32[16,2,8192]{2,1,0:T(2,128)}), f32[16,2,8192]{2,1,0:T(2,128)S(1)}, u32[]{:S(2)}, u32[]{:S(2)}) async-start(f32[16,2,8192]{2,1,0:T(2,128)} %broadcast_in_dim.2), calls=%async_computation.6 | async-start | bytes 2097152 | tf_op jit(solution)/shard_map/all_to_all | solution.py:44
where the time goes:
time: 351 us; the launch traced here: 345 us
  waiting for transfers between devices  129 us (37%)
  local copies, waits for them, and re-layouts  76 us (22%)
  starting transfers between devices  43.7 us (12%)
  matrix products  41.5 us (12%)
  other arithmetic  37.7 us (11%)
  blocking collectives  16.2 us (5%)
    all_to_all x4, waiting for transfers between devices, exchange_in_pieces(): lax.all_to_all(share, axis, split_axis=0, concat_axis=0, tiled=True)  50.8 us
    all_to_all x1, waiting for transfers between devices, local(): lax.all_to_all(mixed_part, 'ctx', split_axis=2, concat_axis=3, tiled=True)  50.8 us
    all_to_all x1, waiting for transfers between devices, copy_for_each(): lax.all_to_all(jnp.broadcast_to(array[None], (size, *array.shape)), axis,...  27.1 us
    all_to_all x4, starting transfers between devices, exchange_in_pieces(): lax.all_to_all(share, axis, split_axis=0, concat_axis=0, tiled=True)  22.5 us
    all_to_all x1, blocking collectives, local(): lax.all_to_all(restored, 'ctx', split_axis=2, concat_axis=3, tiled=True)  16.2 us
    all_to_all x1, starting transfers between devices, copy_for_each(): lax.all_to_all(jnp.broadcast_to(array[None], (size, *array.shape)), axis,...  15.7 us
    slice x4, local copies, waits for them, and re-layouts, rotate(): real_part = values[0] * cosine - values[1] * sine_part  13.9 us
    dot_general x4, matrix products, complex_apply(): jnp.einsum(form, real_part, cosine, precision=precise)  10.7 us
  transfers between devices with their start and end apart: 6, of which 6 were waited for; matrix products, arithmetic and copies ran while one was open for 2% of the time, Pallas kernels for 0%

commit v1 on v0

v1 whole, which is shorter than its diff:
```python
import functools
import math

import jax
import jax.numpy as jnp
import ml_dtypes
import numpy as np
from jax import lax
from jax.experimental import pallas as pl
from jax.experimental.pallas import tpu as pltpu
from jax.sharding import PartitionSpec as P

RADIX = 8
SIDE = 128
TOKENS = RADIX * SIDE * SIDE
LANES = 128
STEP = 16


def real_form(matrix):
    return np.block([[matrix.real, -matrix.imag], [matrix.imag, matrix.real]])


def two_halves(matrix):
    high = matrix.astype(ml_dtypes.bfloat16)
    low = (matrix - high.astype(np.float64)).astype(ml_dtypes.bfloat16)
    return np.stack([high, low])


@functools.cache
def tables():
    q = np.arange(RADIX)[:, None, None]
    first = np.arange(SIDE)[None, :, None]
    second = np.arange(SIDE)[None, None, :]
    turn = np.pi / 16 + np.pi * q / 4 + 2 * np.pi * first
    over_s = np.exp(1j * second * turn / SIDE)
    twiddle = np.exp(1j * second * turn / (SIDE * SIDE))
    over_l = np.exp(2j * np.pi * np.outer(np.arange(SIDE), np.arange(SIDE)) / SIDE)
    forward_s = np.stack([two_halves(real_form(m)) for m in over_s])
    inverse_s = np.stack([two_halves(real_form(m).T) for m in over_s])
    forward_l = two_halves(real_form(over_l).T)
    inverse_l = two_halves(real_form(over_l))
    turns = np.stack([twiddle.real, twiddle.imag], axis=1).astype(np.float32)
    return forward_s, inverse_s, forward_l, inverse_l, turns


def dft4(a, b, c, d, sign):
    t0 = (a[0] + c[0], a[1] + c[1])
    t1 = (a[0] - c[0], a[1] - c[1])
    t2 = (b[0] + d[0], b[1] + d[1])
    t3 = (b[0] - d[0], b[1] - d[1])
    if sign < 0:
        t3 = (-t3[0], -t3[1])
    return [
        (t0[0] + t2[0], t0[1] + t2[1]),
        (t1[0] - t3[1], t1[1] + t3[0]),
        (t0[0] - t2[0], t0[1] - t2[1]),
        (t1[0] + t3[1], t1[1] - t3[0]),
    ]


def dft8(u, sign):
    even = dft4(u[0], u[2], u[4], u[6], sign)
    odd = dft4(u[1], u[3], u[5], u[7], sign)
    half = math.sqrt(0.5)
    turned = [
        odd[0],
        (half * (odd[1][0] - sign * odd[1][1]), half * (odd[1][1] + sign * odd[1][0])),
        (-sign * odd[2][1], sign * odd[2][0]),
        (half * (-odd[3][0] - sign * odd[3][1]), half * (sign * odd[3][0] - odd[3][1])),
    ]
    plus = [(e[0] + o[0], e[1] + o[1]) for e, o in zip(even, turned)]
    minus = [(e[0] - o[0], e[1] - o[1]) for e, o in zip(even, turned)]
    return plus + minus


def split(values):
    high = values.astype(jnp.bfloat16)
    low = (values - high.astype(jnp.float32)).astype(jnp.bfloat16)
    return high, low


def dot(left, right):
    return jnp.dot(left, right, preferred_element_type=jnp.float32)


def dot_from_left(table_high, table_low, high, low):
    return dot(table_high, high) + dot(table_high, low) + dot(table_low, high)


def dot_from_right(high, low, table_high, table_low):
    return dot(high, table_high) + dot(low, table_high) + dot(high, table_low)


def radix_forward(rows_ref, first_row, count, high_ref, low_ref):
    per_block = rows_ref.shape[2] // STEP

    def body(step, carry):
        odd_half = step // per_block
        inner = pl.multiple_of((step % per_block) * STEP, STEP)
        target = pl.multiple_of(step * STEP, STEP)
        for row in range(count):
            u = []
            for r in range(RADIX):
                x = rows_ref[2 * r + odd_half, first_row + row, pl.ds(inner, STEP), :]
                angle = math.pi * r / 16
                u.append((math.cos(angle) * x, math.sin(angle) * x) if r else (x, jnp.zeros_like(x)))
            for q, value in enumerate(dft8(u, 1)):
                for part in range(2):
                    high, low = split(value[part])
                    lanes = pl.ds(row * LANES, LANES)
                    high_ref[q, part, pl.ds(target, STEP), lanes] = high
                    low_ref[q, part, pl.ds(target, STEP), lanes] = low
        return carry

    lax.fori_loop(0, SIDE // STEP, body, 0)


def radix_inverse(values_ref, count, store):
    per_block = SIDE // 2 // STEP

    def body(step, carry):
        odd_half = step // per_block
        inner = pl.multiple_of((step % per_block) * STEP, STEP)
        source = pl.multiple_of(step * STEP, STEP)
        for row in range(count):
            lanes = pl.ds(row * LANES, LANES)
            v = [
                tuple(values_ref[q, part, pl.ds(source, STEP), lanes] for part in range(2))
                for q in range(RADIX)
            ]
            for r, value in enumerate(dft8(v, -1)):
                angle = math.pi * r / 16
                real = math.cos(angle) * value[0] + math.sin(angle) * value[1] if r else value[0]
                store(2 * r + odd_half, row, pl.ds(inner, STEP), real)
        return carry

    lax.fori_loop(0, SIDE // STEP, body, 0)


def spectra_of(q, count, high_ref, low_ref, forward_s, forward_l, turns):
    high = high_ref[q].reshape(2 * SIDE, count * LANES)
    low = low_ref[q].reshape(2 * SIDE, count * LANES)
    z = dot_from_left(forward_s[q, 0], forward_s[q, 1], high, low)
    cosine, sine = turns[q, 0], turns[q, 1]
    rows = []
    for row in range(count):
        real = z[:SIDE, row * LANES : (row + 1) * LANES]
        imag = z[SIDE:, row * LANES : (row + 1) * LANES]
        rows.append(
            jnp.concatenate([real * cosine - imag * sine, real * sine + imag * cosine], axis=1)
        )
    high, low = split(jnp.concatenate(rows, axis=0))
    return dot_from_right(high, low, forward_l[0], forward_l[1])


def back_to_s(q, count, products, inverse_s, inverse_l, turns):
    high, low = split(products)
    u = dot_from_right(high, low, inverse_l[0], inverse_l[1])
    cosine, sine = turns[q, 0], turns[q, 1]
    rows = []
    for row in range(count):
        real = u[row * SIDE : (row + 1) * SIDE, :LANES]
        imag = u[row * SIDE : (row + 1) * SIDE, LANES:]
        rows.append(
            jnp.concatenate([real * cosine + imag * sine, imag * cosine - real * sine], axis=0)
        )
    high, low = split(jnp.concatenate(rows, axis=1))
    return dot_from_left(inverse_s[q, 0], inverse_s[q, 1], high, low)


def times_conjugate(a, b):
    ar, ai, br, bi = a[:, :LANES], a[:, LANES:], b[:, :LANES], b[:, LANES:]
    return ar * br + ai * bi, ai * br - ar * bi


def filter_kernel(
    rows, forward_s, inverse_s, forward_l, inverse_l, turns, terms, grads, high, low, back
):
    radix_forward(rows, 0, 4, high, low)

    def body(q, carry):
        spectra = spectra_of(q, 4, high, low, forward_s, forward_l, turns)
        grads[q] = spectra[2 * SIDE :]
        first = times_conjugate(spectra[2 * SIDE : 3 * SIDE], spectra[:SIDE])
        second = times_conjugate(spectra[3 * SIDE :], spectra[SIDE : 2 * SIDE])
        products = jnp.concatenate([first[0] + second[0], first[1] + second[1]], axis=1)
        out = back_to_s(q, 1, products, inverse_s, inverse_l, turns)
        back[q] = out.reshape(2, SIDE, LANES)
        return carry

    lax.fori_loop(0, RADIX, body, 0)

    def store(block, row, span, value):
        terms[block, span, :] = value

    radix_inverse(back, 1, store)


def input_kernel(
    rows, grads, forward_s, inverse_s, forward_l, inverse_l, turns, out, high, low, back
):
    radix_forward(rows, 4, 1, high, low)

    def body(q, carry):
        spectrum = spectra_of(q, 1, high, low, forward_s, forward_l, turns)
        products = jnp.concatenate(
            [
                jnp.concatenate(times_conjugate(grads[q, b * SIDE : (b + 1) * SIDE], spectrum), axis=1)
                for b in range(2)
            ],
            axis=0,
        )
        values = back_to_s(q, 2, products, inverse_s, inverse_l, turns)
        back[q] = values.reshape(2, SIDE, 2 * LANES)
        return carry

    lax.fori_loop(0, RADIX, body, 0)

    def store(block, row, span, value):
        out[block, row, span, :] = value

    radix_inverse(back, 2, store)


def in_vmem(count):
    return [pl.BlockSpec(memory_space=pltpu.VMEM)] * count


def scratch(rows_in, rows_back):
    return [
        pltpu.VMEM((RADIX, 2, SIDE, rows_in * LANES), jnp.bfloat16),
        pltpu.VMEM((RADIX, 2, SIDE, rows_in * LANES), jnp.bfloat16),
        pltpu.VMEM((RADIX, 2, SIDE, rows_back * LANES), jnp.float32),
    ]


def filter_terms(rows, consts):
    blocks = rows.shape[0]
    return pl.pallas_call(
        filter_kernel,
        out_shape=(
            jax.ShapeDtypeStruct((blocks, rows.shape[2], LANES), jnp.float32),
            jax.ShapeDtypeStruct((RADIX, 2 * SIDE, 2 * LANES), jnp.float32),
        ),
        in_specs=in_vmem(6),
        out_specs=tuple(in_vmem(2)),
        scratch_shapes=scratch(4, 1),
        compiler_params=pltpu.CompilerParams(vmem_limit_bytes=28 << 20),
        cost_estimate=pl.CostEstimate(
            flops=4_000_000_000, bytes_accessed=10_000_000, transcendentals=0
        ),
        name="filter_terms",
    )(rows, *consts)


def input_rows(rows, grads, consts):
    blocks = rows.shape[0]
    return pl.pallas_call(
        input_kernel,
        out_shape=jax.ShapeDtypeStruct((blocks, 2, rows.shape[2], LANES), jnp.float32),
        in_specs=in_vmem(7),
        out_specs=in_vmem(1)[0],
        scratch_shapes=scratch(1, 2),
        compiler_params=pltpu.CompilerParams(vmem_limit_bytes=28 << 20),
        cost_estimate=pl.CostEstimate(
            flops=2_500_000_000, bytes_accessed=10_000_000, transcendentals=0
        ),
        name="input_rows",
    )(rows, grads, *consts)


def local(saved_input, out_grad, filters):
    batch, channels, tokens = saved_input.shape
    groups = filters.shape[0]
    devices = lax.axis_size("ctx")
    chan = lax.axis_size("chan")
    chunks = tokens // LANES
    consts = tuple(jnp.asarray(t) for t in tables())
    shape = (batch, channels, chunks, LANES)
    by_channel = [jnp.swapaxes(v.reshape(shape), 0, 1) for v in (saved_input, out_grad)]
    own_filter = jnp.tile(filters.reshape(groups, 1, chunks, LANES), (channels // groups, 1, 1, 1))
    packed = jnp.concatenate([*by_channel, own_filter], axis=1)
    rows = lax.all_to_all(packed, "ctx", 0, 0, tiled=True)
    terms, grads = filter_terms(rows, consts)
    terms = lax.all_to_all(terms, "ctx", 0, 0, tiled=True)
    inputs = input_rows(rows, grads, consts)
    total = jnp.sum(terms.reshape(devices // groups, groups, chunks, LANES), axis=0)
    inputs, total = lax.optimization_barrier((inputs, total))
    inputs = lax.all_to_all(inputs, "ctx", 0, 0, tiled=True)
    hop = 1
    while hop < chan:
        total = total + lax.ppermute(total, "chan", [(i, i ^ hop) for i in range(chan)])
        hop *= 2
    per_filter = channels // groups
    norm = float(tokens * devices * batch * per_filter * chan) ** -0.5
    filter_grad = total.reshape(groups, tokens) * (norm / TOKENS)
    input_grad = jnp.swapaxes(inputs * (1.0 / TOKENS), 0, 1).reshape(batch, channels, tokens)
    return input_grad.astype(jnp.bfloat16), filter_grad


def solution(mesh):
    placed = (P(None, "chan", "ctx"), P(None, "chan", "ctx"), P(None, "ctx"))
    return jax.shard_map(
        local,
        mesh=mesh,
        in_specs=placed,
        out_specs=(P(None, "chan", "ctx"), P(None, "ctx")),
        check_vma=False,
    )
```

time: 351 us -> 113 us (0.32)
  the two profiles are of different devices: /device:TPU:1 before, /device:TPU:2 now
where the time goes in v1:
time: 113 us
  blocking collectives  39.7 us (35%)
  starting transfers between devices  25.4 us (22%)
  Pallas kernels  23.4 us (21%)
  local copies, waits for them, and re-layouts  13.1 us (12%)
  waiting for transfers between devices  8.77 us (8%)
  other arithmetic  1.56 us (1%)
    all_to_all x1, blocking collectives, local(): rows = lax.all_to_all(packed, 'ctx', 0, 0, tiled=True)  39.7 us
    pallas_call x1, Pallas kernels, filter_terms(): pl.pallas_call(filter_kernel, out_shape=(jax.ShapeDtypeStruct((blocks, ro...  13.5 us
    unnamed x29, local copies, waits for them, and re-layouts  12.6 us
    ppermute x4, starting transfers between devices, local(): lax.ppermute(total, 'chan', [(i, i ^ hop) for i in range(chan)])  12.4 us
    pallas_call x1, Pallas kernels, input_rows(): pl.pallas_call(input_kernel, out_shape=jax.ShapeDtypeStruct((blocks, 2, r...  9.89 us
    ppermute x4, waiting for transfers between devices, local(): lax.ppermute(total, 'chan', [(i, i ^ hop) for i in range(chan)])  8.76 us
    all_to_all x1, starting transfers between devices, local(): inputs = lax.all_to_all(inputs, 'ctx', 0, 0, tiled=True)  7.28 us
    all_to_all x1, starting transfers between devices, local(): terms = lax.all_to_all(terms, 'ctx', 0, 0, tiled=True)  5.73 us
  transfers between devices with their start and end apart: 6, of which 4 were waited for; matrix products, arithmetic and copies ran while one was open for 1% of the time, Pallas kernels for 9%

profile of v1, /device:TPU:2, one launch (start us, length us, event | category | flops | bytes accessed | tf_op | source)
XLA Modules:
  0.0 112.7 jit_solution(15774281653419824353)
XLA Ops:
  0.6 0.0 copy-start.11
  0.6 0.9 copy.24
  1.6 1.4 %copy.15 = f32[4,8,64,128]{3,2,1,0:T(8,128)S(1)} copy(f32[4,8,64,128]{3,1,2,0:T(8,128)} %bitcast.40) | data formatting | bytes 2097152
  3.0 0.0 copy-done.11
  3.0 0.2 copy.16
  3.2 0.2 copy_bitcast_fusion
  3.4 0.1 tile.11
  3.5 0.0 copy-start.9
  3.5 0.0 copy-start.10
  3.5 0.3 pad_maximum_fusion
  3.9 0.0 copy-start.1
  3.9 0.0 copy-start.3
  3.9 0.0 copy-start.7
  3.9 39.7 %all_to_all.15.rows = f32[16,5,64,128]{3,2,1,0:T(8,128)S(1)} all-to-all(f32[16,5,64,128]{3,2,1,0:T(8,128)S(1)} %pad_maximum_fusion), channel_id=1, replica_groups=mesh['chan'=16,'ctx'=16] {'ctx'}, dimensions={0} | all-to-all | bytes 5242880 | tf_op jit(solution)/shard_map/all_to_all | solution.py:284
  43.6 0.0 copy-done.9
  43.6 0.0 copy-done.10
  43.6 0.0 copy-done.1
  43.6 0.0 copy-done.3
  43.7 0.0 copy-done.7
  43.7 13.5 %filter_terms.1 = (f32[16,64,128]{2,1,0:T(8,128)}, f32[8,256,256]{2,1,0:T(8,128)S(1)}) custom-call(f32[16,5,64,128]{3,2,1,0:T(8,128)S(1)} %all_to_all.15.rows, bf16[8,2,256,256]{3,2,1,0:T(8,128)(2,1)S(1)} %copy-done.3, bf16[8,2,256,256]{3,2,1,0:T(8,128)(2,1)S(1)} %copy-done.1, bf16[2,256,256]{2,1,0:T(8,128)(2,1)S(1)} %copy-done.10, ...), custom_call_target="tpu_custom_call" | custom-call | flops 4000000000 | bytes 10000000 | tf_op jit(solution)/shard_map/filter_terms/pallas_call | solution.py:240
  57.1 0.0 copy-start.5
  57.1 1.3 %copy-done.5 = f32[8,256,256]{2,1,0:T(8,128)} copy-done((f32[8,256,256]{2,1,0:T(8,128)}, f32[8,256,256]{2,1,0:T(8,128)S(1)}, u32[]{:S(2)}) %copy-start.5) | copy-done | bytes 2097176
  58.5 5.7 %all-to-all-start.1 = ((f32[16,64,128]{2,1,0:T(8,128)}), f32[16,64,128]{2,1,0:T(8,128)}, u32[]{:S(2)}, u32[]{:S(2)}) async-start(f32[16,64,128]{2,1,0:T(8,128)} %get-tuple-element.7), calls=%async_computation.1 | async-start | bytes 1048576 | tf_op jit(solution)/shard_map/all_to_all | solution.py:286
  64.2 0.0 copy-start.2
  64.2 1.6 %copy-done.2 = bf16[8,2,256,256]{3,2,1,0:T(8,128)(2,1)S(1)} copy-done((bf16[8,2,256,256]{3,2,1,0:T(8,128)(2,1)S(1)}, bf16[8,2,256,256]{3,2,1,0:T(8,128)(2,1)}, u32[]{:S(2)}) %copy-start.2) | copy-done | bytes 2097176
  65.8 0.0 copy-start.4
  65.8 1.6 %copy-done.4 = bf16[8,2,256,256]{3,2,1,0:T(8,128)(2,1)S(1)} copy-done((bf16[8,2,256,256]{3,2,1,0:T(8,128)(2,1)S(1)}, bf16[8,2,256,256]{3,2,1,0:T(8,128)(2,1)}, u32[]{:S(2)}) %copy-start.4) | copy-done | bytes 2097176
  67.4 1.6 %copy-done.6 = f32[8,256,256]{2,1,0:T(8,128)S(1)} copy-done((f32[8,256,256]{2,1,0:T(8,128)S(1)}, f32[8,256,256]{2,1,0:T(8,128)}, u32[]{:S(2)}) %copy-start.6) | copy-done | bytes 2097176
  69.0 1.2 %copy-done.8 = f32[8,2,128,128]{3,2,1,0:T(8,128)S(1)} copy-done((f32[8,2,128,128]{3,2,1,0:T(8,128)S(1)}, f32[8,2,128,128]{3,2,1,0:T(8,128)}, u32[]{:S(2)}) %copy-start.8) | copy-done | bytes 1048600
  70.2 9.9 %input_rows.1 = f32[16,2,64,128]{3,2,1,0:T(8,128)S(1)} custom-call(f32[16,5,64,128]{3,2,1,0:T(8,128)S(1)} %all_to_all.15.rows, f32[8,256,256]{2,1,0:T(8,128)S(1)} %copy-done.6, bf16[8,2,256,256]{3,2,1,0:T(8,128)(2,1)S(1)} %copy-done.4, bf16[8,2,256,256]{3,2,1,0:T(8,128)(2,1)S(1)} %copy-done.2, bf16[2,256,256]{2,1,0:T(8,128)(2,1)S(1)} %copy-done.10, ...), custom_call_target="tpu_custom_call" | custom-call | flops 2500000000 | bytes 10000000 | tf_op jit(solution)/shard_map/input_rows/pallas_call | solution.py:259
  80.1 0.0 copy-start
  80.1 1.0 copy-done
  81.1 0.0 all-to-all-done.1
  81.1 1.1 reduce_sum.9
  82.2 7.3 %all-to-all-start.2 = ((f32[16,2,64,128]{3,2,1,0:T(8,128)}), f32[16,2,64,128]{3,2,1,0:T(8,128)S(1)}, u32[]{:S(2)}, u32[]{:S(2)}) async-start(f32[16,2,64,128]{3,2,1,0:T(8,128)} %copy-done), calls=%async_computation.2 | async-start | bytes 2097152 | tf_op jit(solution)/shard_map/all_to_all | solution.py:290
  89.4 0.0 collective-permute-start
  89.5 1.2 %collective-permute-done = f32[2,64,128]{2,1,0:T(8,128)S(1)} collective-permute-done((f32[2,64,128]{2,1,0:T(8,128)S(1)}, f32[2,64,128]{2,1,0:T(8,128)S(1)}, u32[]{:S(2)}, u32[]{:S(2)}) %collective-permute-start) | collective-permute-done | bytes 65568 | tf_op jit(solution)/shard_map/ppermute | solution.py:293
  90.7 2.0 %collective-permute-start.1 = (f32[2,64,128]{2,1,0:T(8,128)S(1)}, f32[2,64,128]{2,1,0:T(8,128)S(1)}, u32[]{:S(2)}, u32[]{:S(2)}) collective-permute-start(f32[2,64,128]{2,1,0:T(8,128)S(1)} %add.12), channel_id=1, source_target_pairs={{0,32},{16,48},{32,0},{48,16},{64,96},{80,112},{96,64},{112,80},{1... | collective-permute-start | bytes 196616 | tf_op jit(solution)/shard_map/ppermute | solution.py:293
  92.7 2.4 %collective-permute-done.1 = f32[2,64,128]{2,1,0:T(8,128)S(1)} collective-permute-done((f32[2,64,128]{2,1,0:T(8,128)S(1)}, f32[2,64,128]{2,1,0:T(8,128)S(1)}, u32[]{:S(2)}, u32[]{:S(2)}) %collective-permute-start.1) | collective-permute-done | bytes 65568 | tf_op jit(solution)/shard_map/ppermute | solution.py:293
  95.2 3.4 %collective-permute-start.2 = (f32[2,64,128]{2,1,0:T(8,128)S(1)}, f32[2,64,128]{2,1,0:T(8,128)S(1)}, u32[]{:S(2)}, u32[]{:S(2)}) collective-permute-start(f32[2,64,128]{2,1,0:T(8,128)S(1)} %add.13), channel_id=1, source_target_pairs={{0,64},{16,80},{32,96},{48,112},{64,0},{80,16},{96,32},{112,48},{1... | collective-permute-start | bytes 196616 | tf_op jit(solution)/shard_map/ppermute | solution.py:293
  98.5 2.9 %collective-permute-done.2 = f32[2,64,128]{2,1,0:T(8,128)S(1)} collective-permute-done((f32[2,64,128]{2,1,0:T(8,128)S(1)}, f32[2,64,128]{2,1,0:T(8,128)S(1)}, u32[]{:S(2)}, u32[]{:S(2)}) %collective-permute-start.2) | collective-permute-done | bytes 65568 | tf_op jit(solution)/shard_map/ppermute | solution.py:293
  101.4 7.1 %collective-permute-start.3 = (f32[2,64,128]{2,1,0:T(8,128)S(1)}, f32[2,64,128]{2,1,0:T(8,128)S(1)}, u32[]{:S(2)}, u32[]{:S(2)}) collective-permute-start(f32[2,64,128]{2,1,0:T(8,128)S(1)} %add.14), channel_id=1, source_target_pairs={{0,128},{16,144},{32,160},{48,176},{64,192},{80,208},{96,224},{112... | collective-permute-start | bytes 196616 | tf_op jit(solution)/shard_map/ppermute | solution.py:293
  108.4 2.2 %collective-permute-done.3 = f32[2,64,128]{2,1,0:T(8,128)S(1)} collective-permute-done((f32[2,64,128]{2,1,0:T(8,128)S(1)}, f32[2,64,128]{2,1,0:T(8,128)S(1)}, u32[]{:S(2)}, u32[]{:S(2)}) %collective-permute-start.3) | collective-permute-done | bytes 65568 | tf_op jit(solution)/shard_map/ppermute | solution.py:293
  110.7 0.7 copy.23
  111.4 0.0 all-to-all-done.2
  111.4 0.1 fusion
  111.5 0.1 convert_element_type.11
  111.6 1.1 copy.12
  (6 shorter events, 0.0 us)
Async XLA Ops:
  0.6 2.4 %copy-start.11 = (f32[2,16,8192]{2,1,0:T(8,128)S(1)}, f32[2,16,8192]{2,1,0:T(8,128)}, u32[]{:S(2)}) copy-start(f32[2,16,8192]{2,1,0:T(8,128)} %param.9) | copy-start | bytes 3145732
  3.5 40.1 %copy-start.9 = (bf16[2,256,256]{2,1,0:T(8,128)(2,1)S(1)}, bf16[2,256,256]{2,1,0:T(8,128)(2,1)}, u32[]{:S(2)}) copy-start(bf16[2,256,256]{2,1,0:T(8,128)(2,1)} %constant.19.clone.inverse_l) | copy-start | bytes 786436
  3.5 40.1 %copy-start.10 = (bf16[2,256,256]{2,1,0:T(8,128)(2,1)S(1)}, bf16[2,256,256]{2,1,0:T(8,128)(2,1)}, u32[]{:S(2)}) copy-start(bf16[2,256,256]{2,1,0:T(8,128)(2,1)} %constant.18.clone.forward_l) | copy-start | bytes 786436
  3.9 39.8 %copy-start.1 = (bf16[8,2,256,256]{3,2,1,0:T(8,128)(2,1)S(1)}, bf16[8,2,256,256]{3,2,1,0:T(8,128)(2,1)}, u32[]{:S(2)}) copy-start(bf16[8,2,256,256]{3,2,1,0:T(8,128)(2,1)} %constant.17.clone.inverse_s) | copy-start | bytes 6291460
  3.9 39.8 %copy-start.3 = (bf16[8,2,256,256]{3,2,1,0:T(8,128)(2,1)S(1)}, bf16[8,2,256,256]{3,2,1,0:T(8,128)(2,1)}, u32[]{:S(2)}) copy-start(bf16[8,2,256,256]{3,2,1,0:T(8,128)(2,1)} %constant.16.clone.forward_s) | copy-start | bytes 6291460
  3.9 39.8 %copy-start.7 = (f32[8,2,128,128]{3,2,1,0:T(8,128)S(1)}, f32[8,2,128,128]{3,2,1,0:T(8,128)}, u32[]{:S(2)}) copy-start(f32[8,2,128,128]{3,2,1,0:T(8,128)} %constant.20.clone.turns) | copy-start | bytes 3145732
  57.1 1.3 %copy-start.5 = (f32[8,256,256]{2,1,0:T(8,128)}, f32[8,256,256]{2,1,0:T(8,128)S(1)}, u32[]{:S(2)}) copy-start(f32[8,256,256]{2,1,0:T(8,128)S(1)} %get-tuple-element.6.grads) | copy-start | bytes 6291460
  58.5 22.6 %all-to-all-start.1 = ((f32[16,64,128]{2,1,0:T(8,128)}), f32[16,64,128]{2,1,0:T(8,128)}, u32[]{:S(2)}, u32[]{:S(2)}) async-start(f32[16,64,128]{2,1,0:T(8,128)} %get-tuple-element.7), calls=%async_computation.1 | async-start | bytes 1048576 | tf_op jit(solution)/shard_map/all_to_all | solution.py:286
  64.2 1.6 %copy-start.2 = (bf16[8,2,256,256]{3,2,1,0:T(8,128)(2,1)S(1)}, bf16[8,2,256,256]{3,2,1,0:T(8,128)(2,1)}, u32[]{:S(2)}) copy-start(bf16[8,2,256,256]{3,2,1,0:T(8,128)(2,1)} %constant.17.clone.inverse_s) | copy-start | bytes 6291460
  65.8 1.6 %copy-start.4 = (bf16[8,2,256,256]{3,2,1,0:T(8,128)(2,1)S(1)}, bf16[8,2,256,256]{3,2,1,0:T(8,128)(2,1)}, u32[]{:S(2)}) copy-start(bf16[8,2,256,256]{3,2,1,0:T(8,128)(2,1)} %constant.16.clone.forward_s) | copy-start | bytes 6291460
  67.4 1.6 %copy-start.6 = (f32[8,256,256]{2,1,0:T(8,128)S(1)}, f32[8,256,256]{2,1,0:T(8,128)}, u32[]{:S(2)}) copy-start(f32[8,256,256]{2,1,0:T(8,128)} %copy-done.5) | copy-start | bytes 6291460
  69.0 1.2 %copy-start.8 = (f32[8,2,128,128]{3,2,1,0:T(8,128)S(1)}, f32[8,2,128,128]{3,2,1,0:T(8,128)}, u32[]{:S(2)}) copy-start(f32[8,2,128,128]{3,2,1,0:T(8,128)} %constant.20.clone.turns) | copy-start | bytes 3145732
  80.1 1.0 copy-start
  82.2 29.2 %all-to-all-start.2 = ((f32[16,2,64,128]{3,2,1,0:T(8,128)}), f32[16,2,64,128]{3,2,1,0:T(8,128)S(1)}, u32[]{:S(2)}, u32[]{:S(2)}) async-start(f32[16,2,64,128]{3,2,1,0:T(8,128)} %copy-done), calls=%async_computation.2 | async-start | bytes 2097152 | tf_op jit(solution)/shard_map/all_to_all | solution.py:290
  89.4 1.3 %collective-permute-start = (f32[2,64,128]{2,1,0:T(8,128)S(1)}, f32[2,64,128]{2,1,0:T(8,128)S(1)}, u32[]{:S(2)}, u32[]{:S(2)}) collective-permute-start(f32[2,64,128]{2,1,0:T(8,128)S(1)} %reduce_sum.9), channel_id=1, source_target_pairs={{0,16},{16,0},{32,48},{48,32},{64,80},{80,64},{96,112},{112,96},{1... | collective-permute-start | bytes 196616 | tf_op jit(solution)/shard_map/ppermute | solution.py:293
  90.7 4.4 %collective-permute-start.1 = (f32[2,64,128]{2,1,0:T(8,128)S(1)}, f32[2,64,128]{2,1,0:T(8,128)S(1)}, u32[]{:S(2)}, u32[]{:S(2)}) collective-permute-start(f32[2,64,128]{2,1,0:T(8,128)S(1)} %add.12), channel_id=1, source_target_pairs={{0,32},{16,48},{32,0},{48,16},{64,96},{80,112},{96,64},{112,80},{1... | collective-permute-start | bytes 196616 | tf_op jit(solution)/shard_map/ppermute | solution.py:293
  95.2 6.2 %collective-permute-start.2 = (f32[2,64,128]{2,1,0:T(8,128)S(1)}, f32[2,64,128]{2,1,0:T(8,128)S(1)}, u32[]{:S(2)}, u32[]{:S(2)}) collective-permute-start(f32[2,64,128]{2,1,0:T(8,128)S(1)} %add.13), channel_id=1, source_target_pairs={{0,64},{16,80},{32,96},{48,112},{64,0},{80,16},{96,32},{112,48},{1... | collective-permute-start | bytes 196616 | tf_op jit(solution)/shard_map/ppermute | solution.py:293
  101.4 9.3 %collective-permute-start.3 = (f32[2,64,128]{2,1,0:T(8,128)S(1)}, f32[2,64,128]{2,1,0:T(8,128)S(1)}, u32[]{:S(2)}, u32[]{:S(2)}) collective-permute-start(f32[2,64,128]{2,1,0:T(8,128)S(1)} %add.14), channel_id=1, source_target_pairs={{0,128},{16,144},{32,160},{48,176},{64,192},{80,208},{96,224},{112... | collective-permute-start | bytes 196616 | tf_op jit(solution)/shard_map/ppermute | solution.py:293

commit v2 on v1

v2 whole, which is shorter than its diff:
```python
import functools
import math

import jax
import jax.numpy as jnp
import ml_dtypes
import numpy as np
from jax import lax
from jax.experimental import pallas as pl
from jax.experimental.pallas import tpu as pltpu
from jax.sharding import PartitionSpec as P

RADIX = 8
SIDE = 128
TOKENS = RADIX * SIDE * SIDE
LANES = 128
STEP = 32


def two_halves(matrix):
    high = matrix.astype(ml_dtypes.bfloat16)
    low = (matrix - high.astype(np.float64)).astype(ml_dtypes.bfloat16)
    return high, low


@functools.cache
def tables():
    side = np.arange(SIDE)
    turn = np.pi / 2 + 2 * np.pi * side
    forward_s, inverse_s = [], []
    for r in range(RADIX):
        matrix = np.exp(1j * np.outer(turn, side + r / RADIX) / SIDE)
        high, low = two_halves(np.concatenate([matrix.real, matrix.imag], axis=0))
        forward_s.append(
            np.block([[high, high], [low, np.zeros_like(low)]]).astype(ml_dtypes.bfloat16)
        )
        high, low = two_halves(np.concatenate([matrix.real.T, matrix.imag.T], axis=1))
        inverse_s.append(np.concatenate([high, low], axis=0))
    over_r = np.exp(1j * np.outer(np.arange(RADIX), turn) / (RADIX * SIDE))
    over_r = np.stack([over_r.real, over_r.imag], axis=1)[..., None]
    over_r = np.broadcast_to(over_r, (RADIX, 2, SIDE, LANES)).astype(np.float32)
    q = np.arange(RADIX)[:, None, None]
    over_l = np.exp(1j * side * (turn[:, None] + 256 * np.pi * q) / TOKENS)
    over_l = np.stack([over_l.real, over_l.imag], axis=1).astype(np.float32)
    matrix = np.exp(2j * np.pi * np.outer(side, side) / SIDE)
    form = np.block([[matrix.real, matrix.imag], [-matrix.imag, matrix.real]])
    forward_l = np.stack(two_halves(form))
    inverse_l = np.stack(two_halves(form.T))
    return np.stack(forward_s), np.stack(inverse_s), forward_l, inverse_l, over_r, over_l


def dft4(a, b, c, d, sign):
    t0 = (a[0] + c[0], a[1] + c[1])
    t1 = (a[0] - c[0], a[1] - c[1])
    t2 = (b[0] + d[0], b[1] + d[1])
    t3 = (b[0] - d[0], b[1] - d[1])
    if sign < 0:
        t3 = (-t3[0], -t3[1])
    return [
        (t0[0] + t2[0], t0[1] + t2[1]),
        (t1[0] - t3[1], t1[1] + t3[0]),
        (t0[0] - t2[0], t0[1] - t2[1]),
        (t1[0] + t3[1], t1[1] - t3[0]),
    ]


def dft8(u, sign):
    even = dft4(u[0], u[2], u[4], u[6], sign)
    odd = dft4(u[1], u[3], u[5], u[7], sign)
    half = math.sqrt(0.5)
    turned = [
        odd[0],
        (half * (odd[1][0] - sign * odd[1][1]), half * (odd[1][1] + sign * odd[1][0])),
        (-sign * odd[2][1], sign * odd[2][0]),
        (half * (-odd[3][0] - sign * odd[3][1]), half * (sign * odd[3][0] - odd[3][1])),
    ]
    plus = [(e[0] + o[0], e[1] + o[1]) for e, o in zip(even, turned)]
    minus = [(e[0] - o[0], e[1] - o[1]) for e, o in zip(even, turned)]
    return plus + minus


def split(values):
    high = values.astype(jnp.bfloat16)
    low = (values - high.astype(jnp.float32)).astype(jnp.bfloat16)
    return high, low


def dot(left, right):
    return jnp.dot(left, right, preferred_element_type=jnp.float32)


def dot_from_right(values, table):
    high, low = split(values)
    count = values.shape[0]
    both = dot(jnp.concatenate([high, low], axis=0), table[0])
    return both[:count] + both[count:] + dot(high, table[1])


def times(a, b):
    return a[0] * b[0] - a[1] * b[1], a[0] * b[1] + a[1] * b[0]


def times_conjugate(a, b):
    return a[0] * b[0] + a[1] * b[1], a[1] * b[0] - a[0] * b[1]


def parts(values):
    return values[:, :LANES], values[:, LANES:]


def over_s_forward(blocks_of, count, forward_s, loads, z):
    for r in range(RADIX):
        loads[r].wait()
        samples = [blocks_of(row, r).reshape(SIDE, LANES) for row in range(count)]
        high, low = split(jnp.concatenate(samples, axis=1))
        both = dot(forward_s[r], jnp.concatenate([high, low], axis=0))
        out = both[: 2 * SIDE] + both[2 * SIDE :]
        z[r] = out.reshape(2, SIDE, count * LANES)


def over_r_forward(z, row, span, over_l):
    lanes = pl.ds(row * LANES, LANES)
    u = [(z[r, 0, span, lanes], z[r, 1, span, lanes]) for r in range(RADIX)]
    out = []
    for q, value in enumerate(dft8(u, 1)):
        value = times(value, (over_l[q, 0, span, :], over_l[q, 1, span, :]))
        out.append(jnp.concatenate(value, axis=1))
    return out


def over_r_inverse(values, span, over_l):
    v = []
    for q in range(RADIX):
        value = parts(values[q * STEP : (q + 1) * STEP])
        v.append(times_conjugate(value, (over_l[q, 0, span, :], over_l[q, 1, span, :])))
    return dft8(v, -1)


def over_s_inverse(high, low, table):
    both = dot(table, high)
    return both[:SIDE] + both[SIDE:] + dot(table[:SIDE], low)


def load_each(source, target, sems):
    copies = [pltpu.make_async_copy(source.at[r], target.at[r], sems.at[r]) for r in range(RADIX)]
    for copy in copies:
        copy.start()
    return copies


def filter_kernel(
    rows, forward_s, inverse_s, forward_l, inverse_l, over_r, over_l,
    terms, grads, half, z, back, held, forward_in, sems, load_sems,
):
    loads = load_each(forward_s, forward_in, load_sems)
    half[...] = rows[:, 4 * RADIX :]
    over_s_forward(lambda row, r: rows[:, row * RADIX + r], 4, forward_in, loads, z)
    size = RADIX * STEP
    copies = []
    for step in range(SIDE // STEP):
        span = pl.ds(step * STEP, STEP)
        blocks = []
        for row in range(4):
            blocks += over_r_forward(z, row, span, over_l)
        spectra = dot_from_right(jnp.concatenate(blocks, axis=0), forward_l)
        held[step] = spectra[2 * size :]
        copies.append(pltpu.make_async_copy(held.at[step], grads.at[step], sems.at[step]))
        copies[-1].start()
        first = times_conjugate(parts(spectra[2 * size : 3 * size]), parts(spectra[:size]))
        second = times_conjugate(parts(spectra[3 * size :]), parts(spectra[size : 2 * size]))
        product = jnp.concatenate([first[0] + second[0], first[1] + second[1]], axis=1)
        values = dot_from_right(product, inverse_l)
        for r, value in enumerate(over_r_inverse(values, span, over_l)):
            value = times_conjugate(value, (over_r[r, 0, span, :], over_r[r, 1, span, :]))
            lanes = pl.ds(r * LANES, LANES)
            for part in range(2):
                high, low = split(value[part])
                back[0, part, span, lanes] = high
                back[1, part, span, lanes] = low
    shape = (2 * SIDE, RADIX * LANES)
    out = over_s_inverse(back[0].reshape(shape), back[1].reshape(shape), inverse_s[...])
    for r in range(RADIX):
        value = out[:, r * LANES : (r + 1) * LANES]
        terms[:, r] = value.reshape(terms.shape[0], terms.shape[2], LANES)
    for copy in copies:
        copy.wait()


def input_kernel(
    core, mine, other, grads, forward_s, inverse_s, forward_l, inverse_l, over_l,
    out, z, back, grads_in, forward_in, inverse_in, turns_in, out_held, sems, load_sems,
):
    loads = load_each(forward_s, forward_in, load_sems)
    load_turns = pltpu.make_async_copy(over_l, turns_in, sems.at[0])
    load_grads = pltpu.make_async_copy(grads, grads_in, sems.at[1])
    load_inverse = pltpu.make_async_copy(inverse_s, inverse_in, sems.at[2])
    for copy in (load_turns, load_grads, load_inverse):
        copy.start()
    size = RADIX * STEP
    near = core[0] == 0
    per_half = mine.shape[1]

    def filter_block(row, r):
        own, far = mine[:, r % per_half], other[:, r % per_half]
        return jnp.where(near, own, far) if r < per_half else jnp.where(near, far, own)

    over_s_forward(filter_block, 1, forward_in, loads, z)
    load_turns.wait()
    load_grads.wait()
    for step in range(SIDE // STEP):
        span = pl.ds(step * STEP, STEP)
        spectrum = dot_from_right(
            jnp.concatenate(over_r_forward(z, 0, span, turns_in), axis=0), forward_l
        )
        products = []
        for row in range(2):
            grad = grads_in[step, row * size : (row + 1) * size]
            products.append(
                jnp.concatenate(times_conjugate(parts(grad), parts(spectrum)), axis=1)
            )
        values = dot_from_right(jnp.concatenate(products, axis=0), inverse_l)
        for row in range(2):
            lanes = pl.ds(row * LANES, LANES)
            one = values[row * size : (row + 1) * size]
            for r, value in enumerate(over_r_inverse(one, span, turns_in)):
                for part in range(2):
                    high, low = split(value[part])
                    back[0, r, part, span, lanes] = high
                    back[1, r, part, span, lanes] = low
    shape = (2 * SIDE, 2 * LANES)
    load_inverse.wait()
    copies = []
    for r in range(RADIX):
        samples = over_s_inverse(back[0, r].reshape(shape), back[1, r].reshape(shape), inverse_in[r])
        for row in range(2):
            value = samples[:, row * LANES : (row + 1) * LANES]
            out_held[:, row, r] = value.reshape(out.shape[0], out.shape[3], LANES)
        copies.append(pltpu.make_async_copy(out_held.at[:, :, r], out.at[:, :, r], sems.at[3 + r]))
        copies[-1].start()
    for copy in copies:
        copy.wait()


def in_vmem(count):
    return [pl.BlockSpec(memory_space=pltpu.VMEM)] * count


def in_hbm(count):
    return [pl.BlockSpec(memory_space=pltpu.HBM)] * count


def filter_terms(rows, consts):
    blocks, tiles, part, lanes = rows.shape
    forward_s, inverse_s, forward_l, inverse_l, over_r, over_l = consts
    steps = SIDE // STEP
    grads = (steps, 2 * RADIX * STEP, 2 * LANES)
    return pl.pallas_call(
        filter_kernel,
        out_shape=(
            jax.ShapeDtypeStruct((blocks, RADIX, part, lanes), jnp.float32),
            jax.ShapeDtypeStruct(grads, jnp.float32),
            jax.ShapeDtypeStruct((blocks, tiles - 4 * RADIX, part, lanes), jnp.float32),
        ),
        in_specs=[*in_vmem(1), *in_hbm(1), *in_vmem(5)],
        out_specs=(in_vmem(1)[0], in_hbm(1)[0], in_vmem(1)[0]),
        scratch_shapes=[
            pltpu.VMEM((RADIX, 2, SIDE, 4 * LANES), jnp.float32),
            pltpu.VMEM((2, 2, SIDE, RADIX * LANES), jnp.bfloat16),
            pltpu.VMEM(grads, jnp.float32),
            pltpu.VMEM(forward_s.shape, jnp.bfloat16),
            pltpu.SemaphoreType.DMA((steps,)),
            pltpu.SemaphoreType.DMA((RADIX,)),
        ],
        compiler_params=pltpu.CompilerParams(vmem_limit_bytes=50 << 20),
        cost_estimate=pl.CostEstimate(
            flops=4_000_000_000, bytes_accessed=10_000_000, transcendentals=0
        ),
        name="filter_terms",
    )(rows, forward_s, inverse_s[0], forward_l, inverse_l, over_r, over_l)


def input_rows(core, mine, other, grads, consts):
    blocks, tiles, part, lanes = mine.shape
    forward_s, inverse_s, forward_l, inverse_l, _, over_l = consts
    out = (blocks, 2, RADIX, part, lanes)
    return pl.pallas_call(
        input_kernel,
        out_shape=jax.ShapeDtypeStruct(out, jnp.float32),
        in_specs=[
            pl.BlockSpec(memory_space=pltpu.SMEM),
            *in_vmem(2),
            *in_hbm(3),
            *in_vmem(2),
            *in_hbm(1),
        ],
        out_specs=in_hbm(1)[0],
        scratch_shapes=[
            pltpu.VMEM((RADIX, 2, SIDE, LANES), jnp.float32),
            pltpu.VMEM((2, RADIX, 2, SIDE, 2 * LANES), jnp.bfloat16),
            pltpu.VMEM(grads.shape, jnp.float32),
            pltpu.VMEM(forward_s.shape, jnp.bfloat16),
            pltpu.VMEM(inverse_s.shape, jnp.bfloat16),
            pltpu.VMEM(over_l.shape, jnp.float32),
            pltpu.VMEM(out, jnp.float32),
            pltpu.SemaphoreType.DMA((3 + RADIX,)),
            pltpu.SemaphoreType.DMA((RADIX,)),
        ],
        compiler_params=pltpu.CompilerParams(vmem_limit_bytes=60 << 20),
        cost_estimate=pl.CostEstimate(
            flops=2_500_000_000, bytes_accessed=10_000_000, transcendentals=0
        ),
        name="input_rows",
    )(core, mine, other, grads, forward_s, inverse_s, forward_l, inverse_l, over_l)


def sum_over_chan(value, chan):
    depth = chan // 2

    def moved(array, shift):
        ring = [
            (2 * z + c, 2 * ((z + shift) % depth) + c) for z in range(depth) for c in range(2)
        ]
        return lax.ppermute(array, "chan", ring)

    value = value + lax.ppermute(value, "chan", [(i, i ^ 1) for i in range(chan)])
    if depth != 8:
        total = value
        for shift in range(1, depth):
            total = total + moved(value, shift)
        return total
    below, above = moved(value, 1), moved(value, -1)
    pair = value + above
    triple = pair + below
    return triple + moved(triple, -3) + moved(pair, 3)


def local(saved_input, out_grad, filters):
    batch, channels, tokens = saved_input.shape
    groups = filters.shape[0]
    devices = lax.axis_size("ctx")
    chan = lax.axis_size("chan")
    core = lax.axis_index("chan") % 2
    part = tokens // (RADIX * LANES)
    half = RADIX // 2
    consts = tuple(jnp.asarray(t) for t in tables())
    shape = (batch, channels, part, RADIX, LANES)
    by_channel = [
        v.reshape(shape).transpose(1, 0, 3, 2, 4).reshape(channels, batch * RADIX, part, LANES)
        for v in (saved_input, out_grad)
    ]
    own_filter = filters.reshape(groups, part, 2, half, LANES)
    own_filter = jnp.where(core == 0, own_filter[:, :, 0], own_filter[:, :, 1]).swapaxes(1, 2)
    own_filter = jnp.tile(own_filter, (channels // groups, 1, 1, 1))
    packed = jnp.concatenate([*by_channel, own_filter], axis=1)
    rows = lax.all_to_all(packed, "ctx", 0, 0, tiled=True)
    terms, grads, mine = filter_terms(rows, consts)
    other = lax.ppermute(mine, "chan", [(i, i ^ 1) for i in range(chan)])
    terms = lax.all_to_all(terms, "ctx", 0, 0, tiled=True)
    inputs = input_rows(core.reshape(1), mine, other, grads, consts)
    total = jnp.sum(terms.reshape(devices // groups, groups, RADIX, part, LANES), axis=0)
    inputs, total = lax.optimization_barrier((inputs, total))
    inputs = lax.all_to_all(inputs, "ctx", 0, 0, tiled=True)
    total = sum_over_chan(total, chan)
    per_filter = channels // groups
    norm = float(tokens * devices * batch * per_filter * chan) ** -0.5
    filter_grad = total.swapaxes(1, 2).reshape(groups, tokens) * (norm / TOKENS)
    input_grad = (inputs * (1.0 / TOKENS)).transpose(1, 0, 3, 2, 4)
    return input_grad.reshape(batch, channels, tokens).astype(jnp.bfloat16), filter_grad


def solution(mesh):
    placed = (P(None, "chan", "ctx"), P(None, "chan", "ctx"), P(None, "ctx"))
    return jax.shard_map(
        local,
        mesh=mesh,
        in_specs=placed,
        out_specs=(P(None, "chan", "ctx"), P(None, "ctx")),
        check_vma=False,
    )
```

time: 113 us -> 99.2 us (0.88)
  local copies, waits for them, and re-layouts: 13.1 us -> 5.55 us
  Pallas kernels: 23.4 us -> 19.7 us
  waiting for transfers between devices: 8.77 us -> 12.1 us
  blocking collectives: 39.7 us -> 37.1 us
  starting transfers between devices: 25.4 us -> 23.1 us
  other arithmetic: 1.56 us -> 0.39 us
    unnamed x29 -> x19, local copies, waits for them, and re-layouts: 12.6 us -> 3.01 us
    pallas_call x2, Pallas kernels: 23.4 us -> 19.7 us  [the longest x1 11.4 us: filter_terms(): pl.pallas_call(filter_kernel, out_shape=(jax.ShapeDtypeStruct((blocks, RA...]
    all_to_all x1, blocking collectives: 39.7 us -> 37.1 us  [local(): rows = lax.all_to_all(packed, 'ctx', 0, 0, tiled=True)]
    ppermute x4 -> x6, waiting for transfers between devices: 8.76 us -> 11.2 us  [the longest x4 9.98 us: moved(): return lax.ppermute(array, 'chan', ring)]
    reshape x0 -> x3, local copies, waits for them, and re-layouts: none -> 1.39 us  [the longest x1 0.99 us: local(): own_filter = filters.reshape(groups, part, 2, half, LANES)]
    ppermute x4 -> x6, starting transfers between devices: 12.4 us -> 11.3 us  [the longest x4 11.2 us: moved(): return lax.ppermute(array, 'chan', ring)]
  transfers between devices with their start and end apart: 6 -> 8, of which waited for: 4 -> 5; matrix products, arithmetic and copies ran while one was open for 1% -> 1% of each run, Pallas kernels for 9% -> 8%
where the time goes in v2:
time: 99.2 us; the launch traced here: 98.7 us
  blocking collectives  37.1 us (37%)
  starting transfers between devices  23.1 us (23%)
  Pallas kernels  19.7 us (20%)
  waiting for transfers between devices  12.1 us (12%)
  local copies, waits for them, and re-layouts  5.55 us (6%)
    all_to_all x1, blocking collectives, local(): rows = lax.all_to_all(packed, 'ctx', 0, 0, tiled=True)  37.1 us
    pallas_call x1, Pallas kernels, filter_terms(): pl.pallas_call(filter_kernel, out_shape=(jax.ShapeDtypeStruct((blocks, RA...  11.4 us
    ppermute x4, starting transfers between devices, moved(): return lax.ppermute(array, 'chan', ring)  11.2 us
    ppermute x4, waiting for transfers between devices, moved(): return lax.ppermute(array, 'chan', ring)  9.98 us
    pallas_call x1, Pallas kernels, input_rows(): pl.pallas_call(input_kernel, out_shape=jax.ShapeDtypeStruct(out, jnp.floa...  8.32 us
    all_to_all x1, starting transfers between devices, local(): inputs = lax.all_to_all(inputs, 'ctx', 0, 0, tiled=True)  6.42 us
    all_to_all x1, starting transfers between devices, local(): terms = lax.all_to_all(terms, 'ctx', 0, 0, tiled=True)  5.36 us
    unnamed x19, local copies, waits for them, and re-layouts  3.01 us
  transfers between devices with their start and end apart: 8, of which 5 were waited for; matrix products, arithmetic and copies ran while one was open for 1% of the time, Pallas kernels for 8%

profile of v2, /device:TPU:2, one launch (start us, length us, event | category | flops | bytes accessed | tf_op | source)
XLA Modules:
  0.0 98.7 jit_solution(2618674385662245077)
XLA Ops:
  0.6 0.0 copy-start.6
  0.7 1.0 %reshape.41 = f32[2,8,2,4,128]{4,3,2,1,0:T(4,128)S(1)} reshape(f32[2,8192]{1,0:T(2,128)} %param.11) | data formatting | bytes 131072 | tf_op jit(solution)/shard_map/reshape | solution.py:351
  1.7 1.4 %copy.27 = f32[4,8,64,128]{3,2,1,0:T(8,128)S(1)} copy(f32[4,8,64,128]{3,1,2,0:T(8,128)} %bitcast.40) | data formatting | bytes 2097152
  3.1 0.2 copy.22
  3.3 0.0 copy-done.6
  3.3 0.2 copy.28
  3.5 0.2 copy.23
  3.7 0.2 pad_maximum_fusion
  3.9 0.0 copy-start.1
  4.0 0.0 copy-start.2
  4.0 0.0 copy-start.3
  4.0 0.0 copy-start.4
  4.0 0.0 copy-start.5
  4.0 37.1 %all_to_all.15.rows = f32[16,36,8,128]{3,2,1,0:T(8,128)} all-to-all(f32[16,36,8,128]{3,2,1,0:T(8,128)S(1)} %pad_maximum_fusion), channel_id=1, replica_groups=mesh['chan'=16,'ctx'=16] {'ctx'}, dimensions={0} | all-to-all | bytes 4718592 | tf_op jit(solution)/shard_map/all_to_all | solution.py:355
  41.1 0.0 copy-done.1
  41.1 0.0 copy-done.2
  41.1 0.0 copy-done.3
  41.1 0.0 copy-done.4
  41.1 0.0 copy-done.5
  41.1 11.4 %filter_terms.1 = (f32[16,8,8,128]{3,2,1,0:T(8,128)}, f32[4,512,256]{2,1,0:T(8,128)}, f32[16,4,8,128]{3,2,1,0:T(8,128)S(1)}) custom-call(f32[16,36,8,128]{3,2,1,0:T(8,128)} %all_to_all.15.rows, bf16[8,512,256]{2,1,0:T(8,128)(2,1)} %constant.37.clone.forward_s, bf16[256,256]{1,0:T(8,128)(2,1)S(1)} %copy-done.5, bf16[2,256,256]{2,1,0:T(8,128)(2,1)S(1)} %copy-done.4, ...), custom_call_target="tpu_custom_call" | custom-call | flops 4000000000 | bytes 10000000 | tf_op jit(solution)/shard_map/filter_terms/pallas_call | solution.py:257
  52.5 0.0 copy-start
  52.5 0.1 collective-permute-start
  52.6 5.4 %all-to-all-start.1 = ((f32[16,8,8,128]{3,2,1,0:T(8,128)}), f32[16,8,8,128]{3,2,1,0:T(8,128)S(1)}, u32[]{:S(2)}, u32[]{:S(2)}) async-start(f32[16,8,8,128]{3,2,1,0:T(8,128)} %get-tuple-element.9), calls=%async_computation.1 | async-start | bytes 1048576 | tf_op jit(solution)/shard_map/all_to_all | solution.py:358
  58.0 0.0 collective-permute-done.other
  58.0 0.0 copy-start.7
  58.0 0.0 copy-done
  58.0 0.7 copy-done.7
  58.7 8.3 %input_rows.1 = f32[16,2,8,8,128]{4,3,2,1,0:T(8,128)} custom-call(s32[1]{0:T(128)} %bitcast.core, f32[16,4,8,128]{3,2,1,0:T(8,128)} %copy-done, f32[16,4,8,128]{3,2,1,0:T(8,128)} %copy-done.7, f32[4,512,256]{2,1,0:T(8,128)} %get-tuple-element.8.grads, bf16[8,512,256]{2,1,0:T(8,128)(2,1)} %constant.37.clone.forward_s, ...), custom_call_target="tpu_custom_call" | custom-call | flops 2500000000 | bytes 10000000 | tf_op jit(solution)/shard_map/input_rows/pallas_call | solution.py:286
  67.0 0.8 all-to-all-done.1
  67.9 6.4 %all-to-all-start.2 = ((f32[16,2,8,8,128]{4,3,2,1,0:T(8,128)}), f32[16,2,8,8,128]{4,3,2,1,0:T(8,128)S(1)}, u32[]{:S(2)}, u32[]{:S(2)}) async-start(f32[16,2,8,8,128]{4,3,2,1,0:T(8,128)} %input_rows.1), calls=%async_computation.2 | async-start | bytes 2097152 | tf_op jit(solution)/shard_map/all_to_all | solution.py:362
  74.3 0.0 collective-permute-start.1
  74.3 1.2 %collective-permute-done.1 = f32[2,8,8,128]{3,2,1,0:T(8,128)S(1)} collective-permute-done((f32[2,8,8,128]{3,2,1,0:T(8,128)S(1)}, f32[2,8,8,128]{3,2,1,0:T(8,128)S(1)}, u32[]{:S(2)}, u32[]{:S(2)}) %collective-permute-start.1) | collective-permute-done | bytes 65568 | tf_op jit(solution)/shard_map/ppermute | solution.py:325
  75.6 2.0 %collective-permute-start.3 = (f32[2,8,8,128]{3,2,1,0:T(8,128)S(1)}, f32[2,8,8,128]{3,2,1,0:T(8,128)S(1)}, u32[]{:S(2)}, u32[]{:S(2)}) collective-permute-start(f32[2,8,8,128]{3,2,1,0:T(8,128)S(1)} %add.20), channel_id=1, source_target_pairs={{0,32},{16,48},{32,64},{48,80},{64,96},{80,112},{96,128},{112,144}... | collective-permute-start | bytes 196616 | tf_op jit(solution)/shard_map/ppermute | solution.py:323
  77.5 4.1 %collective-permute-start.2 = (f32[2,8,8,128]{3,2,1,0:T(8,128)S(1)}, f32[2,8,8,128]{3,2,1,0:T(8,128)S(1)}, u32[]{:S(2)}, u32[]{:S(2)}) collective-permute-start(f32[2,8,8,128]{3,2,1,0:T(8,128)S(1)} %add.20), channel_id=1, source_target_pairs={{0,224},{16,240},{32,0},{48,16},{64,32},{80,48},{96,64},{112,80},{... | collective-permute-start | bytes 196616 | tf_op jit(solution)/shard_map/ppermute | solution.py:323
  81.6 2.3 %collective-permute-done.3 = f32[2,8,8,128]{3,2,1,0:T(8,128)S(1)} collective-permute-done((f32[2,8,8,128]{3,2,1,0:T(8,128)S(1)}, f32[2,8,8,128]{3,2,1,0:T(8,128)S(1)}, u32[]{:S(2)}, u32[]{:S(2)}) %collective-permute-start.3) | collective-permute-done | bytes 65568 | tf_op jit(solution)/shard_map/ppermute | solution.py:323
  84.0 0.0 collective-permute-done.2
  84.0 5.0 %collective-permute-start.5 = (f32[2,8,8,128]{3,2,1,0:T(8,128)S(1)}, f32[2,8,8,128]{3,2,1,0:T(8,128)S(1)}, u32[]{:S(2)}, u32[]{:S(2)}) collective-permute-start(f32[2,8,8,128]{3,2,1,0:T(8,128)S(1)} %get-tuple-element.13), channel_id=1, source_target_pairs={{0,96},{16,112},{32,128},{48,144},{64,160},{80,176},{96,192},{112,... | collective-permute-start | bytes 196616 | tf_op jit(solution)/shard_map/ppermute | solution.py:323
  89.0 0.1 collective-permute-start.4
  89.1 3.2 %collective-permute-done.5 = f32[2,8,8,128]{3,2,1,0:T(8,128)S(1)} collective-permute-done((f32[2,8,8,128]{3,2,1,0:T(8,128)S(1)}, f32[2,8,8,128]{3,2,1,0:T(8,128)S(1)}, u32[]{:S(2)}, u32[]{:S(2)}) %collective-permute-start.5) | collective-permute-done | bytes 65568 | tf_op jit(solution)/shard_map/ppermute | solution.py:323
  92.3 4.4 %collective-permute-done.4 = f32[2,8,8,128]{3,2,1,0:T(8,128)S(1)} collective-permute-done((f32[2,8,8,128]{3,2,1,0:T(8,128)S(1)}, f32[2,8,8,128]{3,2,1,0:T(8,128)S(1)}, u32[]{:S(2)}, u32[]{:S(2)}) %collective-permute-start.4) | collective-permute-done | bytes 65568 | tf_op jit(solution)/shard_map/ppermute | solution.py:323
  96.8 0.7 copy.32
  97.5 0.0 all-to-all-done.2
  97.5 0.1 fusion
  97.6 0.1 copy.25
  97.7 1.0 %convert_element_type.11 = bf16[2,16,8192]{2,1,0:T(8,128)(2,1)} reshape(bf16[2,16,8,8,128]{4,3,2,1,0:T(8,128)(2,1)S(1)} %copy.25) | data formatting | bytes 1048576 | tf_op jit(solution)/shard_map/convert_element_type | solution.py:368
  (8 shorter events, 0.1 us)
Async XLA Ops:
  0.6 2.7 %copy-start.6 = (f32[2,16,8192]{2,1,0:T(8,128)S(1)}, f32[2,16,8192]{2,1,0:T(8,128)}, u32[]{:S(2)}) copy-start(f32[2,16,8192]{2,1,0:T(8,128)} %param.10) | copy-start | bytes 3145732
  3.9 37.1 %copy-start.1 = (f32[8,2,128,128]{3,2,1,0:T(8,128)S(1)}, f32[8,2,128,128]{3,2,1,0:T(8,128)}, u32[]{:S(2)}) copy-start(f32[8,2,128,128]{3,2,1,0:T(8,128)} %constant.42.clone.over_l) | copy-start | bytes 3145732
  4.0 37.1 %copy-start.2 = (f32[8,2,128,128]{3,2,1,0:T(8,128)S(1)}, f32[8,2,128,128]{3,2,1,0:T(8,128)}, u32[]{:S(2)}) copy-start(f32[8,2,128,128]{3,2,1,0:T(8,128)} %constant.41.clone.over_r) | copy-start | bytes 3145732
  4.0 37.1 %copy-start.3 = (bf16[2,256,256]{2,1,0:T(8,128)(2,1)S(1)}, bf16[2,256,256]{2,1,0:T(8,128)(2,1)}, u32[]{:S(2)}) copy-start(bf16[2,256,256]{2,1,0:T(8,128)(2,1)} %constant.40.clone.inverse_l) | copy-start | bytes 786436
  4.0 37.1 %copy-start.4 = (bf16[2,256,256]{2,1,0:T(8,128)(2,1)S(1)}, bf16[2,256,256]{2,1,0:T(8,128)(2,1)}, u32[]{:S(2)}) copy-start(bf16[2,256,256]{2,1,0:T(8,128)(2,1)} %constant.39.clone.forward_l) | copy-start | bytes 786436
  4.0 37.1 %copy-start.5 = (bf16[256,256]{1,0:T(8,128)(2,1)S(1)}, bf16[256,256]{1,0:T(8,128)(2,1)}, u32[]{:S(2)}) copy-start(bf16[256,256]{1,0:T(8,128)(2,1)} %constant.44.inverse_s) | copy-start | bytes 393220
  52.5 5.5 %copy-start = (f32[16,4,8,128]{3,2,1,0:T(8,128)}, f32[16,4,8,128]{3,2,1,0:T(8,128)S(1)}, u32[]{:S(2)}) copy-start(f32[16,4,8,128]{3,2,1,0:T(8,128)S(1)} %get-tuple-element.7.mine) | copy-start | bytes 786436
  52.5 5.5 %collective-permute-start = (f32[16,4,8,128]{3,2,1,0:T(8,128)S(1)}, f32[16,4,8,128]{3,2,1,0:T(8,128)S(1)}, u32[]{:S(2)}, u32[]{:S(2)}) collective-permute-start(f32[16,4,8,128]{3,2,1,0:T(8,128)S(1)} %get-tuple-element.7.mine), channel_id=1, source_target_pairs={{0,16},{16,0},{32,48},{48,32},{64,80},{80,64},{96,112},{112,96},{1... | collective-permute-start | bytes 786440 | tf_op jit(solution)/shard_map/ppermute | solution.py:357
  52.6 15.2 %all-to-all-start.1 = ((f32[16,8,8,128]{3,2,1,0:T(8,128)}), f32[16,8,8,128]{3,2,1,0:T(8,128)S(1)}, u32[]{:S(2)}, u32[]{:S(2)}) async-start(f32[16,8,8,128]{3,2,1,0:T(8,128)} %get-tuple-element.9), calls=%async_computation.1 | async-start | bytes 1048576 | tf_op jit(solution)/shard_map/all_to_all | solution.py:358
  58.0 0.7 copy-start.7
  67.9 29.6 %all-to-all-start.2 = ((f32[16,2,8,8,128]{4,3,2,1,0:T(8,128)}), f32[16,2,8,8,128]{4,3,2,1,0:T(8,128)S(1)}, u32[]{:S(2)}, u32[]{:S(2)}) async-start(f32[16,2,8,8,128]{4,3,2,1,0:T(8,128)} %input_rows.1), calls=%async_computation.2 | async-start | bytes 2097152 | tf_op jit(solution)/shard_map/all_to_all | solution.py:362
  74.3 1.3 %collective-permute-start.1 = (f32[2,8,8,128]{3,2,1,0:T(8,128)S(1)}, f32[2,8,8,128]{3,2,1,0:T(8,128)S(1)}, u32[]{:S(2)}, u32[]{:S(2)}) collective-permute-start(f32[2,8,8,128]{3,2,1,0:T(8,128)S(1)} %reduce_sum.9), channel_id=1, source_target_pairs={{0,16},{16,0},{32,48},{48,32},{64,80},{80,64},{96,112},{112,96},{1... | collective-permute-start | bytes 196616 | tf_op jit(solution)/shard_map/ppermute | solution.py:325
  75.6 8.4 %collective-permute-start.3 = (f32[2,8,8,128]{3,2,1,0:T(8,128)S(1)}, f32[2,8,8,128]{3,2,1,0:T(8,128)S(1)}, u32[]{:S(2)}, u32[]{:S(2)}) collective-permute-start(f32[2,8,8,128]{3,2,1,0:T(8,128)S(1)} %add.20), channel_id=1, source_target_pairs={{0,32},{16,48},{32,64},{48,80},{64,96},{80,112},{96,128},{112,144}... | collective-permute-start | bytes 196616 | tf_op jit(solution)/shard_map/ppermute | solution.py:323
  77.5 6.4 %collective-permute-start.2 = (f32[2,8,8,128]{3,2,1,0:T(8,128)S(1)}, f32[2,8,8,128]{3,2,1,0:T(8,128)S(1)}, u32[]{:S(2)}, u32[]{:S(2)}) collective-permute-start(f32[2,8,8,128]{3,2,1,0:T(8,128)S(1)} %add.20), channel_id=1, source_target_pairs={{0,224},{16,240},{32,0},{48,16},{64,32},{80,48},{96,64},{112,80},{... | collective-permute-start | bytes 196616 | tf_op jit(solution)/shard_map/ppermute | solution.py:323
  84.0 8.3 %collective-permute-start.5 = (f32[2,8,8,128]{3,2,1,0:T(8,128)S(1)}, f32[2,8,8,128]{3,2,1,0:T(8,128)S(1)}, u32[]{:S(2)}, u32[]{:S(2)}) collective-permute-start(f32[2,8,8,128]{3,2,1,0:T(8,128)S(1)} %get-tuple-element.13), channel_id=1, source_target_pairs={{0,96},{16,112},{32,128},{48,144},{64,160},{80,176},{96,192},{112,... | collective-permute-start | bytes 196616 | tf_op jit(solution)/shard_map/ppermute | solution.py:323
  89.0 7.7 %collective-permute-start.4 = (f32[2,8,8,128]{3,2,1,0:T(8,128)S(1)}, f32[2,8,8,128]{3,2,1,0:T(8,128)S(1)}, u32[]{:S(2)}, u32[]{:S(2)}) collective-permute-start(f32[2,8,8,128]{3,2,1,0:T(8,128)S(1)} %get-tuple-element.12), channel_id=1, source_target_pairs={{0,160},{16,176},{32,192},{48,208},{64,224},{80,240},{96,0},{112,1... | collective-permute-start | bytes 196616 | tf_op jit(solution)/shard_map/ppermute | solution.py:323

commit v3 on v2

--- a/solution.py
+++ b/solution.py
@@ -31,9 +31,7 @@
     for r in range(RADIX):
         matrix = np.exp(1j * np.outer(turn, side + r / RADIX) / SIDE)
         high, low = two_halves(np.concatenate([matrix.real, matrix.imag], axis=0))
-        forward_s.append(
-            np.block([[high, high], [low, np.zeros_like(low)]]).astype(ml_dtypes.bfloat16)
-        )
+        forward_s.append(np.concatenate([high, low], axis=0))
         high, low = two_halves(np.concatenate([matrix.real.T, matrix.imag.T], axis=1))
         inverse_s.append(np.concatenate([high, low], axis=0))
     over_r = np.exp(1j * np.outer(np.arange(RADIX), turn) / (RADIX * SIDE))
@@ -108,12 +106,20 @@
     return values[:, :LANES], values[:, LANES:]
 
 
-def over_s_forward(blocks_of, count, forward_s, loads, z):
+def over_s_forward(blocks_of, count, forward_s, z):
     for r in range(RADIX):
-        loads[r].wait()
         samples = [blocks_of(row, r).reshape(SIDE, LANES) for row in range(count)]
         high, low = split(jnp.concatenate(samples, axis=1))
-        both = dot(forward_s[r], jnp.concatenate([high, low], axis=0))
+        first = forward_s[r, : 2 * SIDE]
+        second = forward_s[r, 2 * SIDE :]
+        table = jnp.concatenate(
+            [
+                jnp.concatenate([first, first], axis=1),
+                jnp.concatenate([second, jnp.zeros_like(second)], axis=1),
+            ],
+            axis=0,
+        )
+        both = dot(table, jnp.concatenate([high, low], axis=0))
         out = both[: 2 * SIDE] + both[2 * SIDE :]
         z[r] = out.reshape(2, SIDE, count * LANES)
 
@@ -141,20 +147,12 @@
     return both[:SIDE] + both[SIDE:] + dot(table[:SIDE], low)
 
 
-def load_each(source, target, sems):
-    copies = [pltpu.make_async_copy(source.at[r], target.at[r], sems.at[r]) for r in range(RADIX)]
-    for copy in copies:
-        copy.start()
-    return copies
-
-
 def filter_kernel(
     rows, forward_s, inverse_s, forward_l, inverse_l, over_r, over_l,
-    terms, grads, half, z, back, held, forward_in, sems, load_sems,
+    terms, grads, half, z, back, held, sems,
 ):
-    loads = load_each(forward_s, forward_in, load_sems)
     half[...] = rows[:, 4 * RADIX :]
-    over_s_forward(lambda row, r: rows[:, row * RADIX + r], 4, forward_in, loads, z)
+    over_s_forward(lambda row, r: rows[:, row * RADIX + r], 4, forward_s, z)
     size = RADIX * STEP
     copies = []
     for step in range(SIDE // STEP):
@@ -165,7 +163,6 @@
         spectra = dot_from_right(jnp.concatenate(blocks, axis=0), forward_l)
         held[step] = spectra[2 * size :]
         copies.append(pltpu.make_async_copy(held.at[step], grads.at[step], sems.at[step]))
-        copies[-1].start()
         first = times_conjugate(parts(spectra[2 * size : 3 * size]), parts(spectra[:size]))
         second = times_conjugate(parts(spectra[3 * size :]), parts(spectra[size : 2 * size]))
         product = jnp.concatenate([first[0] + second[0], first[1] + second[1]], axis=1)
@@ -177,6 +174,8 @@
                 high, low = split(value[part])
                 back[0, part, span, lanes] = high
                 back[1, part, span, lanes] = low
+    for copy in copies:
+        copy.start()
     shape = (2 * SIDE, RADIX * LANES)
     out = over_s_inverse(back[0].reshape(shape), back[1].reshape(shape), inverse_s[...])
     for r in range(RADIX):
@@ -188,9 +187,10 @@
 
 def input_kernel(
     core, mine, other, grads, forward_s, inverse_s, forward_l, inverse_l, over_l,
-    out, z, back, grads_in, forward_in, inverse_in, turns_in, out_held, sems, load_sems,
+    out, z, back, grads_in, forward_in, inverse_in, turns_in, out_held, sems,
 ):
-    loads = load_each(forward_s, forward_in, load_sems)
+    load_forward = pltpu.make_async_copy(forward_s, forward_in, sems.at[3 + RADIX])
+    load_forward.start()
     load_turns = pltpu.make_async_copy(over_l, turns_in, sems.at[0])
     load_grads = pltpu.make_async_copy(grads, grads_in, sems.at[1])
     load_inverse = pltpu.make_async_copy(inverse_s, inverse_in, sems.at[2])
@@ -204,7 +204,8 @@
         own, far = mine[:, r % per_half], other[:, r % per_half]
         return jnp.where(near, own, far) if r < per_half else jnp.where(near, far, own)
 
-    over_s_forward(filter_block, 1, forward_in, loads, z)
+    load_forward.wait()
+    over_s_forward(filter_block, 1, forward_in, z)
     load_turns.wait()
     load_grads.wait()
     for step in range(SIDE // STEP):
@@ -261,17 +262,15 @@
             jax.ShapeDtypeStruct(grads, jnp.float32),
             jax.ShapeDtypeStruct((blocks, tiles - 4 * RADIX, part, lanes), jnp.float32),
         ),
-        in_specs=[*in_vmem(1), *in_hbm(1), *in_vmem(5)],
+        in_specs=in_vmem(7),
         out_specs=(in_vmem(1)[0], in_hbm(1)[0], in_vmem(1)[0]),
         scratch_shapes=[
             pltpu.VMEM((RADIX, 2, SIDE, 4 * LANES), jnp.float32),
             pltpu.VMEM((2, 2, SIDE, RADIX * LANES), jnp.bfloat16),
             pltpu.VMEM(grads, jnp.float32),
-            pltpu.VMEM(forward_s.shape, jnp.bfloat16),
             pltpu.SemaphoreType.DMA((steps,)),
-            pltpu.SemaphoreType.DMA((RADIX,)),
         ],
-        compiler_params=pltpu.CompilerParams(vmem_limit_bytes=50 << 20),
+        compiler_params=pltpu.CompilerParams(vmem_limit_bytes=48 << 20),
         cost_estimate=pl.CostEstimate(
             flops=4_000_000_000, bytes_accessed=10_000_000, transcendentals=0
         ),
@@ -302,8 +301,7 @@
             pltpu.VMEM(inverse_s.shape, jnp.bfloat16),
             pltpu.VMEM(over_l.shape, jnp.float32),
             pltpu.VMEM(out, jnp.float32),
-            pltpu.SemaphoreType.DMA((3 + RADIX,)),
-            pltpu.SemaphoreType.DMA((RADIX,)),
+            pltpu.SemaphoreType.DMA((4 + RADIX,)),
         ],
         compiler_params=pltpu.CompilerParams(vmem_limit_bytes=60 << 20),
         cost_estimate=pl.CostEstimate(
@@ -316,22 +314,24 @@
 def sum_over_chan(value, chan):
     depth = chan // 2
 
-    def moved(array, shift):
-        ring = [
-            (2 * z + c, 2 * ((z + shift) % depth) + c) for z in range(depth) for c in range(2)
-        ]
+    def moved(array, shift, swap=False):
+        ring = []
+        for z in range(depth):
+            ring.append((2 * z, 2 * ((z + shift) % depth) + swap))
+            ring.append((2 * z + 1, 2 * ((z - shift) % depth) + 1 - swap))
         return lax.ppermute(array, "chan", ring)
 
-    value = value + lax.ppermute(value, "chan", [(i, i ^ 1) for i in range(chan)])
-    if depth != 8:
+    value = value + moved(value, 0, True)
+    if depth < 2 or depth & (depth - 1):
         total = value
         for shift in range(1, depth):
             total = total + moved(value, shift)
         return total
-    below, above = moved(value, 1), moved(value, -1)
-    pair = value + above
-    triple = pair + below
-    return triple + moved(triple, -3) + moved(pair, 3)
+    reach = 1
+    while 2 * reach < depth:
+        value = value + moved(value, reach)
+        reach *= 2
+    return value + moved(value, 1, True)
 
 
 def local(saved_input, out_grad, filters):

time: 99.2 us -> 94.8 us (0.956)
  starting transfers between devices: 23.1 us -> 13.5 us
  waiting for transfers between devices: 12.1 us -> 19.9 us
  Pallas kernels: 19.7 us -> 16.9 us
    ppermute x4, starting transfers between devices: 11.2 us -> 2.18 us  [moved(): return lax.ppermute(array, 'chan', ring)]
    ppermute x4, waiting for transfers between devices: 9.98 us -> 18 us  [moved(): return lax.ppermute(array, 'chan', ring)]
    pallas_call x1, Pallas kernels: 11.4 us -> 9.62 us  [filter_terms(): pl.pallas_call(filter_kernel, out_shape=(jax.ShapeDtypeStruct((blocks, RA...]
    ppermute x1 -> x0, waiting for transfers between devices: 1.24 us -> none  [sum_over_chan(): lax.ppermute(value, 'chan', [(i, i ^ 1) for i in range(chan)])]
    pallas_call x1, Pallas kernels: 8.32 us -> 7.27 us  [input_rows(): pl.pallas_call(input_kernel, out_shape=jax.ShapeDtypeStruct(out, jnp.floa...]
    all_to_all x1, waiting for transfers between devices: 0.84 us -> 1.89 us  [local(): terms = lax.all_to_all(terms, 'ctx', 0, 0, tiled=True)]
    unnamed x19 -> x21, local copies, waits for them, and re-layouts: 3.01 us -> 3.02 us
  transfers between devices with their start and end apart: 8 -> 7, of which waited for: 5 -> 5; matrix products, arithmetic and copies ran while one was open for 1% -> 1% of each run, Pallas kernels for 8% -> 8%
where the time goes in v3:
time: 94.8 us; the launch traced here: 94.3 us
  blocking collectives  37.2 us (39%)
  waiting for transfers between devices  19.9 us (21%)
  Pallas kernels  16.9 us (18%)
  starting transfers between devices  13.5 us (14%)
  local copies, waits for them, and re-layouts  5.57 us (6%)
    all_to_all x1, blocking collectives, local(): rows = lax.all_to_all(packed, 'ctx', 0, 0, tiled=True)  37.2 us
    ppermute x4, waiting for transfers between devices, moved(): return lax.ppermute(array, 'chan', ring)  18 us
    pallas_call x1, Pallas kernels, filter_terms(): pl.pallas_call(filter_kernel, out_shape=(jax.ShapeDtypeStruct((blocks, RA...  9.62 us
    pallas_call x1, Pallas kernels, input_rows(): pl.pallas_call(input_kernel, out_shape=jax.ShapeDtypeStruct(out, jnp.floa...  7.27 us
    all_to_all x1, starting transfers between devices, local(): inputs = lax.all_to_all(inputs, 'ctx', 0, 0, tiled=True)  5.84 us
    all_to_all x1, starting transfers between devices, local(): terms = lax.all_to_all(terms, 'ctx', 0, 0, tiled=True)  5.36 us
    unnamed x21, local copies, waits for them, and re-layouts  3.02 us
    ppermute x4, starting transfers between devices, moved(): return lax.ppermute(array, 'chan', ring)  2.18 us
  transfers between devices with their start and end apart: 7, of which 5 were waited for; matrix products, arithmetic and copies ran while one was open for 1% of the time, Pallas kernels for 8%

profile of v3, /device:TPU:2, one launch (start us, length us, event | category | flops | bytes accessed | tf_op | source)
XLA Modules:
  0.0 94.3 jit_solution(455836018022277458)
XLA Ops:
  0.6 0.0 copy-start.7
  0.7 1.0 %reshape.41 = f32[2,8,2,4,128]{4,3,2,1,0:T(4,128)S(1)} reshape(f32[2,8192]{1,0:T(2,128)} %param.11) | data formatting | bytes 131072 | tf_op jit(solution)/shard_map/reshape | solution.py:351
  1.7 1.4 %copy.27 = f32[4,8,64,128]{3,2,1,0:T(8,128)S(1)} copy(f32[4,8,64,128]{3,1,2,0:T(8,128)} %bitcast.40) | data formatting | bytes 2097152
  3.1 0.2 copy.22
  3.3 0.0 copy-done.7
  3.3 0.2 copy.28
  3.5 0.2 copy.23
  3.7 0.2 pad_maximum_fusion
  3.9 0.0 copy-start.1
  4.0 0.0 copy-start.2
  4.0 0.0 copy-start.3
  4.0 0.0 copy-start.4
  4.0 0.0 copy-start.5
  4.0 0.0 copy-start.6
  4.0 37.2 %all_to_all.15.rows = f32[16,36,8,128]{3,2,1,0:T(8,128)} all-to-all(f32[16,36,8,128]{3,2,1,0:T(8,128)S(1)} %pad_maximum_fusion), channel_id=1, replica_groups=mesh['chan'=16,'ctx'=16] {'ctx'}, dimensions={0} | all-to-all | bytes 4718592 | tf_op jit(solution)/shard_map/all_to_all | solution.py:355
  41.2 0.0 copy-done.1
  41.2 0.0 copy-done.2
  41.2 0.0 copy-done.3
  41.2 0.0 copy-done.4
  41.3 0.0 copy-done.5
  41.3 0.0 copy-done.6
  41.3 9.6 %filter_terms.1 = (f32[16,8,8,128]{3,2,1,0:T(8,128)}, f32[4,512,256]{2,1,0:T(8,128)}, f32[16,4,8,128]{3,2,1,0:T(8,128)S(1)}) custom-call(f32[16,36,8,128]{3,2,1,0:T(8,128)} %all_to_all.15.rows, bf16[8,512,128]{2,1,0:T(8,128)(2,1)S(1)} %copy-done.2, bf16[256,256]{1,0:T(8,128)(2,1)S(1)} %copy-done.6, bf16[2,256,256]{2,1,0:T(8,128)(2,1)S(1)} %copy-done.5, ...), custom_call_target="tpu_custom_call" | custom-call | flops 4000000000 | bytes 10000000 | tf_op jit(solution)/shard_map/filter_terms/pallas_call | solution.py:258
  50.9 0.0 copy-start
  50.9 0.1 collective-permute-start
  51.0 5.4 %all-to-all-start.1 = ((f32[16,8,8,128]{3,2,1,0:T(8,128)}), f32[16,8,8,128]{3,2,1,0:T(8,128)S(1)}, u32[]{:S(2)}, u32[]{:S(2)}) async-start(f32[16,8,8,128]{3,2,1,0:T(8,128)} %get-tuple-element.9), calls=%async_computation.1 | async-start | bytes 1048576 | tf_op jit(solution)/shard_map/all_to_all | solution.py:358
  56.4 0.0 collective-permute-done.other
  56.4 0.0 copy-start.8
  56.4 0.0 copy-done
  56.4 0.7 copy-done.8
  57.1 7.3 %input_rows.1 = f32[16,2,8,8,128]{4,3,2,1,0:T(8,128)} custom-call(s32[1]{0:T(128)} %bitcast.core, f32[16,4,8,128]{3,2,1,0:T(8,128)} %copy-done, f32[16,4,8,128]{3,2,1,0:T(8,128)} %copy-done.8, f32[4,512,256]{2,1,0:T(8,128)} %get-tuple-element.8.grads, bf16[8,512,128]{2,1,0:T(8,128)(2,1)} %constant.37.clone.forward_s, ...), custom_call_target="tpu_custom_call" | custom-call | flops 2500000000 | bytes 10000000 | tf_op jit(solution)/shard_map/input_rows/pallas_call | solution.py:285
  64.3 1.9 %all-to-all-done.1 = f32[16,8,8,128]{3,2,1,0:T(8,128)S(1)} async-done(((f32[16,8,8,128]{3,2,1,0:T(8,128)}), f32[16,8,8,128]{3,2,1,0:T(8,128)S(1)}, u32[]{:S(2)}, u32[]{:S(2)}) %all-to-all-start.1) | async-done | bytes 524320 | tf_op jit(solution)/shard_map/all_to_all | solution.py:358
  66.3 5.8 %all-to-all-start.2 = ((f32[16,2,8,8,128]{4,3,2,1,0:T(8,128)}), f32[16,2,8,8,128]{4,3,2,1,0:T(8,128)S(1)}, u32[]{:S(2)}, u32[]{:S(2)}) async-start(f32[16,2,8,8,128]{4,3,2,1,0:T(8,128)} %input_rows.1), calls=%async_computation.2 | async-start | bytes 2097152 | tf_op jit(solution)/shard_map/all_to_all | solution.py:362
  72.1 0.0 collective-permute-start.1
  72.1 1.2 %collective-permute-done.1 = f32[2,8,8,128]{3,2,1,0:T(8,128)S(1)} collective-permute-done((f32[2,8,8,128]{3,2,1,0:T(8,128)S(1)}, f32[2,8,8,128]{3,2,1,0:T(8,128)S(1)}, u32[]{:S(2)}, u32[]{:S(2)}) %collective-permute-start.1) | collective-permute-done | bytes 65568 | tf_op jit(solution)/shard_map/ppermute | solution.py:322
  73.4 2.0 %collective-permute-start.2 = (f32[2,8,8,128]{3,2,1,0:T(8,128)S(1)}, f32[2,8,8,128]{3,2,1,0:T(8,128)S(1)}, u32[]{:S(2)}, u32[]{:S(2)}) collective-permute-start(f32[2,8,8,128]{3,2,1,0:T(8,128)S(1)} %add.17), channel_id=1, source_target_pairs={{0,32},{16,240},{32,64},{48,16},{64,96},{80,48},{96,128},{112,80},... | collective-permute-start | bytes 196616 | tf_op jit(solution)/shard_map/ppermute | solution.py:322
  75.4 6.2 %collective-permute-done.2 = f32[2,8,8,128]{3,2,1,0:T(8,128)S(1)} collective-permute-done((f32[2,8,8,128]{3,2,1,0:T(8,128)S(1)}, f32[2,8,8,128]{3,2,1,0:T(8,128)S(1)}, u32[]{:S(2)}, u32[]{:S(2)}) %collective-permute-start.2) | collective-permute-done | bytes 65568 | tf_op jit(solution)/shard_map/ppermute | solution.py:322
  81.6 0.1 collective-permute-start.3
  81.7 6.9 %collective-permute-done.3 = f32[2,8,8,128]{3,2,1,0:T(8,128)S(1)} collective-permute-done((f32[2,8,8,128]{3,2,1,0:T(8,128)S(1)}, f32[2,8,8,128]{3,2,1,0:T(8,128)S(1)}, u32[]{:S(2)}, u32[]{:S(2)}) %collective-permute-start.3) | collective-permute-done | bytes 65568 | tf_op jit(solution)/shard_map/ppermute | solution.py:322
  88.6 0.1 collective-permute-start.4
  88.7 3.7 %collective-permute-done.4 = f32[2,8,8,128]{3,2,1,0:T(8,128)S(1)} collective-permute-done((f32[2,8,8,128]{3,2,1,0:T(8,128)S(1)}, f32[2,8,8,128]{3,2,1,0:T(8,128)S(1)}, u32[]{:S(2)}, u32[]{:S(2)}) %collective-permute-start.4) | collective-permute-done | bytes 65568 | tf_op jit(solution)/shard_map/ppermute | solution.py:322
  92.4 0.7 copy.32
  93.1 0.0 all-to-all-done.2
  93.1 0.1 fusion
  93.2 0.1 copy.25
  93.3 1.0 %convert_element_type.11 = bf16[2,16,8192]{2,1,0:T(8,128)(2,1)} reshape(bf16[2,16,8,8,128]{4,3,2,1,0:T(8,128)(2,1)S(1)} %copy.25) | data formatting | bytes 1048576 | tf_op jit(solution)/shard_map/convert_element_type | solution.py:368
  (9 shorter events, 0.1 us)
Async XLA Ops:
  0.6 2.7 %copy-start.7 = (f32[2,16,8192]{2,1,0:T(8,128)S(1)}, f32[2,16,8192]{2,1,0:T(8,128)}, u32[]{:S(2)}) copy-start(f32[2,16,8192]{2,1,0:T(8,128)} %param.10) | copy-start | bytes 3145732
  3.9 37.3 %copy-start.1 = (f32[8,2,128,128]{3,2,1,0:T(8,128)S(1)}, f32[8,2,128,128]{3,2,1,0:T(8,128)}, u32[]{:S(2)}) copy-start(f32[8,2,128,128]{3,2,1,0:T(8,128)} %constant.42.clone.over_l) | copy-start | bytes 3145732
  4.0 37.3 %copy-start.2 = (bf16[8,512,128]{2,1,0:T(8,128)(2,1)S(1)}, bf16[8,512,128]{2,1,0:T(8,128)(2,1)}, u32[]{:S(2)}) copy-start(bf16[8,512,128]{2,1,0:T(8,128)(2,1)} %constant.37.clone.forward_s) | copy-start | bytes 3145732
  4.0 37.3 %copy-start.3 = (f32[8,2,128,128]{3,2,1,0:T(8,128)S(1)}, f32[8,2,128,128]{3,2,1,0:T(8,128)}, u32[]{:S(2)}) copy-start(f32[8,2,128,128]{3,2,1,0:T(8,128)} %constant.41.clone.over_r) | copy-start | bytes 3145732
  4.0 37.3 %copy-start.4 = (bf16[2,256,256]{2,1,0:T(8,128)(2,1)S(1)}, bf16[2,256,256]{2,1,0:T(8,128)(2,1)}, u32[]{:S(2)}) copy-start(bf16[2,256,256]{2,1,0:T(8,128)(2,1)} %constant.40.clone.inverse_l) | copy-start | bytes 786436
  4.0 37.3 %copy-start.5 = (bf16[2,256,256]{2,1,0:T(8,128)(2,1)S(1)}, bf16[2,256,256]{2,1,0:T(8,128)(2,1)}, u32[]{:S(2)}) copy-start(bf16[2,256,256]{2,1,0:T(8,128)(2,1)} %constant.39.clone.forward_l) | copy-start | bytes 786436
  4.0 37.3 %copy-start.6 = (bf16[256,256]{1,0:T(8,128)(2,1)S(1)}, bf16[256,256]{1,0:T(8,128)(2,1)}, u32[]{:S(2)}) copy-start(bf16[256,256]{1,0:T(8,128)(2,1)} %constant.44.inverse_s) | copy-start | bytes 393220
  50.9 5.5 %copy-start = (f32[16,4,8,128]{3,2,1,0:T(8,128)}, f32[16,4,8,128]{3,2,1,0:T(8,128)S(1)}, u32[]{:S(2)}) copy-start(f32[16,4,8,128]{3,2,1,0:T(8,128)S(1)} %get-tuple-element.7.mine) | copy-start | bytes 786436
  50.9 5.5 %collective-permute-start = (f32[16,4,8,128]{3,2,1,0:T(8,128)S(1)}, f32[16,4,8,128]{3,2,1,0:T(8,128)S(1)}, u32[]{:S(2)}, u32[]{:S(2)}) collective-permute-start(f32[16,4,8,128]{3,2,1,0:T(8,128)S(1)} %get-tuple-element.7.mine), channel_id=1, source_target_pairs={{0,16},{16,0},{32,48},{48,32},{64,80},{80,64},{96,112},{112,96},{1... | collective-permute-start | bytes 786440 | tf_op jit(solution)/shard_map/ppermute | solution.py:357
  51.0 15.2 %all-to-all-start.1 = ((f32[16,8,8,128]{3,2,1,0:T(8,128)}), f32[16,8,8,128]{3,2,1,0:T(8,128)S(1)}, u32[]{:S(2)}, u32[]{:S(2)}) async-start(f32[16,8,8,128]{3,2,1,0:T(8,128)} %get-tuple-element.9), calls=%async_computation.1 | async-start | bytes 1048576 | tf_op jit(solution)/shard_map/all_to_all | solution.py:358
  56.4 0.7 copy-start.8
  66.3 26.8 %all-to-all-start.2 = ((f32[16,2,8,8,128]{4,3,2,1,0:T(8,128)}), f32[16,2,8,8,128]{4,3,2,1,0:T(8,128)S(1)}, u32[]{:S(2)}, u32[]{:S(2)}) async-start(f32[16,2,8,8,128]{4,3,2,1,0:T(8,128)} %input_rows.1), calls=%async_computation.2 | async-start | bytes 2097152 | tf_op jit(solution)/shard_map/all_to_all | solution.py:362
  72.1 1.3 %collective-permute-start.1 = (f32[2,8,8,128]{3,2,1,0:T(8,128)S(1)}, f32[2,8,8,128]{3,2,1,0:T(8,128)S(1)}, u32[]{:S(2)}, u32[]{:S(2)}) collective-permute-start(f32[2,8,8,128]{3,2,1,0:T(8,128)S(1)} %reduce_sum.9), channel_id=1, source_target_pairs={{0,16},{16,0},{32,48},{48,32},{64,80},{80,64},{96,112},{112,96},{1... | collective-permute-start | bytes 196616 | tf_op jit(solution)/shard_map/ppermute | solution.py:322
  73.4 8.2 %collective-permute-start.2 = (f32[2,8,8,128]{3,2,1,0:T(8,128)S(1)}, f32[2,8,8,128]{3,2,1,0:T(8,128)S(1)}, u32[]{:S(2)}, u32[]{:S(2)}) collective-permute-start(f32[2,8,8,128]{3,2,1,0:T(8,128)S(1)} %add.17), channel_id=1, source_target_pairs={{0,32},{16,240},{32,64},{48,16},{64,96},{80,48},{96,128},{112,80},... | collective-permute-start | bytes 196616 | tf_op jit(solution)/shard_map/ppermute | solution.py:322
  81.6 7.0 %collective-permute-start.3 = (f32[2,8,8,128]{3,2,1,0:T(8,128)S(1)}, f32[2,8,8,128]{3,2,1,0:T(8,128)S(1)}, u32[]{:S(2)}, u32[]{:S(2)}) collective-permute-start(f32[2,8,8,128]{3,2,1,0:T(8,128)S(1)} %add.18), channel_id=1, source_target_pairs={{0,64},{16,208},{32,96},{48,240},{64,128},{80,16},{96,160},{112,48... | collective-permute-start | bytes 196616 | tf_op jit(solution)/shard_map/ppermute | solution.py:322
  88.6 3.8 %collective-permute-start.4 = (f32[2,8,8,128]{3,2,1,0:T(8,128)S(1)}, f32[2,8,8,128]{3,2,1,0:T(8,128)S(1)}, u32[]{:S(2)}, u32[]{:S(2)}) collective-permute-start(f32[2,8,8,128]{3,2,1,0:T(8,128)S(1)} %add.19), channel_id=1, source_target_pairs={{0,48},{16,224},{32,80},{48,0},{64,112},{80,32},{96,144},{112,64},... | collective-permute-start | bytes 196616 | tf_op jit(solution)/shard_map/ppermute | solution.py:322

commit v4 on v3

--- a/solution.py
+++ b/solution.py
@@ -147,22 +147,30 @@
     return both[:SIDE] + both[SIDE:] + dot(table[:SIDE], low)
 
 
+def place(step, row, part):
+    tiles = RADIX * STEP // 8
+    block, first = divmod(((step * 2 + part) * 2 + row) * tiles, 4 * RADIX)
+    return block, pl.ds(first, tiles)
+
+
 def filter_kernel(
     rows, forward_s, inverse_s, forward_l, inverse_l, over_r, over_l,
-    terms, grads, half, z, back, held, sems,
+    terms, kept, half, z, back,
 ):
-    half[...] = rows[:, 4 * RADIX :]
+    own_half = rows[:, 4 * RADIX :]
+    half[...] = own_half
+    kept[:, 4 * RADIX :] = own_half
     over_s_forward(lambda row, r: rows[:, row * RADIX + r], 4, forward_s, z)
     size = RADIX * STEP
-    copies = []
     for step in range(SIDE // STEP):
         span = pl.ds(step * STEP, STEP)
         blocks = []
         for row in range(4):
             blocks += over_r_forward(z, row, span, over_l)
         spectra = dot_from_right(jnp.concatenate(blocks, axis=0), forward_l)
-        held[step] = spectra[2 * size :]
-        copies.append(pltpu.make_async_copy(held.at[step], grads.at[step], sems.at[step]))
+        for row in range(2):
+            for part, value in enumerate(parts(spectra[(2 + row) * size : (3 + row) * size])):
+                kept[place(step, row, part)] = value.reshape(size // 8, 8, LANES)
         first = times_conjugate(parts(spectra[2 * size : 3 * size]), parts(spectra[:size]))
         second = times_conjugate(parts(spectra[3 * size :]), parts(spectra[size : 2 * size]))
         product = jnp.concatenate([first[0] + second[0], first[1] + second[1]], axis=1)
@@ -174,40 +182,34 @@
                 high, low = split(value[part])
                 back[0, part, span, lanes] = high
                 back[1, part, span, lanes] = low
-    for copy in copies:
-        copy.start()
     shape = (2 * SIDE, RADIX * LANES)
     out = over_s_inverse(back[0].reshape(shape), back[1].reshape(shape), inverse_s[...])
     for r in range(RADIX):
         value = out[:, r * LANES : (r + 1) * LANES]
         terms[:, r] = value.reshape(terms.shape[0], terms.shape[2], LANES)
-    for copy in copies:
-        copy.wait()
 
 
 def input_kernel(
-    core, mine, other, grads, forward_s, inverse_s, forward_l, inverse_l, over_l,
-    out, z, back, grads_in, forward_in, inverse_in, turns_in, out_held, sems,
+    core, kept, other, forward_s, inverse_s, forward_l, inverse_l, over_l,
+    out, z, back, forward_in, inverse_in, turns_in, out_held, sems,
 ):
-    load_forward = pltpu.make_async_copy(forward_s, forward_in, sems.at[3 + RADIX])
+    load_forward = pltpu.make_async_copy(forward_s, forward_in, sems.at[2 + RADIX])
     load_forward.start()
     load_turns = pltpu.make_async_copy(over_l, turns_in, sems.at[0])
-    load_grads = pltpu.make_async_copy(grads, grads_in, sems.at[1])
-    load_inverse = pltpu.make_async_copy(inverse_s, inverse_in, sems.at[2])
-    for copy in (load_turns, load_grads, load_inverse):
+    load_inverse = pltpu.make_async_copy(inverse_s, inverse_in, sems.at[1])
+    for copy in (load_turns, load_inverse):
         copy.start()
     size = RADIX * STEP
     near = core[0] == 0
-    per_half = mine.shape[1]
+    per_half = other.shape[1]
 
     def filter_block(row, r):
-        own, far = mine[:, r % per_half], other[:, r % per_half]
+        own, far = kept[:, 4 * RADIX + r % per_half], other[:, r % per_half]
         return jnp.where(near, own, far) if r < per_half else jnp.where(near, far, own)
 
     load_forward.wait()
     over_s_forward(filter_block, 1, forward_in, z)
     load_turns.wait()
-    load_grads.wait()
     for step in range(SIDE // STEP):
         span = pl.ds(step * STEP, STEP)
         spectrum = dot_from_right(
@@ -215,10 +217,8 @@
         )
         products = []
         for row in range(2):
-            grad = grads_in[step, row * size : (row + 1) * size]
-            products.append(
-                jnp.concatenate(times_conjugate(parts(grad), parts(spectrum)), axis=1)
-            )
+            grad = [kept[place(step, row, part)].reshape(size, LANES) for part in range(2)]
+            products.append(jnp.concatenate(times_conjugate(grad, parts(spectrum)), axis=1))
         values = dot_from_right(jnp.concatenate(products, axis=0), inverse_l)
         for row in range(2):
             lanes = pl.ds(row * LANES, LANES)
@@ -236,7 +236,7 @@
         for row in range(2):
             value = samples[:, row * LANES : (row + 1) * LANES]
             out_held[:, row, r] = value.reshape(out.shape[0], out.shape[3], LANES)
-        copies.append(pltpu.make_async_copy(out_held.at[:, :, r], out.at[:, :, r], sems.at[3 + r]))
+        copies.append(pltpu.make_async_copy(out_held.at[:, :, r], out.at[:, :, r], sems.at[2 + r]))
         copies[-1].start()
     for copy in copies:
         copy.wait()
@@ -253,24 +253,21 @@
 def filter_terms(rows, consts):
     blocks, tiles, part, lanes = rows.shape
     forward_s, inverse_s, forward_l, inverse_l, over_r, over_l = consts
-    steps = SIDE // STEP
-    grads = (steps, 2 * RADIX * STEP, 2 * LANES)
     return pl.pallas_call(
         filter_kernel,
         out_shape=(
             jax.ShapeDtypeStruct((blocks, RADIX, part, lanes), jnp.float32),
-            jax.ShapeDtypeStruct(grads, jnp.float32),
+            jax.ShapeDtypeStruct(rows.shape, jnp.float32),
             jax.ShapeDtypeStruct((blocks, tiles - 4 * RADIX, part, lanes), jnp.float32),
         ),
         in_specs=in_vmem(7),
-        out_specs=(in_vmem(1)[0], in_hbm(1)[0], in_vmem(1)[0]),
+        out_specs=tuple(in_vmem(3)),
+        input_output_aliases={0: 1},
         scratch_shapes=[
             pltpu.VMEM((RADIX, 2, SIDE, 4 * LANES), jnp.float32),
             pltpu.VMEM((2, 2, SIDE, RADIX * LANES), jnp.bfloat16),
-            pltpu.VMEM(grads, jnp.float32),
-            pltpu.SemaphoreType.DMA((steps,)),
         ],
-        compiler_params=pltpu.CompilerParams(vmem_limit_bytes=48 << 20),
+        compiler_params=pltpu.CompilerParams(vmem_limit_bytes=20 << 20),
         cost_estimate=pl.CostEstimate(
             flops=4_000_000_000, bytes_accessed=10_000_000, transcendentals=0
         ),
@@ -278,8 +275,8 @@
     )(rows, forward_s, inverse_s[0], forward_l, inverse_l, over_r, over_l)
 
 
-def input_rows(core, mine, other, grads, consts):
-    blocks, tiles, part, lanes = mine.shape
+def input_rows(core, kept, other, consts):
+    blocks, tiles, part, lanes = kept.shape
     forward_s, inverse_s, forward_l, inverse_l, _, over_l = consts
     out = (blocks, 2, RADIX, part, lanes)
     return pl.pallas_call(
@@ -288,7 +285,7 @@
         in_specs=[
             pl.BlockSpec(memory_space=pltpu.SMEM),
             *in_vmem(2),
-            *in_hbm(3),
+            *in_hbm(2),
             *in_vmem(2),
             *in_hbm(1),
         ],
@@ -296,19 +293,18 @@
         scratch_shapes=[
             pltpu.VMEM((RADIX, 2, SIDE, LANES), jnp.float32),
             pltpu.VMEM((2, RADIX, 2, SIDE, 2 * LANES), jnp.bfloat16),
-            pltpu.VMEM(grads.shape, jnp.float32),
             pltpu.VMEM(forward_s.shape, jnp.bfloat16),
             pltpu.VMEM(inverse_s.shape, jnp.bfloat16),
             pltpu.VMEM(over_l.shape, jnp.float32),
             pltpu.VMEM(out, jnp.float32),
-            pltpu.SemaphoreType.DMA((4 + RADIX,)),
+            pltpu.SemaphoreType.DMA((3 + RADIX,)),
         ],
         compiler_params=pltpu.CompilerParams(vmem_limit_bytes=60 << 20),
         cost_estimate=pl.CostEstimate(
             flops=2_500_000_000, bytes_accessed=10_000_000, transcendentals=0
         ),
         name="input_rows",
-    )(core, mine, other, grads, forward_s, inverse_s, forward_l, inverse_l, over_l)
+    )(core, kept, other, forward_s, inverse_s, forward_l, inverse_l, over_l)
 
 
 def sum_over_chan(value, chan):
@@ -326,12 +322,12 @@
         total = value
         for shift in range(1, depth):
             total = total + moved(value, shift)
-        return total
+        return total, jnp.zeros_like(total)
     reach = 1
     while 2 * reach < depth:
         value = value + moved(value, reach)
         reach *= 2
-    return value + moved(value, 1, True)
+    return value, moved(value, 1, True)
 
 
 def local(saved_input, out_grad, filters):
@@ -353,19 +349,22 @@
     own_filter = jnp.tile(own_filter, (channels // groups, 1, 1, 1))
     packed = jnp.concatenate([*by_channel, own_filter], axis=1)
     rows = lax.all_to_all(packed, "ctx", 0, 0, tiled=True)
-    terms, grads, mine = filter_terms(rows, consts)
+    terms, kept, mine = filter_terms(rows, consts)
     other = lax.ppermute(mine, "chan", [(i, i ^ 1) for i in range(chan)])
     terms = lax.all_to_all(terms, "ctx", 0, 0, tiled=True)
-    inputs = input_rows(core.reshape(1), mine, other, grads, consts)
+    inputs = input_rows(core.reshape(1), kept, other, consts)
     total = jnp.sum(terms.reshape(devices // groups, groups, RADIX, part, LANES), axis=0)
     inputs, total = lax.optimization_barrier((inputs, total))
     inputs = lax.all_to_all(inputs, "ctx", 0, 0, tiled=True)
-    total = sum_over_chan(total, chan)
+    inputs = (inputs * (1.0 / TOKENS)).transpose(1, 0, 3, 2, 4)
+    input_grad = inputs.reshape(batch, channels, tokens).astype(jnp.bfloat16)
+    total, last = sum_over_chan(total, chan)
+    input_grad, last = lax.optimization_barrier((input_grad, last))
+    total = total + last
     per_filter = channels // groups
     norm = float(tokens * devices * batch * per_filter * chan) ** -0.5
     filter_grad = total.swapaxes(1, 2).reshape(groups, tokens) * (norm / TOKENS)
-    input_grad = (inputs * (1.0 / TOKENS)).transpose(1, 0, 3, 2, 4)
-    return input_grad.reshape(batch, channels, tokens).astype(jnp.bfloat16), filter_grad
+    return input_grad, filter_grad
 
 
 def solution(mesh):

time: 94.8 us -> 92.4 us (0.975)
  Pallas kernels: 16.9 us -> 14.9 us
  waiting for transfers between devices: 19.9 us -> 18.4 us
  local copies, waits for them, and re-layouts: 5.57 us -> 7 us
    pallas_call x1, Pallas kernels: 9.62 us -> 7.25 us  [filter_terms(): pl.pallas_call(filter_kernel, out_shape=(jax.ShapeDtypeStruct((blocks, RA...]
    unnamed x21, local copies, waits for them, and re-layouts: 3.02 us -> 4.45 us
    ppermute x4, waiting for transfers between devices: 18 us -> 16.8 us  [moved(): return lax.ppermute(array, 'chan', ring)]
where the time goes in v4:
time: 92.4 us; the launch traced here: 91.9 us
  blocking collectives  37.1 us (40%)
  waiting for transfers between devices  18.4 us (20%)
  Pallas kernels  14.9 us (16%)
  starting transfers between devices  13.4 us (15%)
  local copies, waits for them, and re-layouts  7 us (8%)
    all_to_all x1, blocking collectives, local(): rows = lax.all_to_all(packed, 'ctx', 0, 0, tiled=True)  37.1 us
    ppermute x4, waiting for transfers between devices, moved(): return lax.ppermute(array, 'chan', ring)  16.8 us
    pallas_call x1, Pallas kernels, input_rows(): pl.pallas_call(input_kernel, out_shape=jax.ShapeDtypeStruct(out, jnp.floa...  7.6 us
    pallas_call x1, Pallas kernels, filter_terms(): pl.pallas_call(filter_kernel, out_shape=(jax.ShapeDtypeStruct((blocks, RA...  7.25 us
    all_to_all x1, starting transfers between devices, local(): inputs = lax.all_to_all(inputs, 'ctx', 0, 0, tiled=True)  5.84 us
    all_to_all x1, starting transfers between devices, local(): terms = lax.all_to_all(terms, 'ctx', 0, 0, tiled=True)  5.34 us
    unnamed x21, local copies, waits for them, and re-layouts  4.45 us
    ppermute x4, starting transfers between devices, moved(): return lax.ppermute(array, 'chan', ring)  2.17 us
  transfers between devices with their start and end apart: 7, of which 5 were waited for; matrix products, arithmetic and copies ran while one was open for 1% of the time, Pallas kernels for 8%

profile of v4, /device:TPU:2, one launch (start us, length us, event | category | flops | bytes accessed | tf_op | source)
XLA Modules:
  0.0 91.9 jit_solution(13657936774842531911)
XLA Ops:
  0.6 0.0 copy-start.7
  0.7 1.0 %reshape.41 = f32[2,8,2,4,128]{4,3,2,1,0:T(4,128)S(1)} reshape(f32[2,8192]{1,0:T(2,128)} %param.11) | data formatting | bytes 131072 | tf_op jit(solution)/shard_map/reshape | solution.py:347
  1.7 1.4 %copy.28 = f32[4,8,64,128]{3,2,1,0:T(8,128)S(1)} copy(f32[4,8,64,128]{3,1,2,0:T(8,128)} %bitcast.40) | data formatting | bytes 2097152
  3.1 0.2 copy.23
  3.3 0.0 copy-done.7
  3.3 0.2 copy.29
  3.5 0.2 copy.24
  3.7 0.2 pad_maximum_fusion
  3.9 0.0 copy-start.1
  4.0 0.0 copy-start.2
  4.0 0.0 copy-start.3
  4.0 0.0 copy-start.4
  4.0 0.0 copy-start.5
  4.0 0.0 copy-start.6
  4.0 37.1 %all_to_all.15.rows = f32[16,36,8,128]{3,2,1,0:T(8,128)S(1)} all-to-all(f32[16,36,8,128]{3,2,1,0:T(8,128)S(1)} %pad_maximum_fusion), channel_id=1, replica_groups=mesh['chan'=16,'ctx'=16] {'ctx'}, dimensions={0} | all-to-all | bytes 4718592 | tf_op jit(solution)/shard_map/all_to_all | solution.py:351
  41.1 0.0 copy-done.1
  41.1 0.0 copy-done.2
  41.1 0.0 copy-done.3
  41.1 0.0 copy-done.4
  41.1 0.0 copy-done.5
  41.2 0.0 copy-done.6
  41.2 7.3 %filter_terms.1 = (f32[16,8,8,128]{3,2,1,0:T(8,128)}, f32[16,36,8,128]{3,2,1,0:T(8,128)S(1)}, f32[16,4,8,128]{3,2,1,0:T(8,128)S(1)}) custom-call(f32[16,36,8,128]{3,2,1,0:T(8,128)S(1)} %all_to_all.15.rows, bf16[8,512,128]{2,1,0:T(8,128)(2,1)S(1)} %copy-done.2, bf16[256,256]{1,0:T(8,128)(2,1)S(1)} %copy-done.6, ...), custom_call_target="tpu_custom_call", output_to_operand_aliasing={{1}: (0, {})} | custom-call | flops 4000000000 | bytes 10000000 | tf_op jit(solution)/shard_map/filter_terms/pallas_call | solution.py:256
  48.4 0.0 copy-start
  48.4 1.4 %copy-done = f32[16,36,8,128]{3,2,1,0:T(8,128)} copy-done((f32[16,36,8,128]{3,2,1,0:T(8,128)}, f32[16,36,8,128]{3,2,1,0:T(8,128)S(1)}, u32[]{:S(2)}) %copy-start) | copy-done | bytes 2359320
  49.9 0.0 collective-permute-start
  49.9 5.3 %all-to-all-start.1 = ((f32[16,8,8,128]{3,2,1,0:T(8,128)}), f32[16,8,8,128]{3,2,1,0:T(8,128)S(1)}, u32[]{:S(2)}, u32[]{:S(2)}) async-start(f32[16,8,8,128]{3,2,1,0:T(8,128)} %get-tuple-element.11), calls=%async_computation.1 | async-start | bytes 1048576 | tf_op jit(solution)/shard_map/all_to_all | solution.py:354
  55.2 0.0 collective-permute-done.other
  55.2 0.0 copy-start.8
  55.2 0.7 copy-done.8
  55.9 7.6 %input_rows.1 = f32[16,2,8,8,128]{4,3,2,1,0:T(8,128)} custom-call(s32[1]{0:T(128)} %bitcast.core, f32[16,36,8,128]{3,2,1,0:T(8,128)} %copy-done, f32[16,4,8,128]{3,2,1,0:T(8,128)} %copy-done.8, bf16[8,512,128]{2,1,0:T(8,128)(2,1)} %constant.37.clone.forward_s, bf16[8,256,256]{2,1,0:T(8,128)(2,1)} %constant.38.clone.inverse_s, ...), custom_call_target="tpu_custom_call" | custom-call | flops 2500000000 | bytes 10000000 | tf_op jit(solution)/shard_map/input_rows/pallas_call | solution.py:282
  63.5 1.6 %all-to-all-done.1 = f32[16,8,8,128]{3,2,1,0:T(8,128)S(1)} async-done(((f32[16,8,8,128]{3,2,1,0:T(8,128)}), f32[16,8,8,128]{3,2,1,0:T(8,128)S(1)}, u32[]{:S(2)}, u32[]{:S(2)}) %all-to-all-start.1) | async-done | bytes 524320 | tf_op jit(solution)/shard_map/all_to_all | solution.py:354
  65.1 5.8 %all-to-all-start.2 = ((f32[16,2,8,8,128]{4,3,2,1,0:T(8,128)}), f32[16,2,8,8,128]{4,3,2,1,0:T(8,128)S(1)}, u32[]{:S(2)}, u32[]{:S(2)}) async-start(f32[16,2,8,8,128]{4,3,2,1,0:T(8,128)} %input_rows.1), calls=%async_computation.2 | async-start | bytes 2097152 | tf_op jit(solution)/shard_map/all_to_all | solution.py:358
  71.0 0.0 collective-permute-start.1
  71.0 1.2 %collective-permute-done.1 = f32[2,8,8,128]{3,2,1,0:T(8,128)S(1)} collective-permute-done((f32[2,8,8,128]{3,2,1,0:T(8,128)S(1)}, f32[2,8,8,128]{3,2,1,0:T(8,128)S(1)}, u32[]{:S(2)}, u32[]{:S(2)}) %collective-permute-start.1) | collective-permute-done | bytes 65568 | tf_op jit(solution)/shard_map/ppermute | solution.py:318
  72.2 2.0 %collective-permute-start.2 = (f32[2,8,8,128]{3,2,1,0:T(8,128)S(1)}, f32[2,8,8,128]{3,2,1,0:T(8,128)S(1)}, u32[]{:S(2)}, u32[]{:S(2)}) collective-permute-start(f32[2,8,8,128]{3,2,1,0:T(8,128)S(1)} %add.17), channel_id=1, source_target_pairs={{0,32},{16,240},{32,64},{48,16},{64,96},{80,48},{96,128},{112,80},... | collective-permute-start | bytes 196616 | tf_op jit(solution)/shard_map/ppermute | solution.py:318
  74.2 6.2 %collective-permute-done.2 = f32[2,8,8,128]{3,2,1,0:T(8,128)S(1)} collective-permute-done((f32[2,8,8,128]{3,2,1,0:T(8,128)S(1)}, f32[2,8,8,128]{3,2,1,0:T(8,128)S(1)}, u32[]{:S(2)}, u32[]{:S(2)}) %collective-permute-start.2) | collective-permute-done | bytes 65568 | tf_op jit(solution)/shard_map/ppermute | solution.py:318
  80.4 0.1 collective-permute-start.3
  80.5 6.9 %collective-permute-done.3 = f32[2,8,8,128]{3,2,1,0:T(8,128)S(1)} collective-permute-done((f32[2,8,8,128]{3,2,1,0:T(8,128)S(1)}, f32[2,8,8,128]{3,2,1,0:T(8,128)S(1)}, u32[]{:S(2)}, u32[]{:S(2)}) %collective-permute-start.3) | collective-permute-done | bytes 65568 | tf_op jit(solution)/shard_map/ppermute | solution.py:318
  87.4 0.1 collective-permute-start.4
  87.5 0.0 all-to-all-done.2
  87.6 0.1 fusion
  87.7 0.1 copy.26
  87.8 1.0 %convert_element_type.11 = bf16[2,16,8192]{2,1,0:T(8,128)(2,1)} reshape(bf16[2,16,8,8,128]{4,3,2,1,0:T(8,128)(2,1)S(1)} %copy.26) | data formatting | bytes 1048576 | tf_op jit(solution)/shard_map/convert_element_type | solution.py:360
  88.8 2.4 %collective-permute-done.4 = f32[2,8,8,128]{3,2,1,0:T(8,128)S(1)} collective-permute-done((f32[2,8,8,128]{3,2,1,0:T(8,128)S(1)}, f32[2,8,8,128]{3,2,1,0:T(8,128)S(1)}, u32[]{:S(2)}, u32[]{:S(2)}) %collective-permute-start.4) | collective-permute-done | bytes 65568 | tf_op jit(solution)/shard_map/ppermute | solution.py:318
  91.3 0.7 copy.33
  (9 shorter events, 0.1 us)
Async XLA Ops:
  0.6 2.7 %copy-start.7 = (f32[2,16,8192]{2,1,0:T(8,128)S(1)}, f32[2,16,8192]{2,1,0:T(8,128)}, u32[]{:S(2)}) copy-start(f32[2,16,8192]{2,1,0:T(8,128)} %param.10) | copy-start | bytes 3145732
  3.9 37.2 %copy-start.1 = (f32[8,2,128,128]{3,2,1,0:T(8,128)S(1)}, f32[8,2,128,128]{3,2,1,0:T(8,128)}, u32[]{:S(2)}) copy-start(f32[8,2,128,128]{3,2,1,0:T(8,128)} %constant.42.clone.over_l) | copy-start | bytes 3145732
  4.0 37.2 %copy-start.2 = (bf16[8,512,128]{2,1,0:T(8,128)(2,1)S(1)}, bf16[8,512,128]{2,1,0:T(8,128)(2,1)}, u32[]{:S(2)}) copy-start(bf16[8,512,128]{2,1,0:T(8,128)(2,1)} %constant.37.clone.forward_s) | copy-start | bytes 3145732
  4.0 37.2 %copy-start.3 = (f32[8,2,128,128]{3,2,1,0:T(8,128)S(1)}, f32[8,2,128,128]{3,2,1,0:T(8,128)}, u32[]{:S(2)}) copy-start(f32[8,2,128,128]{3,2,1,0:T(8,128)} %constant.41.clone.over_r) | copy-start | bytes 3145732
  4.0 37.2 %copy-start.4 = (bf16[2,256,256]{2,1,0:T(8,128)(2,1)S(1)}, bf16[2,256,256]{2,1,0:T(8,128)(2,1)}, u32[]{:S(2)}) copy-start(bf16[2,256,256]{2,1,0:T(8,128)(2,1)} %constant.40.clone.inverse_l) | copy-start | bytes 786436
  4.0 37.2 %copy-start.5 = (bf16[2,256,256]{2,1,0:T(8,128)(2,1)S(1)}, bf16[2,256,256]{2,1,0:T(8,128)(2,1)}, u32[]{:S(2)}) copy-start(bf16[2,256,256]{2,1,0:T(8,128)(2,1)} %constant.39.clone.forward_l) | copy-start | bytes 786436
  4.0 37.2 %copy-start.6 = (bf16[256,256]{1,0:T(8,128)(2,1)S(1)}, bf16[256,256]{1,0:T(8,128)(2,1)}, u32[]{:S(2)}) copy-start(bf16[256,256]{1,0:T(8,128)(2,1)} %constant.44.inverse_s) | copy-start | bytes 393220
  48.4 1.4 %copy-start = (f32[16,36,8,128]{3,2,1,0:T(8,128)}, f32[16,36,8,128]{3,2,1,0:T(8,128)S(1)}, u32[]{:S(2)}) copy-start(f32[16,36,8,128]{3,2,1,0:T(8,128)S(1)} %get-tuple-element.9.kept) | copy-start | bytes 7077892
  49.9 5.4 %collective-permute-start = (f32[16,4,8,128]{3,2,1,0:T(8,128)S(1)}, f32[16,4,8,128]{3,2,1,0:T(8,128)S(1)}, u32[]{:S(2)}, u32[]{:S(2)}) collective-permute-start(f32[16,4,8,128]{3,2,1,0:T(8,128)S(1)} %get-tuple-element.10), channel_id=1, source_target_pairs={{0,16},{16,0},{32,48},{48,32},{64,80},{80,64},{96,112},{112,96},{1... | collective-permute-start | bytes 786440 | tf_op jit(solution)/shard_map/ppermute | solution.py:353
  49.9 15.2 %all-to-all-start.1 = ((f32[16,8,8,128]{3,2,1,0:T(8,128)}), f32[16,8,8,128]{3,2,1,0:T(8,128)S(1)}, u32[]{:S(2)}, u32[]{:S(2)}) async-start(f32[16,8,8,128]{3,2,1,0:T(8,128)} %get-tuple-element.11), calls=%async_computation.1 | async-start | bytes 1048576 | tf_op jit(solution)/shard_map/all_to_all | solution.py:354
  55.2 0.7 copy-start.8
  65.1 22.4 %all-to-all-start.2 = ((f32[16,2,8,8,128]{4,3,2,1,0:T(8,128)}), f32[16,2,8,8,128]{4,3,2,1,0:T(8,128)S(1)}, u32[]{:S(2)}, u32[]{:S(2)}) async-start(f32[16,2,8,8,128]{4,3,2,1,0:T(8,128)} %input_rows.1), calls=%async_computation.2 | async-start | bytes 2097152 | tf_op jit(solution)/shard_map/all_to_all | solution.py:358
  71.0 1.3 %collective-permute-start.1 = (f32[2,8,8,128]{3,2,1,0:T(8,128)S(1)}, f32[2,8,8,128]{3,2,1,0:T(8,128)S(1)}, u32[]{:S(2)}, u32[]{:S(2)}) collective-permute-start(f32[2,8,8,128]{3,2,1,0:T(8,128)S(1)} %reduce_sum.9), channel_id=1, source_target_pairs={{0,16},{16,0},{32,48},{48,32},{64,80},{80,64},{96,112},{112,96},{1... | collective-permute-start | bytes 196616 | tf_op jit(solution)/shard_map/ppermute | solution.py:318
  72.2 8.2 %collective-permute-start.2 = (f32[2,8,8,128]{3,2,1,0:T(8,128)S(1)}, f32[2,8,8,128]{3,2,1,0:T(8,128)S(1)}, u32[]{:S(2)}, u32[]{:S(2)}) collective-permute-start(f32[2,8,8,128]{3,2,1,0:T(8,128)S(1)} %add.17), channel_id=1, source_target_pairs={{0,32},{16,240},{32,64},{48,16},{64,96},{80,48},{96,128},{112,80},... | collective-permute-start | bytes 196616 | tf_op jit(solution)/shard_map/ppermute | solution.py:318
  80.4 7.0 %collective-permute-start.3 = (f32[2,8,8,128]{3,2,1,0:T(8,128)S(1)}, f32[2,8,8,128]{3,2,1,0:T(8,128)S(1)}, u32[]{:S(2)}, u32[]{:S(2)}) collective-permute-start(f32[2,8,8,128]{3,2,1,0:T(8,128)S(1)} %add.18), channel_id=1, source_target_pairs={{0,64},{16,208},{32,96},{48,240},{64,128},{80,16},{96,160},{112,48... | collective-permute-start | bytes 196616 | tf_op jit(solution)/shard_map/ppermute | solution.py:318
  87.4 3.8 %collective-permute-start.4 = (f32[2,8,8,128]{3,2,1,0:T(8,128)S(1)}, f32[2,8,8,128]{3,2,1,0:T(8,128)S(1)}, u32[]{:S(2)}, u32[]{:S(2)}) collective-permute-start(f32[2,8,8,128]{3,2,1,0:T(8,128)S(1)} %add.19), channel_id=1, source_target_pairs={{0,48},{16,224},{32,80},{48,0},{64,112},{80,32},{96,144},{112,64},... | collective-permute-start | bytes 196616 | tf_op jit(solution)/shard_map/ppermute | solution.py:318

commit v5 on v3

--- a/solution.py
+++ b/solution.py
@@ -250,6 +250,56 @@
     return [pl.BlockSpec(memory_space=pltpu.HBM)] * count
 
 
+def layout_kernel(core, saved_input, out_grad, filters, out, samples, filter_in, sems):
+    batch, channels, tokens = saved_input.shape
+    groups = filters.shape[0]
+    per_half = RADIX // 2
+    loads = []
+    for array, source in enumerate((saved_input, out_grad)):
+        for b in range(batch):
+            slot = array * batch + b
+            loads.append(pltpu.make_async_copy(source.at[b], samples.at[slot], sems.at[slot]))
+    load_filter = pltpu.make_async_copy(filters, filter_in, sems.at[2 * batch])
+    for copy in [load_filter, *loads]:
+        copy.start()
+    load_filter.wait()
+    for group in range(groups):
+        for r in range(per_half):
+            for s in range(tokens // (RADIX * LANES)):
+                start = pl.multiple_of((s * RADIX + core[0] * per_half + r) * LANES, LANES)
+                row = filter_in[pl.ds(group, 1), pl.ds(start, LANES)]
+                out[group, 2 * batch * RADIX + r, pl.ds(s, 1), :] = row
+    for channel in range(groups, channels):
+        out[channel, 2 * batch * RADIX :] = out[channel % groups, 2 * batch * RADIX :]
+    for slot, load in enumerate(loads):
+        load.wait()
+        for first in range(0, channels, 8):
+            for r in range(RADIX):
+                for s in range(tokens // (RADIX * LANES)):
+                    value = samples[slot, pl.ds(first, 8), pl.ds((s * RADIX + r) * LANES, LANES)]
+                    out[pl.ds(first, 8), slot * RADIX + r, s, :] = value
+
+
+def laid_out(core, saved_input, out_grad, filters):
+    arrays = (saved_input, out_grad, filters)
+    batch, channels, tokens = saved_input.shape
+    part = tokens // (RADIX * LANES)
+    tiles = 2 * batch * RADIX + RADIX // 2
+    return pl.pallas_call(
+        layout_kernel,
+        out_shape=jax.ShapeDtypeStruct((channels, tiles, part, LANES), jnp.float32),
+        in_specs=[pl.BlockSpec(memory_space=pltpu.SMEM), *in_hbm(3)],
+        out_specs=in_vmem(1)[0],
+        scratch_shapes=[
+            pltpu.VMEM((2 * batch, channels, tokens), jnp.float32),
+            pltpu.VMEM(filters.shape, jnp.float32),
+            pltpu.SemaphoreType.DMA((2 * batch + 1,)),
+        ],
+        compiler_params=pltpu.CompilerParams(vmem_limit_bytes=40 << 20),
+        name="laid_out",
+    )(core, *(pltpu.with_memory_space_constraint(v, pltpu.HBM) for v in arrays))
+
+
 def filter_terms(rows, consts):
     blocks, tiles, part, lanes = rows.shape
     forward_s, inverse_s, forward_l, inverse_l, over_r, over_l = consts
@@ -259,7 +309,7 @@
         filter_kernel,
         out_shape=(
             jax.ShapeDtypeStruct((blocks, RADIX, part, lanes), jnp.float32),
-            jax.ShapeDtypeStruct(grads, jnp.float32),
+            pltpu.HBM(grads, jnp.float32),
             jax.ShapeDtypeStruct((blocks, tiles - 4 * RADIX, part, lanes), jnp.float32),
         ),
         in_specs=in_vmem(7),
@@ -270,7 +320,7 @@
             pltpu.VMEM(grads, jnp.float32),
             pltpu.SemaphoreType.DMA((steps,)),
         ],
-        compiler_params=pltpu.CompilerParams(vmem_limit_bytes=48 << 20),
+        compiler_params=pltpu.CompilerParams(vmem_limit_bytes=20 << 20),
         cost_estimate=pl.CostEstimate(
             flops=4_000_000_000, bytes_accessed=10_000_000, transcendentals=0
         ),
@@ -326,12 +376,12 @@
         total = value
         for shift in range(1, depth):
             total = total + moved(value, shift)
-        return total
+        return total, jnp.zeros_like(total)
     reach = 1
     while 2 * reach < depth:
         value = value + moved(value, reach)
         reach *= 2
-    return value + moved(value, 1, True)
+    return value, moved(value, 1, True)
 
 
 def local(saved_input, out_grad, filters):
@@ -341,17 +391,8 @@
     chan = lax.axis_size("chan")
     core = lax.axis_index("chan") % 2
     part = tokens // (RADIX * LANES)
-    half = RADIX // 2
     consts = tuple(jnp.asarray(t) for t in tables())
-    shape = (batch, channels, part, RADIX, LANES)
-    by_channel = [
-        v.reshape(shape).transpose(1, 0, 3, 2, 4).reshape(channels, batch * RADIX, part, LANES)
-        for v in (saved_input, out_grad)
-    ]
-    own_filter = filters.reshape(groups, part, 2, half, LANES)
-    own_filter = jnp.where(core == 0, own_filter[:, :, 0], own_filter[:, :, 1]).swapaxes(1, 2)
-    own_filter = jnp.tile(own_filter, (channels // groups, 1, 1, 1))
-    packed = jnp.concatenate([*by_channel, own_filter], axis=1)
+    packed = laid_out(core.reshape(1), saved_input, out_grad, filters)
     rows = lax.all_to_all(packed, "ctx", 0, 0, tiled=True)
     terms, grads, mine = filter_terms(rows, consts)
     other = lax.ppermute(mine, "chan", [(i, i ^ 1) for i in range(chan)])
@@ -360,12 +401,15 @@
     total = jnp.sum(terms.reshape(devices // groups, groups, RADIX, part, LANES), axis=0)
     inputs, total = lax.optimization_barrier((inputs, total))
     inputs = lax.all_to_all(inputs, "ctx", 0, 0, tiled=True)
-    total = sum_over_chan(total, chan)
+    inputs = (inputs * (1.0 / TOKENS)).transpose(1, 0, 3, 2, 4)
+    input_grad = inputs.reshape(batch, channels, tokens).astype(jnp.bfloat16)
+    total, last = sum_over_chan(total, chan)
+    input_grad, last = lax.optimization_barrier((input_grad, last))
+    total = total + last
     per_filter = channels // groups
     norm = float(tokens * devices * batch * per_filter * chan) ** -0.5
     filter_grad = total.swapaxes(1, 2).reshape(groups, tokens) * (norm / TOKENS)
-    input_grad = (inputs * (1.0 / TOKENS)).transpose(1, 0, 3, 2, 4)
-    return input_grad.reshape(batch, channels, tokens).astype(jnp.bfloat16), filter_grad
+    return input_grad, filter_grad
 
 
 def solution(mesh):

time: 94.8 us -> 90.6 us (0.956)
  local copies, waits for them, and re-layouts: 5.57 us -> 2.54 us
  waiting for transfers between devices: 19.9 us -> 18.6 us
    pallas_call x0 -> x1, Pallas kernels: none -> 2.28 us  [laid_out(): pl.pallas_call(layout_kernel, out_shape=jax.ShapeDtypeStruct((channels, t...]
    pallas_call x1, Pallas kernels: 9.62 us -> 7.87 us  [filter_terms(): pl.pallas_call(filter_kernel, out_shape=(jax.ShapeDtypeStruct((blocks, RA...]
    unnamed x21 -> x17, local copies, waits for them, and re-layouts: 3.02 us -> 1.41 us
    reshape x3 -> x0, local copies, waits for them, and re-layouts: 1.39 us -> none  [the longest x1 0.99 us: local(): own_filter = filters.reshape(groups, part, 2, half, LANES)]
    ppermute x4, waiting for transfers between devices: 18 us -> 16.8 us  [moved(): return lax.ppermute(array, 'chan', ring)]
where the time goes in v5:
time: 90.6 us; the launch traced here: 90.2 us
  blocking collectives  37.1 us (41%)
  waiting for transfers between devices  18.6 us (21%)
  Pallas kernels  17.4 us (19%)
  starting transfers between devices  13.5 us (15%)
  local copies, waits for them, and re-layouts  2.54 us (3%)
    all_to_all x1, blocking collectives, local(): rows = lax.all_to_all(packed, 'ctx', 0, 0, tiled=True)  37.1 us
    ppermute x4, waiting for transfers between devices, moved(): return lax.ppermute(array, 'chan', ring)  16.8 us
    pallas_call x1, Pallas kernels, filter_terms(): pl.pallas_call(filter_kernel, out_shape=(jax.ShapeDtypeStruct((blocks, RA...  7.87 us
    pallas_call x1, Pallas kernels, input_rows(): pl.pallas_call(input_kernel, out_shape=jax.ShapeDtypeStruct(out, jnp.floa...  7.3 us
    all_to_all x1, starting transfers between devices, local(): inputs = lax.all_to_all(inputs, 'ctx', 0, 0, tiled=True)  5.84 us
    all_to_all x1, starting transfers between devices, local(): terms = lax.all_to_all(terms, 'ctx', 0, 0, tiled=True)  5.36 us
    pallas_call x1, Pallas kernels, laid_out(): pl.pallas_call(layout_kernel, out_shape=jax.ShapeDtypeStruct((channels, t...  2.28 us
    ppermute x4, starting transfers between devices, moved(): return lax.ppermute(array, 'chan', ring)  2.17 us
  transfers between devices with their start and end apart: 7, of which 5 were waited for; matrix products, arithmetic and copies ran while one was open for 1% of the time, Pallas kernels for 8%

profile of v5, /device:TPU:2, one launch (start us, length us, event | category | flops | bytes accessed | tf_op | source)
XLA Modules:
  0.0 90.2 jit_solution(11772584798072957729)
XLA Ops:
  0.6 2.3 %laid_out.1 = f32[16,36,8,128]{3,2,1,0:T(8,128)S(1)} custom-call(s32[1]{0:T(128)} %bitcast.core, f32[2,16,8192]{2,1,0:T(8,128)} %saved_input.1, f32[2,16,8192]{2,1,0:T(8,128)} %out_grad.1, f32[2,8192]{1,0:T(2,128)} %filters.1), custom_call_target="tpu_custom_call" | custom-call | tf_op jit(solution)/shard_map/laid_out/pallas_call | solution.py:288
  2.9 0.0 copy-start.1
  2.9 0.0 copy-start.2
  3.0 0.0 copy-start.3
  3.0 0.0 copy-start.4
  3.0 0.0 copy-start.5
  3.0 0.0 copy-start.6
  3.0 37.1 %all_to_all.15.rows = f32[16,36,8,128]{3,2,1,0:T(8,128)S(1)} all-to-all(f32[16,36,8,128]{3,2,1,0:T(8,128)S(1)} %laid_out.1), channel_id=1, replica_groups=mesh['chan'=16,'ctx'=16] {'ctx'}, dimensions={0} | all-to-all | bytes 4718592 | tf_op jit(solution)/shard_map/all_to_all | solution.py:396
  40.1 0.0 copy-done.1
  40.1 0.0 copy-done.2
  40.1 0.0 copy-done.3
  40.1 0.0 copy-done.4
  40.1 0.0 copy-done.5
  40.1 0.0 copy-done.6
  40.1 7.9 %filter_terms.1 = (f32[16,8,8,128]{3,2,1,0:T(8,128)}, f32[4,512,256]{2,1,0:T(8,128)}, f32[16,4,8,128]{3,2,1,0:T(8,128)S(1)}) custom-call(f32[16,36,8,128]{3,2,1,0:T(8,128)S(1)} %all_to_all.15.rows, bf16[8,512,128]{2,1,0:T(8,128)(2,1)S(1)} %copy-done.2, bf16[256,256]{1,0:T(8,128)(2,1)S(1)} %copy-done.6, bf16[2,256,256]{2,1,0:T(8,128)(2,1)S(1)} %copy-done.5, ...), custom_call_target="tpu_custom_call" | custom-call | flops 4000000000 | bytes 10000000 | tf_op jit(solution)/shard_map/filter_terms/pallas_call | solution.py:308
  48.0 0.0 copy-start
  48.0 0.1 collective-permute-start
  48.1 5.4 %all-to-all-start.1 = ((f32[16,8,8,128]{3,2,1,0:T(8,128)}), f32[16,8,8,128]{3,2,1,0:T(8,128)S(1)}, u32[]{:S(2)}, u32[]{:S(2)}) async-start(f32[16,8,8,128]{3,2,1,0:T(8,128)} %get-tuple-element.11), calls=%async_computation.1 | async-start | bytes 1048576 | tf_op jit(solution)/shard_map/all_to_all | solution.py:399
  53.5 0.0 collective-permute-done.other
  53.5 0.0 copy-start.7
  53.5 0.0 copy-done
  53.5 0.7 copy-done.7
  54.2 7.3 %input_rows.1 = f32[16,2,8,8,128]{4,3,2,1,0:T(8,128)} custom-call(s32[1]{0:T(128)} %bitcast.core, f32[16,4,8,128]{3,2,1,0:T(8,128)} %copy-done, f32[16,4,8,128]{3,2,1,0:T(8,128)} %copy-done.7, f32[4,512,256]{2,1,0:T(8,128)} %get-tuple-element.10.grads, bf16[8,512,128]{2,1,0:T(8,128)(2,1)} %constant.36.clone.forward_s, ...), custom_call_target="tpu_custom_call" | custom-call | flops 2500000000 | bytes 10000000 | tf_op jit(solution)/shard_map/input_rows/pallas_call | solution.py:335
  61.5 1.9 %all-to-all-done.1 = f32[16,8,8,128]{3,2,1,0:T(8,128)S(1)} async-done(((f32[16,8,8,128]{3,2,1,0:T(8,128)}), f32[16,8,8,128]{3,2,1,0:T(8,128)S(1)}, u32[]{:S(2)}, u32[]{:S(2)}) %all-to-all-start.1) | async-done | bytes 524320 | tf_op jit(solution)/shard_map/all_to_all | solution.py:399
  63.4 5.8 %all-to-all-start.2 = ((f32[16,2,8,8,128]{4,3,2,1,0:T(8,128)}), f32[16,2,8,8,128]{4,3,2,1,0:T(8,128)S(1)}, u32[]{:S(2)}, u32[]{:S(2)}) async-start(f32[16,2,8,8,128]{4,3,2,1,0:T(8,128)} %input_rows.1), calls=%async_computation.2 | async-start | bytes 2097152 | tf_op jit(solution)/shard_map/all_to_all | solution.py:403
  69.2 0.0 collective-permute-start.1
  69.2 1.2 %collective-permute-done.1 = f32[2,8,8,128]{3,2,1,0:T(8,128)S(1)} collective-permute-done((f32[2,8,8,128]{3,2,1,0:T(8,128)S(1)}, f32[2,8,8,128]{3,2,1,0:T(8,128)S(1)}, u32[]{:S(2)}, u32[]{:S(2)}) %collective-permute-start.1) | collective-permute-done | bytes 65568 | tf_op jit(solution)/shard_map/ppermute | solution.py:372
  70.5 2.0 %collective-permute-start.2 = (f32[2,8,8,128]{3,2,1,0:T(8,128)S(1)}, f32[2,8,8,128]{3,2,1,0:T(8,128)S(1)}, u32[]{:S(2)}, u32[]{:S(2)}) collective-permute-start(f32[2,8,8,128]{3,2,1,0:T(8,128)S(1)} %add.17), channel_id=1, source_target_pairs={{0,32},{16,240},{32,64},{48,16},{64,96},{80,48},{96,128},{112,80},... | collective-permute-start | bytes 196616 | tf_op jit(solution)/shard_map/ppermute | solution.py:372
  72.5 6.2 %collective-permute-done.2 = f32[2,8,8,128]{3,2,1,0:T(8,128)S(1)} collective-permute-done((f32[2,8,8,128]{3,2,1,0:T(8,128)S(1)}, f32[2,8,8,128]{3,2,1,0:T(8,128)S(1)}, u32[]{:S(2)}, u32[]{:S(2)}) %collective-permute-start.2) | collective-permute-done | bytes 65568 | tf_op jit(solution)/shard_map/ppermute | solution.py:372
  78.7 0.1 collective-permute-start.3
  78.8 6.9 %collective-permute-done.3 = f32[2,8,8,128]{3,2,1,0:T(8,128)S(1)} collective-permute-done((f32[2,8,8,128]{3,2,1,0:T(8,128)S(1)}, f32[2,8,8,128]{3,2,1,0:T(8,128)S(1)}, u32[]{:S(2)}, u32[]{:S(2)}) %collective-permute-start.3) | collective-permute-done | bytes 65568 | tf_op jit(solution)/shard_map/ppermute | solution.py:372
  85.7 0.1 collective-permute-start.4
  85.8 0.0 all-to-all-done.2
  85.8 0.1 fusion
  85.9 0.1 copy.13
  86.1 1.0 %convert_element_type.11 = bf16[2,16,8192]{2,1,0:T(8,128)(2,1)} reshape(bf16[2,16,8,8,128]{4,3,2,1,0:T(8,128)(2,1)S(1)} %copy.13) | data formatting | bytes 1048576 | tf_op jit(solution)/shard_map/convert_element_type | solution.py:405
  87.1 2.4 %collective-permute-done.4 = f32[2,8,8,128]{3,2,1,0:T(8,128)S(1)} collective-permute-done((f32[2,8,8,128]{3,2,1,0:T(8,128)S(1)}, f32[2,8,8,128]{3,2,1,0:T(8,128)S(1)}, u32[]{:S(2)}, u32[]{:S(2)}) %collective-permute-start.4) | collective-permute-done | bytes 65568 | tf_op jit(solution)/shard_map/ppermute | solution.py:372
  89.5 0.7 copy.18
  (6 shorter events, 0.1 us)
Async XLA Ops:
  2.9 37.2 %copy-start.1 = (f32[8,2,128,128]{3,2,1,0:T(8,128)S(1)}, f32[8,2,128,128]{3,2,1,0:T(8,128)}, u32[]{:S(2)}) copy-start(f32[8,2,128,128]{3,2,1,0:T(8,128)} %constant.41.clone.over_l) | copy-start | bytes 3145732
  2.9 37.2 %copy-start.2 = (bf16[8,512,128]{2,1,0:T(8,128)(2,1)S(1)}, bf16[8,512,128]{2,1,0:T(8,128)(2,1)}, u32[]{:S(2)}) copy-start(bf16[8,512,128]{2,1,0:T(8,128)(2,1)} %constant.36.clone.forward_s) | copy-start | bytes 3145732
  3.0 37.2 %copy-start.3 = (f32[8,2,128,128]{3,2,1,0:T(8,128)S(1)}, f32[8,2,128,128]{3,2,1,0:T(8,128)}, u32[]{:S(2)}) copy-start(f32[8,2,128,128]{3,2,1,0:T(8,128)} %constant.40.clone.over_r) | copy-start | bytes 3145732
  3.0 37.2 %copy-start.4 = (bf16[2,256,256]{2,1,0:T(8,128)(2,1)S(1)}, bf16[2,256,256]{2,1,0:T(8,128)(2,1)}, u32[]{:S(2)}) copy-start(bf16[2,256,256]{2,1,0:T(8,128)(2,1)} %constant.39.clone.inverse_l) | copy-start | bytes 786436
  3.0 37.2 %copy-start.5 = (bf16[2,256,256]{2,1,0:T(8,128)(2,1)S(1)}, bf16[2,256,256]{2,1,0:T(8,128)(2,1)}, u32[]{:S(2)}) copy-start(bf16[2,256,256]{2,1,0:T(8,128)(2,1)} %constant.38.clone.forward_l) | copy-start | bytes 786436
  3.0 37.2 %copy-start.6 = (bf16[256,256]{1,0:T(8,128)(2,1)S(1)}, bf16[256,256]{1,0:T(8,128)(2,1)}, u32[]{:S(2)}) copy-start(bf16[256,256]{1,0:T(8,128)(2,1)} %constant.43.inverse_s) | copy-start | bytes 393220
  48.0 5.5 %copy-start = (f32[16,4,8,128]{3,2,1,0:T(8,128)}, f32[16,4,8,128]{3,2,1,0:T(8,128)S(1)}, u32[]{:S(2)}) copy-start(f32[16,4,8,128]{3,2,1,0:T(8,128)S(1)} %get-tuple-element.9.mine) | copy-start | bytes 786436
  48.0 5.5 %collective-permute-start = (f32[16,4,8,128]{3,2,1,0:T(8,128)S(1)}, f32[16,4,8,128]{3,2,1,0:T(8,128)S(1)}, u32[]{:S(2)}, u32[]{:S(2)}) collective-permute-start(f32[16,4,8,128]{3,2,1,0:T(8,128)S(1)} %get-tuple-element.9.mine), channel_id=1, source_target_pairs={{0,16},{16,0},{32,48},{48,32},{64,80},{80,64},{96,112},{112,96},{1... | collective-permute-start | bytes 786440 | tf_op jit(solution)/shard_map/ppermute | solution.py:398
  48.1 15.2 %all-to-all-start.1 = ((f32[16,8,8,128]{3,2,1,0:T(8,128)}), f32[16,8,8,128]{3,2,1,0:T(8,128)S(1)}, u32[]{:S(2)}, u32[]{:S(2)}) async-start(f32[16,8,8,128]{3,2,1,0:T(8,128)} %get-tuple-element.11), calls=%async_computation.1 | async-start | bytes 1048576 | tf_op jit(solution)/shard_map/all_to_all | solution.py:399
  53.5 0.7 copy-start.7
  63.4 22.4 %all-to-all-start.2 = ((f32[16,2,8,8,128]{4,3,2,1,0:T(8,128)}), f32[16,2,8,8,128]{4,3,2,1,0:T(8,128)S(1)}, u32[]{:S(2)}, u32[]{:S(2)}) async-start(f32[16,2,8,8,128]{4,3,2,1,0:T(8,128)} %input_rows.1), calls=%async_computation.2 | async-start | bytes 2097152 | tf_op jit(solution)/shard_map/all_to_all | solution.py:403
  69.2 1.3 %collective-permute-start.1 = (f32[2,8,8,128]{3,2,1,0:T(8,128)S(1)}, f32[2,8,8,128]{3,2,1,0:T(8,128)S(1)}, u32[]{:S(2)}, u32[]{:S(2)}) collective-permute-start(f32[2,8,8,128]{3,2,1,0:T(8,128)S(1)} %reduce_sum.9), channel_id=1, source_target_pairs={{0,16},{16,0},{32,48},{48,32},{64,80},{80,64},{96,112},{112,96},{1... | collective-permute-start | bytes 196616 | tf_op jit(solution)/shard_map/ppermute | solution.py:372
  70.5 8.2 %collective-permute-start.2 = (f32[2,8,8,128]{3,2,1,0:T(8,128)S(1)}, f32[2,8,8,128]{3,2,1,0:T(8,128)S(1)}, u32[]{:S(2)}, u32[]{:S(2)}) collective-permute-start(f32[2,8,8,128]{3,2,1,0:T(8,128)S(1)} %add.17), channel_id=1, source_target_pairs={{0,32},{16,240},{32,64},{48,16},{64,96},{80,48},{96,128},{112,80},... | collective-permute-start | bytes 196616 | tf_op jit(solution)/shard_map/ppermute | solution.py:372
  78.7 7.0 %collective-permute-start.3 = (f32[2,8,8,128]{3,2,1,0:T(8,128)S(1)}, f32[2,8,8,128]{3,2,1,0:T(8,128)S(1)}, u32[]{:S(2)}, u32[]{:S(2)}) collective-permute-start(f32[2,8,8,128]{3,2,1,0:T(8,128)S(1)} %add.18), channel_id=1, source_target_pairs={{0,64},{16,208},{32,96},{48,240},{64,128},{80,16},{96,160},{112,48... | collective-permute-start | bytes 196616 | tf_op jit(solution)/shard_map/ppermute | solution.py:372
  85.7 3.8 %collective-permute-start.4 = (f32[2,8,8,128]{3,2,1,0:T(8,128)S(1)}, f32[2,8,8,128]{3,2,1,0:T(8,128)S(1)}, u32[]{:S(2)}, u32[]{:S(2)}) collective-permute-start(f32[2,8,8,128]{3,2,1,0:T(8,128)S(1)} %add.19), channel_id=1, source_target_pairs={{0,48},{16,224},{32,80},{48,0},{64,112},{80,32},{96,144},{112,64},... | collective-permute-start | bytes 196616 | tf_op jit(solution)/shard_map/ppermute | solution.py:372

commit v6 on v5

--- a/solution.py
+++ b/solution.py
@@ -106,9 +106,9 @@
     return values[:, :LANES], values[:, LANES:]
 
 
-def over_s_forward(blocks_of, count, forward_s, z):
-    for r in range(RADIX):
-        samples = [blocks_of(row, r).reshape(SIDE, LANES) for row in range(count)]
+def over_s_forward(blocks_of, rows, radices, forward_s, z):
+    for r in radices:
+        samples = [blocks_of(row, r).reshape(SIDE, LANES) for row in rows]
         high, low = split(jnp.concatenate(samples, axis=1))
         first = forward_s[r, : 2 * SIDE]
         second = forward_s[r, 2 * SIDE :]
@@ -121,7 +121,8 @@
         )
         both = dot(table, jnp.concatenate([high, low], axis=0))
         out = both[: 2 * SIDE] + both[2 * SIDE :]
-        z[r] = out.reshape(2, SIDE, count * LANES)
+        lanes = pl.ds(rows[0] * LANES, len(rows) * LANES)
+        z[r, :, :, lanes] = out.reshape(2, SIDE, len(rows) * LANES)
 
 
 def over_r_forward(z, row, span, over_l):
@@ -149,22 +150,32 @@
 
 def filter_kernel(
     rows, forward_s, inverse_s, forward_l, inverse_l, over_r, over_l,
-    terms, grads, half, z, back, held, sems,
+    terms, grads, half, z, back, held, inputs, sems,
 ):
     half[...] = rows[:, 4 * RADIX :]
-    over_s_forward(lambda row, r: rows[:, row * RADIX + r], 4, forward_s, z)
+    def samples(row, r):
+        return rows[:, row * RADIX + r]
+
+    def spectra_of(first_row, span):
+        blocks = over_r_forward(z, first_row, span, over_l)
+        blocks += over_r_forward(z, first_row + 1, span, over_l)
+        return dot_from_right(jnp.concatenate(blocks, axis=0), forward_l)
+
+    over_s_forward(samples, range(2), range(RADIX), forward_s, z)
     size = RADIX * STEP
+    steps = SIDE // STEP
+    each = RADIX // steps
+    for step in range(steps):
+        over_s_forward(samples, range(2, 4), range(step * each, (step + 1) * each), forward_s, z)
+        inputs[step] = spectra_of(0, pl.ds(step * STEP, STEP))
     copies = []
-    for step in range(SIDE // STEP):
+    for step in range(steps):
         span = pl.ds(step * STEP, STEP)
-        blocks = []
-        for row in range(4):
-            blocks += over_r_forward(z, row, span, over_l)
-        spectra = dot_from_right(jnp.concatenate(blocks, axis=0), forward_l)
-        held[step] = spectra[2 * size :]
+        spectra = spectra_of(2, span)
+        held[step] = spectra
         copies.append(pltpu.make_async_copy(held.at[step], grads.at[step], sems.at[step]))
-        first = times_conjugate(parts(spectra[2 * size : 3 * size]), parts(spectra[:size]))
-        second = times_conjugate(parts(spectra[3 * size :]), parts(spectra[size : 2 * size]))
+        first = times_conjugate(parts(spectra[:size]), parts(inputs[step, :size]))
+        second = times_conjugate(parts(spectra[size:]), parts(inputs[step, size:]))
         product = jnp.concatenate([first[0] + second[0], first[1] + second[1]], axis=1)
         values = dot_from_right(product, inverse_l)
         for r, value in enumerate(over_r_inverse(values, span, over_l)):
@@ -205,7 +216,7 @@
         return jnp.where(near, own, far) if r < per_half else jnp.where(near, far, own)
 
     load_forward.wait()
-    over_s_forward(filter_block, 1, forward_in, z)
+    over_s_forward(filter_block, range(1), range(RADIX), forward_in, z)
     load_turns.wait()
     load_grads.wait()
     for step in range(SIDE // STEP):
@@ -318,6 +329,7 @@
             pltpu.VMEM((RADIX, 2, SIDE, 4 * LANES), jnp.float32),
             pltpu.VMEM((2, 2, SIDE, RADIX * LANES), jnp.bfloat16),
             pltpu.VMEM(grads, jnp.float32),
+            pltpu.VMEM(grads, jnp.float32),
             pltpu.SemaphoreType.DMA((steps,)),
         ],
         compiler_params=pltpu.CompilerParams(vmem_limit_bytes=20 << 20),

time: 90.6 us -> 89.7 us (0.990)
    pallas_call x1, Pallas kernels: 7.87 us -> 6.91 us  [filter_terms(): pl.pallas_call(filter_kernel, out_shape=(jax.ShapeDtypeStruct((blocks, RA...]
where the time goes in v6:
time: 89.7 us; the launch traced here: 89.3 us
  blocking collectives  37.1 us (41%)
  waiting for transfers between devices  18.6 us (21%)
  Pallas kernels  16.5 us (18%)
  starting transfers between devices  13.5 us (15%)
  local copies, waits for them, and re-layouts  2.54 us (3%)
    all_to_all x1, blocking collectives, local(): rows = lax.all_to_all(packed, 'ctx', 0, 0, tiled=True)  37.1 us
    ppermute x4, waiting for transfers between devices, moved(): return lax.ppermute(array, 'chan', ring)  16.8 us
    pallas_call x1, Pallas kernels, input_rows(): pl.pallas_call(input_kernel, out_shape=jax.ShapeDtypeStruct(out, jnp.floa...  7.3 us
    pallas_call x1, Pallas kernels, filter_terms(): pl.pallas_call(filter_kernel, out_shape=(jax.ShapeDtypeStruct((blocks, RA...  6.91 us
    all_to_all x1, starting transfers between devices, local(): inputs = lax.all_to_all(inputs, 'ctx', 0, 0, tiled=True)  5.84 us
    all_to_all x1, starting transfers between devices, local(): terms = lax.all_to_all(terms, 'ctx', 0, 0, tiled=True)  5.36 us
    pallas_call x1, Pallas kernels, laid_out(): pl.pallas_call(layout_kernel, out_shape=jax.ShapeDtypeStruct((channels, t...  2.28 us
    ppermute x4, starting transfers between devices, moved(): return lax.ppermute(array, 'chan', ring)  2.18 us
  transfers between devices with their start and end apart: 7, of which 5 were waited for; matrix products, arithmetic and copies ran while one was open for 1% of the time, Pallas kernels for 8%

profile of v6, /device:TPU:2, one launch (start us, length us, event | category | flops | bytes accessed | tf_op | source)
XLA Modules:
  0.0 89.3 jit_solution(15296610543171263198)
XLA Ops:
  0.6 2.3 %laid_out.1 = f32[16,36,8,128]{3,2,1,0:T(8,128)S(1)} custom-call(s32[1]{0:T(128)} %bitcast.core, f32[2,16,8192]{2,1,0:T(8,128)} %saved_input.1, f32[2,16,8192]{2,1,0:T(8,128)} %out_grad.1, f32[2,8192]{1,0:T(2,128)} %filters.1), custom_call_target="tpu_custom_call" | custom-call | tf_op jit(solution)/shard_map/laid_out/pallas_call | solution.py:299
  2.9 0.0 copy-start.1
  2.9 0.0 copy-start.2
  3.0 0.0 copy-start.3
  3.0 0.0 copy-start.4
  3.0 0.0 copy-start.5
  3.0 0.0 copy-start.6
  3.0 37.1 %all_to_all.15.rows = f32[16,36,8,128]{3,2,1,0:T(8,128)S(1)} all-to-all(f32[16,36,8,128]{3,2,1,0:T(8,128)S(1)} %laid_out.1), channel_id=1, replica_groups=mesh['chan'=16,'ctx'=16] {'ctx'}, dimensions={0} | all-to-all | bytes 4718592 | tf_op jit(solution)/shard_map/all_to_all | solution.py:408
  40.1 0.0 copy-done.1
  40.1 0.0 copy-done.2
  40.1 0.0 copy-done.3
  40.1 0.0 copy-done.4
  40.1 0.0 copy-done.5
  40.1 0.0 copy-done.6
  40.1 6.9 %filter_terms.1 = (f32[16,8,8,128]{3,2,1,0:T(8,128)}, f32[4,512,256]{2,1,0:T(8,128)}, f32[16,4,8,128]{3,2,1,0:T(8,128)S(1)}) custom-call(f32[16,36,8,128]{3,2,1,0:T(8,128)S(1)} %all_to_all.15.rows, bf16[8,512,128]{2,1,0:T(8,128)(2,1)S(1)} %copy-done.2, bf16[256,256]{1,0:T(8,128)(2,1)S(1)} %copy-done.6, bf16[2,256,256]{2,1,0:T(8,128)(2,1)S(1)} %copy-done.5, ...), custom_call_target="tpu_custom_call" | custom-call | flops 4000000000 | bytes 10000000 | tf_op jit(solution)/shard_map/filter_terms/pallas_call | solution.py:319
  47.1 0.0 copy-start
  47.1 0.1 collective-permute-start
  47.2 5.4 %all-to-all-start.1 = ((f32[16,8,8,128]{3,2,1,0:T(8,128)}), f32[16,8,8,128]{3,2,1,0:T(8,128)S(1)}, u32[]{:S(2)}, u32[]{:S(2)}) async-start(f32[16,8,8,128]{3,2,1,0:T(8,128)} %get-tuple-element.11), calls=%async_computation.1 | async-start | bytes 1048576 | tf_op jit(solution)/shard_map/all_to_all | solution.py:411
  52.5 0.0 collective-permute-done.other
  52.5 0.0 copy-start.7
  52.5 0.0 copy-done
  52.6 0.7 copy-done.7
  53.2 7.3 %input_rows.1 = f32[16,2,8,8,128]{4,3,2,1,0:T(8,128)} custom-call(s32[1]{0:T(128)} %bitcast.core, f32[16,4,8,128]{3,2,1,0:T(8,128)} %copy-done, f32[16,4,8,128]{3,2,1,0:T(8,128)} %copy-done.7, f32[4,512,256]{2,1,0:T(8,128)} %get-tuple-element.10.grads, bf16[8,512,128]{2,1,0:T(8,128)(2,1)} %constant.36.clone.forward_s, ...), custom_call_target="tpu_custom_call" | custom-call | flops 2500000000 | bytes 10000000 | tf_op jit(solution)/shard_map/input_rows/pallas_call | solution.py:347
  60.5 1.9 %all-to-all-done.1 = f32[16,8,8,128]{3,2,1,0:T(8,128)S(1)} async-done(((f32[16,8,8,128]{3,2,1,0:T(8,128)}), f32[16,8,8,128]{3,2,1,0:T(8,128)S(1)}, u32[]{:S(2)}, u32[]{:S(2)}) %all-to-all-start.1) | async-done | bytes 524320 | tf_op jit(solution)/shard_map/all_to_all | solution.py:411
  62.4 5.8 %all-to-all-start.2 = ((f32[16,2,8,8,128]{4,3,2,1,0:T(8,128)}), f32[16,2,8,8,128]{4,3,2,1,0:T(8,128)S(1)}, u32[]{:S(2)}, u32[]{:S(2)}) async-start(f32[16,2,8,8,128]{4,3,2,1,0:T(8,128)} %input_rows.1), calls=%async_computation.2 | async-start | bytes 2097152 | tf_op jit(solution)/shard_map/all_to_all | solution.py:415
  68.3 0.0 collective-permute-start.1
  68.3 1.2 %collective-permute-done.1 = f32[2,8,8,128]{3,2,1,0:T(8,128)S(1)} collective-permute-done((f32[2,8,8,128]{3,2,1,0:T(8,128)S(1)}, f32[2,8,8,128]{3,2,1,0:T(8,128)S(1)}, u32[]{:S(2)}, u32[]{:S(2)}) %collective-permute-start.1) | collective-permute-done | bytes 65568 | tf_op jit(solution)/shard_map/ppermute | solution.py:384
  69.5 2.0 %collective-permute-start.2 = (f32[2,8,8,128]{3,2,1,0:T(8,128)S(1)}, f32[2,8,8,128]{3,2,1,0:T(8,128)S(1)}, u32[]{:S(2)}, u32[]{:S(2)}) collective-permute-start(f32[2,8,8,128]{3,2,1,0:T(8,128)S(1)} %add.17), channel_id=1, source_target_pairs={{0,32},{16,240},{32,64},{48,16},{64,96},{80,48},{96,128},{112,80},... | collective-permute-start | bytes 196616 | tf_op jit(solution)/shard_map/ppermute | solution.py:384
  71.5 6.2 %collective-permute-done.2 = f32[2,8,8,128]{3,2,1,0:T(8,128)S(1)} collective-permute-done((f32[2,8,8,128]{3,2,1,0:T(8,128)S(1)}, f32[2,8,8,128]{3,2,1,0:T(8,128)S(1)}, u32[]{:S(2)}, u32[]{:S(2)}) %collective-permute-start.2) | collective-permute-done | bytes 65568 | tf_op jit(solution)/shard_map/ppermute | solution.py:384
  77.7 0.1 collective-permute-start.3
  77.8 6.9 %collective-permute-done.3 = f32[2,8,8,128]{3,2,1,0:T(8,128)S(1)} collective-permute-done((f32[2,8,8,128]{3,2,1,0:T(8,128)S(1)}, f32[2,8,8,128]{3,2,1,0:T(8,128)S(1)}, u32[]{:S(2)}, u32[]{:S(2)}) %collective-permute-start.3) | collective-permute-done | bytes 65568 | tf_op jit(solution)/shard_map/ppermute | solution.py:384
  84.8 0.1 collective-permute-start.4
  84.9 0.0 all-to-all-done.2
  84.9 0.1 fusion
  85.0 0.1 copy.13
  85.1 1.0 %convert_element_type.11 = bf16[2,16,8192]{2,1,0:T(8,128)(2,1)} reshape(bf16[2,16,8,8,128]{4,3,2,1,0:T(8,128)(2,1)S(1)} %copy.13) | data formatting | bytes 1048576 | tf_op jit(solution)/shard_map/convert_element_type | solution.py:417
  86.1 2.4 %collective-permute-done.4 = f32[2,8,8,128]{3,2,1,0:T(8,128)S(1)} collective-permute-done((f32[2,8,8,128]{3,2,1,0:T(8,128)S(1)}, f32[2,8,8,128]{3,2,1,0:T(8,128)S(1)}, u32[]{:S(2)}, u32[]{:S(2)}) %collective-permute-start.4) | collective-permute-done | bytes 65568 | tf_op jit(solution)/shard_map/ppermute | solution.py:384
  88.6 0.7 copy.18
  (6 shorter events, 0.1 us)
Async XLA Ops:
  2.9 37.2 %copy-start.1 = (f32[8,2,128,128]{3,2,1,0:T(8,128)S(1)}, f32[8,2,128,128]{3,2,1,0:T(8,128)}, u32[]{:S(2)}) copy-start(f32[8,2,128,128]{3,2,1,0:T(8,128)} %constant.41.clone.over_l) | copy-start | bytes 3145732
  2.9 37.2 %copy-start.2 = (bf16[8,512,128]{2,1,0:T(8,128)(2,1)S(1)}, bf16[8,512,128]{2,1,0:T(8,128)(2,1)}, u32[]{:S(2)}) copy-start(bf16[8,512,128]{2,1,0:T(8,128)(2,1)} %constant.36.clone.forward_s) | copy-start | bytes 3145732
  3.0 37.2 %copy-start.3 = (f32[8,2,128,128]{3,2,1,0:T(8,128)S(1)}, f32[8,2,128,128]{3,2,1,0:T(8,128)}, u32[]{:S(2)}) copy-start(f32[8,2,128,128]{3,2,1,0:T(8,128)} %constant.40.clone.over_r) | copy-start | bytes 3145732
  3.0 37.2 %copy-start.4 = (bf16[2,256,256]{2,1,0:T(8,128)(2,1)S(1)}, bf16[2,256,256]{2,1,0:T(8,128)(2,1)}, u32[]{:S(2)}) copy-start(bf16[2,256,256]{2,1,0:T(8,128)(2,1)} %constant.39.clone.inverse_l) | copy-start | bytes 786436
  3.0 37.2 %copy-start.5 = (bf16[2,256,256]{2,1,0:T(8,128)(2,1)S(1)}, bf16[2,256,256]{2,1,0:T(8,128)(2,1)}, u32[]{:S(2)}) copy-start(bf16[2,256,256]{2,1,0:T(8,128)(2,1)} %constant.38.clone.forward_l) | copy-start | bytes 786436
  3.0 37.2 %copy-start.6 = (bf16[256,256]{1,0:T(8,128)(2,1)S(1)}, bf16[256,256]{1,0:T(8,128)(2,1)}, u32[]{:S(2)}) copy-start(bf16[256,256]{1,0:T(8,128)(2,1)} %constant.43.inverse_s) | copy-start | bytes 393220
  47.1 5.5 %copy-start = (f32[16,4,8,128]{3,2,1,0:T(8,128)}, f32[16,4,8,128]{3,2,1,0:T(8,128)S(1)}, u32[]{:S(2)}) copy-start(f32[16,4,8,128]{3,2,1,0:T(8,128)S(1)} %get-tuple-element.9.mine) | copy-start | bytes 786436
  47.1 5.5 %collective-permute-start = (f32[16,4,8,128]{3,2,1,0:T(8,128)S(1)}, f32[16,4,8,128]{3,2,1,0:T(8,128)S(1)}, u32[]{:S(2)}, u32[]{:S(2)}) collective-permute-start(f32[16,4,8,128]{3,2,1,0:T(8,128)S(1)} %get-tuple-element.9.mine), channel_id=1, source_target_pairs={{0,16},{16,0},{32,48},{48,32},{64,80},{80,64},{96,112},{112,96},{1... | collective-permute-start | bytes 786440 | tf_op jit(solution)/shard_map/ppermute | solution.py:410
  47.2 15.2 %all-to-all-start.1 = ((f32[16,8,8,128]{3,2,1,0:T(8,128)}), f32[16,8,8,128]{3,2,1,0:T(8,128)S(1)}, u32[]{:S(2)}, u32[]{:S(2)}) async-start(f32[16,8,8,128]{3,2,1,0:T(8,128)} %get-tuple-element.11), calls=%async_computation.1 | async-start | bytes 1048576 | tf_op jit(solution)/shard_map/all_to_all | solution.py:411
  52.5 0.7 copy-start.7
  62.4 22.4 %all-to-all-start.2 = ((f32[16,2,8,8,128]{4,3,2,1,0:T(8,128)}), f32[16,2,8,8,128]{4,3,2,1,0:T(8,128)S(1)}, u32[]{:S(2)}, u32[]{:S(2)}) async-start(f32[16,2,8,8,128]{4,3,2,1,0:T(8,128)} %input_rows.1), calls=%async_computation.2 | async-start | bytes 2097152 | tf_op jit(solution)/shard_map/all_to_all | solution.py:415
  68.3 1.3 %collective-permute-start.1 = (f32[2,8,8,128]{3,2,1,0:T(8,128)S(1)}, f32[2,8,8,128]{3,2,1,0:T(8,128)S(1)}, u32[]{:S(2)}, u32[]{:S(2)}) collective-permute-start(f32[2,8,8,128]{3,2,1,0:T(8,128)S(1)} %reduce_sum.9), channel_id=1, source_target_pairs={{0,16},{16,0},{32,48},{48,32},{64,80},{80,64},{96,112},{112,96},{1... | collective-permute-start | bytes 196616 | tf_op jit(solution)/shard_map/ppermute | solution.py:384
  69.5 8.2 %collective-permute-start.2 = (f32[2,8,8,128]{3,2,1,0:T(8,128)S(1)}, f32[2,8,8,128]{3,2,1,0:T(8,128)S(1)}, u32[]{:S(2)}, u32[]{:S(2)}) collective-permute-start(f32[2,8,8,128]{3,2,1,0:T(8,128)S(1)} %add.17), channel_id=1, source_target_pairs={{0,32},{16,240},{32,64},{48,16},{64,96},{80,48},{96,128},{112,80},... | collective-permute-start | bytes 196616 | tf_op jit(solution)/shard_map/ppermute | solution.py:384
  77.7 7.0 %collective-permute-start.3 = (f32[2,8,8,128]{3,2,1,0:T(8,128)S(1)}, f32[2,8,8,128]{3,2,1,0:T(8,128)S(1)}, u32[]{:S(2)}, u32[]{:S(2)}) collective-permute-start(f32[2,8,8,128]{3,2,1,0:T(8,128)S(1)} %add.18), channel_id=1, source_target_pairs={{0,64},{16,208},{32,96},{48,240},{64,128},{80,16},{96,160},{112,48... | collective-permute-start | bytes 196616 | tf_op jit(solution)/shard_map/ppermute | solution.py:384
  84.8 3.8 %collective-permute-start.4 = (f32[2,8,8,128]{3,2,1,0:T(8,128)S(1)}, f32[2,8,8,128]{3,2,1,0:T(8,128)S(1)}, u32[]{:S(2)}, u32[]{:S(2)}) collective-permute-start(f32[2,8,8,128]{3,2,1,0:T(8,128)S(1)} %add.19), channel_id=1, source_target_pairs={{0,48},{16,224},{32,80},{48,0},{64,112},{80,32},{96,144},{112,64},... | collective-permute-start | bytes 196616 | tf_op jit(solution)/shard_map/ppermute | solution.py:384

commit v7 on v6

--- a/solution.py
+++ b/solution.py
@@ -169,9 +169,12 @@
         over_s_forward(samples, range(2, 4), range(step * each, (step + 1) * each), forward_s, z)
         inputs[step] = spectra_of(0, pl.ds(step * STEP, STEP))
     copies = []
+    following = spectra_of(2, pl.ds(0, STEP))
     for step in range(steps):
         span = pl.ds(step * STEP, STEP)
-        spectra = spectra_of(2, span)
+        spectra = following
+        if step + 1 < steps:
+            following = spectra_of(2, pl.ds((step + 1) * STEP, STEP))
         held[step] = spectra
         copies.append(pltpu.make_async_copy(held.at[step], grads.at[step], sems.at[step]))
         first = times_conjugate(parts(spectra[:size]), parts(inputs[step, :size]))

time: 89.7 us -> 88.9 us (level)
  no operation moved by 1% of the time
where the time goes in v7:
time: 88.9 us; the launch traced here: 88.5 us
  blocking collectives  37.1 us (42%)
  waiting for transfers between devices  18.6 us (21%)
  Pallas kernels  15.7 us (18%)
  starting transfers between devices  13.5 us (15%)
  local copies, waits for them, and re-layouts  2.54 us (3%)
    all_to_all x1, blocking collectives, local(): rows = lax.all_to_all(packed, 'ctx', 0, 0, tiled=True)  37.1 us
    ppermute x4, waiting for transfers between devices, moved(): return lax.ppermute(array, 'chan', ring)  16.8 us
    pallas_call x1, Pallas kernels, input_rows(): pl.pallas_call(input_kernel, out_shape=jax.ShapeDtypeStruct(out, jnp.floa...  7.3 us
    pallas_call x1, Pallas kernels, filter_terms(): pl.pallas_call(filter_kernel, out_shape=(jax.ShapeDtypeStruct((blocks, RA...  6.16 us
    all_to_all x1, starting transfers between devices, local(): inputs = lax.all_to_all(inputs, 'ctx', 0, 0, tiled=True)  5.84 us
    all_to_all x1, starting transfers between devices, local(): terms = lax.all_to_all(terms, 'ctx', 0, 0, tiled=True)  5.36 us
    pallas_call x1, Pallas kernels, laid_out(): pl.pallas_call(layout_kernel, out_shape=jax.ShapeDtypeStruct((channels, t...  2.28 us
    ppermute x4, starting transfers between devices, moved(): return lax.ppermute(array, 'chan', ring)  2.18 us
  transfers between devices with their start and end apart: 7, of which 5 were waited for; matrix products, arithmetic and copies ran while one was open for 1% of the time, Pallas kernels for 8%

profile of v7, /device:TPU:2, one launch (start us, length us, event | category | flops | bytes accessed | tf_op | source)
XLA Modules:
  0.0 88.5 jit_solution(3870370354338812341)
XLA Ops:
  0.6 2.3 %laid_out.1 = f32[16,36,8,128]{3,2,1,0:T(8,128)S(1)} custom-call(s32[1]{0:T(128)} %bitcast.core, f32[2,16,8192]{2,1,0:T(8,128)} %saved_input.1, f32[2,16,8192]{2,1,0:T(8,128)} %out_grad.1, f32[2,8192]{1,0:T(2,128)} %filters.1), custom_call_target="tpu_custom_call" | custom-call | tf_op jit(solution)/shard_map/laid_out/pallas_call | solution.py:302
  2.9 0.0 copy-start.1
  2.9 0.0 copy-start.2
  3.0 0.0 copy-start.3
  3.0 0.0 copy-start.4
  3.0 0.0 copy-start.5
  3.0 0.0 copy-start.6
  3.0 37.1 %all_to_all.15.rows = f32[16,36,8,128]{3,2,1,0:T(8,128)S(1)} all-to-all(f32[16,36,8,128]{3,2,1,0:T(8,128)S(1)} %laid_out.1), channel_id=1, replica_groups=mesh['chan'=16,'ctx'=16] {'ctx'}, dimensions={0} | all-to-all | bytes 4718592 | tf_op jit(solution)/shard_map/all_to_all | solution.py:411
  40.1 0.0 copy-done.1
  40.1 0.0 copy-done.2
  40.1 0.0 copy-done.3
  40.1 0.0 copy-done.4
  40.1 0.0 copy-done.5
  40.1 0.0 copy-done.6
  40.1 6.2 %filter_terms.1 = (f32[16,8,8,128]{3,2,1,0:T(8,128)}, f32[4,512,256]{2,1,0:T(8,128)}, f32[16,4,8,128]{3,2,1,0:T(8,128)S(1)}) custom-call(f32[16,36,8,128]{3,2,1,0:T(8,128)S(1)} %all_to_all.15.rows, bf16[8,512,128]{2,1,0:T(8,128)(2,1)S(1)} %copy-done.2, bf16[256,256]{1,0:T(8,128)(2,1)S(1)} %copy-done.6, bf16[2,256,256]{2,1,0:T(8,128)(2,1)S(1)} %copy-done.5, ...), custom_call_target="tpu_custom_call" | custom-call | flops 4000000000 | bytes 10000000 | tf_op jit(solution)/shard_map/filter_terms/pallas_call | solution.py:322
  46.3 0.0 copy-start
  46.3 0.1 collective-permute-start
  46.4 5.4 %all-to-all-start.1 = ((f32[16,8,8,128]{3,2,1,0:T(8,128)}), f32[16,8,8,128]{3,2,1,0:T(8,128)S(1)}, u32[]{:S(2)}, u32[]{:S(2)}) async-start(f32[16,8,8,128]{3,2,1,0:T(8,128)} %get-tuple-element.11), calls=%async_computation.1 | async-start | bytes 1048576 | tf_op jit(solution)/shard_map/all_to_all | solution.py:414
  51.8 0.0 collective-permute-done.other
  51.8 0.0 copy-start.7
  51.8 0.0 copy-done
  51.8 0.7 copy-done.7
  52.5 7.3 %input_rows.1 = f32[16,2,8,8,128]{4,3,2,1,0:T(8,128)} custom-call(s32[1]{0:T(128)} %bitcast.core, f32[16,4,8,128]{3,2,1,0:T(8,128)} %copy-done, f32[16,4,8,128]{3,2,1,0:T(8,128)} %copy-done.7, f32[4,512,256]{2,1,0:T(8,128)} %get-tuple-element.10.grads, bf16[8,512,128]{2,1,0:T(8,128)(2,1)} %constant.36.clone.forward_s, ...), custom_call_target="tpu_custom_call" | custom-call | flops 2500000000 | bytes 10000000 | tf_op jit(solution)/shard_map/input_rows/pallas_call | solution.py:350
  59.8 1.9 %all-to-all-done.1 = f32[16,8,8,128]{3,2,1,0:T(8,128)S(1)} async-done(((f32[16,8,8,128]{3,2,1,0:T(8,128)}), f32[16,8,8,128]{3,2,1,0:T(8,128)S(1)}, u32[]{:S(2)}, u32[]{:S(2)}) %all-to-all-start.1) | async-done | bytes 524320 | tf_op jit(solution)/shard_map/all_to_all | solution.py:414
  61.7 5.8 %all-to-all-start.2 = ((f32[16,2,8,8,128]{4,3,2,1,0:T(8,128)}), f32[16,2,8,8,128]{4,3,2,1,0:T(8,128)S(1)}, u32[]{:S(2)}, u32[]{:S(2)}) async-start(f32[16,2,8,8,128]{4,3,2,1,0:T(8,128)} %input_rows.1), calls=%async_computation.2 | async-start | bytes 2097152 | tf_op jit(solution)/shard_map/all_to_all | solution.py:418
  67.5 0.0 collective-permute-start.1
  67.5 1.2 %collective-permute-done.1 = f32[2,8,8,128]{3,2,1,0:T(8,128)S(1)} collective-permute-done((f32[2,8,8,128]{3,2,1,0:T(8,128)S(1)}, f32[2,8,8,128]{3,2,1,0:T(8,128)S(1)}, u32[]{:S(2)}, u32[]{:S(2)}) %collective-permute-start.1) | collective-permute-done | bytes 65568 | tf_op jit(solution)/shard_map/ppermute | solution.py:387
  68.8 2.0 %collective-permute-start.2 = (f32[2,8,8,128]{3,2,1,0:T(8,128)S(1)}, f32[2,8,8,128]{3,2,1,0:T(8,128)S(1)}, u32[]{:S(2)}, u32[]{:S(2)}) collective-permute-start(f32[2,8,8,128]{3,2,1,0:T(8,128)S(1)} %add.17), channel_id=1, source_target_pairs={{0,32},{16,240},{32,64},{48,16},{64,96},{80,48},{96,128},{112,80},... | collective-permute-start | bytes 196616 | tf_op jit(solution)/shard_map/ppermute | solution.py:387
  70.8 6.2 %collective-permute-done.2 = f32[2,8,8,128]{3,2,1,0:T(8,128)S(1)} collective-permute-done((f32[2,8,8,128]{3,2,1,0:T(8,128)S(1)}, f32[2,8,8,128]{3,2,1,0:T(8,128)S(1)}, u32[]{:S(2)}, u32[]{:S(2)}) %collective-permute-start.2) | collective-permute-done | bytes 65568 | tf_op jit(solution)/shard_map/ppermute | solution.py:387
  77.0 0.1 collective-permute-start.3
  77.1 6.9 %collective-permute-done.3 = f32[2,8,8,128]{3,2,1,0:T(8,128)S(1)} collective-permute-done((f32[2,8,8,128]{3,2,1,0:T(8,128)S(1)}, f32[2,8,8,128]{3,2,1,0:T(8,128)S(1)}, u32[]{:S(2)}, u32[]{:S(2)}) %collective-permute-start.3) | collective-permute-done | bytes 65568 | tf_op jit(solution)/shard_map/ppermute | solution.py:387
  84.0 0.1 collective-permute-start.4
  84.1 0.0 all-to-all-done.2
  84.1 0.1 fusion
  84.2 0.1 copy.13
  84.3 1.0 %convert_element_type.11 = bf16[2,16,8192]{2,1,0:T(8,128)(2,1)} reshape(bf16[2,16,8,8,128]{4,3,2,1,0:T(8,128)(2,1)S(1)} %copy.13) | data formatting | bytes 1048576 | tf_op jit(solution)/shard_map/convert_element_type | solution.py:420
  85.4 2.4 %collective-permute-done.4 = f32[2,8,8,128]{3,2,1,0:T(8,128)S(1)} collective-permute-done((f32[2,8,8,128]{3,2,1,0:T(8,128)S(1)}, f32[2,8,8,128]{3,2,1,0:T(8,128)S(1)}, u32[]{:S(2)}, u32[]{:S(2)}) %collective-permute-start.4) | collective-permute-done | bytes 65568 | tf_op jit(solution)/shard_map/ppermute | solution.py:387
  87.8 0.7 copy.18
  (6 shorter events, 0.1 us)
Async XLA Ops:
  2.9 37.2 %copy-start.1 = (f32[8,2,128,128]{3,2,1,0:T(8,128)S(1)}, f32[8,2,128,128]{3,2,1,0:T(8,128)}, u32[]{:S(2)}) copy-start(f32[8,2,128,128]{3,2,1,0:T(8,128)} %constant.41.clone.over_l) | copy-start | bytes 3145732
  2.9 37.2 %copy-start.2 = (bf16[8,512,128]{2,1,0:T(8,128)(2,1)S(1)}, bf16[8,512,128]{2,1,0:T(8,128)(2,1)}, u32[]{:S(2)}) copy-start(bf16[8,512,128]{2,1,0:T(8,128)(2,1)} %constant.36.clone.forward_s) | copy-start | bytes 3145732
  3.0 37.2 %copy-start.3 = (f32[8,2,128,128]{3,2,1,0:T(8,128)S(1)}, f32[8,2,128,128]{3,2,1,0:T(8,128)}, u32[]{:S(2)}) copy-start(f32[8,2,128,128]{3,2,1,0:T(8,128)} %constant.40.clone.over_r) | copy-start | bytes 3145732
  3.0 37.2 %copy-start.4 = (bf16[2,256,256]{2,1,0:T(8,128)(2,1)S(1)}, bf16[2,256,256]{2,1,0:T(8,128)(2,1)}, u32[]{:S(2)}) copy-start(bf16[2,256,256]{2,1,0:T(8,128)(2,1)} %constant.39.clone.inverse_l) | copy-start | bytes 786436
  3.0 37.2 %copy-start.5 = (bf16[2,256,256]{2,1,0:T(8,128)(2,1)S(1)}, bf16[2,256,256]{2,1,0:T(8,128)(2,1)}, u32[]{:S(2)}) copy-start(bf16[2,256,256]{2,1,0:T(8,128)(2,1)} %constant.38.clone.forward_l) | copy-start | bytes 786436
  3.0 37.2 %copy-start.6 = (bf16[256,256]{1,0:T(8,128)(2,1)S(1)}, bf16[256,256]{1,0:T(8,128)(2,1)}, u32[]{:S(2)}) copy-start(bf16[256,256]{1,0:T(8,128)(2,1)} %constant.43.inverse_s) | copy-start | bytes 393220
  46.3 5.5 %copy-start = (f32[16,4,8,128]{3,2,1,0:T(8,128)}, f32[16,4,8,128]{3,2,1,0:T(8,128)S(1)}, u32[]{:S(2)}) copy-start(f32[16,4,8,128]{3,2,1,0:T(8,128)S(1)} %get-tuple-element.9.mine) | copy-start | bytes 786436
  46.3 5.5 %collective-permute-start = (f32[16,4,8,128]{3,2,1,0:T(8,128)S(1)}, f32[16,4,8,128]{3,2,1,0:T(8,128)S(1)}, u32[]{:S(2)}, u32[]{:S(2)}) collective-permute-start(f32[16,4,8,128]{3,2,1,0:T(8,128)S(1)} %get-tuple-element.9.mine), channel_id=1, source_target_pairs={{0,16},{16,0},{32,48},{48,32},{64,80},{80,64},{96,112},{112,96},{1... | collective-permute-start | bytes 786440 | tf_op jit(solution)/shard_map/ppermute | solution.py:413
  46.4 15.2 %all-to-all-start.1 = ((f32[16,8,8,128]{3,2,1,0:T(8,128)}), f32[16,8,8,128]{3,2,1,0:T(8,128)S(1)}, u32[]{:S(2)}, u32[]{:S(2)}) async-start(f32[16,8,8,128]{3,2,1,0:T(8,128)} %get-tuple-element.11), calls=%async_computation.1 | async-start | bytes 1048576 | tf_op jit(solution)/shard_map/all_to_all | solution.py:414
  51.8 0.7 copy-start.7
  61.7 22.4 %all-to-all-start.2 = ((f32[16,2,8,8,128]{4,3,2,1,0:T(8,128)}), f32[16,2,8,8,128]{4,3,2,1,0:T(8,128)S(1)}, u32[]{:S(2)}, u32[]{:S(2)}) async-start(f32[16,2,8,8,128]{4,3,2,1,0:T(8,128)} %input_rows.1), calls=%async_computation.2 | async-start | bytes 2097152 | tf_op jit(solution)/shard_map/all_to_all | solution.py:418
  67.5 1.3 %collective-permute-start.1 = (f32[2,8,8,128]{3,2,1,0:T(8,128)S(1)}, f32[2,8,8,128]{3,2,1,0:T(8,128)S(1)}, u32[]{:S(2)}, u32[]{:S(2)}) collective-permute-start(f32[2,8,8,128]{3,2,1,0:T(8,128)S(1)} %reduce_sum.9), channel_id=1, source_target_pairs={{0,16},{16,0},{32,48},{48,32},{64,80},{80,64},{96,112},{112,96},{1... | collective-permute-start | bytes 196616 | tf_op jit(solution)/shard_map/ppermute | solution.py:387
  68.8 8.2 %collective-permute-start.2 = (f32[2,8,8,128]{3,2,1,0:T(8,128)S(1)}, f32[2,8,8,128]{3,2,1,0:T(8,128)S(1)}, u32[]{:S(2)}, u32[]{:S(2)}) collective-permute-start(f32[2,8,8,128]{3,2,1,0:T(8,128)S(1)} %add.17), channel_id=1, source_target_pairs={{0,32},{16,240},{32,64},{48,16},{64,96},{80,48},{96,128},{112,80},... | collective-permute-start | bytes 196616 | tf_op jit(solution)/shard_map/ppermute | solution.py:387
  77.0 7.0 %collective-permute-start.3 = (f32[2,8,8,128]{3,2,1,0:T(8,128)S(1)}, f32[2,8,8,128]{3,2,1,0:T(8,128)S(1)}, u32[]{:S(2)}, u32[]{:S(2)}) collective-permute-start(f32[2,8,8,128]{3,2,1,0:T(8,128)S(1)} %add.18), channel_id=1, source_target_pairs={{0,64},{16,208},{32,96},{48,240},{64,128},{80,16},{96,160},{112,48... | collective-permute-start | bytes 196616 | tf_op jit(solution)/shard_map/ppermute | solution.py:387
  84.0 3.8 %collective-permute-start.4 = (f32[2,8,8,128]{3,2,1,0:T(8,128)S(1)}, f32[2,8,8,128]{3,2,1,0:T(8,128)S(1)}, u32[]{:S(2)}, u32[]{:S(2)}) collective-permute-start(f32[2,8,8,128]{3,2,1,0:T(8,128)S(1)} %add.19), channel_id=1, source_target_pairs={{0,48},{16,224},{32,80},{48,0},{64,112},{80,32},{96,144},{112,64},... | collective-permute-start | bytes 196616 | tf_op jit(solution)/shard_map/ppermute | solution.py:387

commit v8 on v7

--- a/solution.py
+++ b/solution.py
@@ -190,11 +190,14 @@
                 back[1, part, span, lanes] = low
     for copy in copies:
         copy.start()
-    shape = (2 * SIDE, RADIX * LANES)
-    out = over_s_inverse(back[0].reshape(shape), back[1].reshape(shape), inverse_s[...])
-    for r in range(RADIX):
-        value = out[:, r * LANES : (r + 1) * LANES]
-        terms[:, r] = value.reshape(terms.shape[0], terms.shape[2], LANES)
+    shape = (2 * SIDE, 2 * LANES)
+    for first in range(0, RADIX, 2):
+        lanes = pl.ds(first * LANES, 2 * LANES)
+        high, low = (back[half_of, :, :, lanes].reshape(shape) for half_of in range(2))
+        out = over_s_inverse(high, low, inverse_s[...])
+        for r in range(2):
+            value = out[:, r * LANES : (r + 1) * LANES]
+            terms[:, first + r] = value.reshape(terms.shape[0], terms.shape[2], LANES)
     for copy in copies:
         copy.wait()
 

time: 88.9 us -> 89.2 us (level)
  no operation moved by 1% of the time
where the time goes in v8:
time: 89.2 us; the launch traced here: 88.8 us
  blocking collectives  37.1 us (42%)
  waiting for transfers between devices  18.6 us (21%)
  Pallas kernels  16 us (18%)
  starting transfers between devices  13.5 us (15%)
  local copies, waits for them, and re-layouts  2.54 us (3%)
    all_to_all x1, blocking collectives, local(): rows = lax.all_to_all(packed, 'ctx', 0, 0, tiled=True)  37.1 us
    ppermute x4, waiting for transfers between devices, moved(): return lax.ppermute(array, 'chan', ring)  16.8 us
    pallas_call x1, Pallas kernels, input_rows(): pl.pallas_call(input_kernel, out_shape=jax.ShapeDtypeStruct(out, jnp.floa...  7.3 us
    pallas_call x1, Pallas kernels, filter_terms(): pl.pallas_call(filter_kernel, out_shape=(jax.ShapeDtypeStruct((blocks, RA...  6.42 us
    all_to_all x1, starting transfers between devices, local(): inputs = lax.all_to_all(inputs, 'ctx', 0, 0, tiled=True)  5.84 us
    all_to_all x1, starting transfers between devices, local(): terms = lax.all_to_all(terms, 'ctx', 0, 0, tiled=True)  5.36 us
    pallas_call x1, Pallas kernels, laid_out(): pl.pallas_call(layout_kernel, out_shape=jax.ShapeDtypeStruct((channels, t...  2.28 us
    ppermute x4, starting transfers between devices, moved(): return lax.ppermute(array, 'chan', ring)  2.18 us
  transfers between devices with their start and end apart: 7, of which 5 were waited for; matrix products, arithmetic and copies ran while one was open for 1% of the time, Pallas kernels for 8%

profile of v8, /device:TPU:2, one launch (start us, length us, event | category | flops | bytes accessed | tf_op | source)
XLA Modules:
  0.0 88.8 jit_solution(8284210320483085339)
XLA Ops:
  0.6 2.3 %laid_out.1 = f32[16,36,8,128]{3,2,1,0:T(8,128)S(1)} custom-call(s32[1]{0:T(128)} %bitcast.core, f32[2,16,8192]{2,1,0:T(8,128)} %saved_input.1, f32[2,16,8192]{2,1,0:T(8,128)} %out_grad.1, f32[2,8192]{1,0:T(2,128)} %filters.1), custom_call_target="tpu_custom_call" | custom-call | tf_op jit(solution)/shard_map/laid_out/pallas_call | solution.py:305
  2.9 0.0 copy-start.1
  2.9 0.0 copy-start.2
  3.0 0.0 copy-start.3
  3.0 0.0 copy-start.4
  3.0 0.0 copy-start.5
  3.0 0.0 copy-start.6
  3.0 37.1 %all_to_all.15.rows = f32[16,36,8,128]{3,2,1,0:T(8,128)S(1)} all-to-all(f32[16,36,8,128]{3,2,1,0:T(8,128)S(1)} %laid_out.1), channel_id=1, replica_groups=mesh['chan'=16,'ctx'=16] {'ctx'}, dimensions={0} | all-to-all | bytes 4718592 | tf_op jit(solution)/shard_map/all_to_all | solution.py:414
  40.1 0.0 copy-done.1
  40.1 0.0 copy-done.2
  40.1 0.0 copy-done.3
  40.1 0.0 copy-done.4
  40.1 0.0 copy-done.5
  40.1 0.0 copy-done.6
  40.1 6.4 %filter_terms.1 = (f32[16,8,8,128]{3,2,1,0:T(8,128)}, f32[4,512,256]{2,1,0:T(8,128)}, f32[16,4,8,128]{3,2,1,0:T(8,128)S(1)}) custom-call(f32[16,36,8,128]{3,2,1,0:T(8,128)S(1)} %all_to_all.15.rows, bf16[8,512,128]{2,1,0:T(8,128)(2,1)S(1)} %copy-done.2, bf16[256,256]{1,0:T(8,128)(2,1)S(1)} %copy-done.6, bf16[2,256,256]{2,1,0:T(8,128)(2,1)S(1)} %copy-done.5, ...), custom_call_target="tpu_custom_call" | custom-call | flops 4000000000 | bytes 10000000 | tf_op jit(solution)/shard_map/filter_terms/pallas_call | solution.py:325
  46.6 0.0 copy-start
  46.6 0.1 collective-permute-start
  46.7 5.4 %all-to-all-start.1 = ((f32[16,8,8,128]{3,2,1,0:T(8,128)}), f32[16,8,8,128]{3,2,1,0:T(8,128)S(1)}, u32[]{:S(2)}, u32[]{:S(2)}) async-start(f32[16,8,8,128]{3,2,1,0:T(8,128)} %get-tuple-element.11), calls=%async_computation.1 | async-start | bytes 1048576 | tf_op jit(solution)/shard_map/all_to_all | solution.py:417
  52.0 0.0 collective-permute-done.other
  52.1 0.0 copy-start.7
  52.1 0.0 copy-done
  52.1 0.7 copy-done.7
  52.8 7.3 %input_rows.1 = f32[16,2,8,8,128]{4,3,2,1,0:T(8,128)} custom-call(s32[1]{0:T(128)} %bitcast.core, f32[16,4,8,128]{3,2,1,0:T(8,128)} %copy-done, f32[16,4,8,128]{3,2,1,0:T(8,128)} %copy-done.7, f32[4,512,256]{2,1,0:T(8,128)} %get-tuple-element.10.grads, bf16[8,512,128]{2,1,0:T(8,128)(2,1)} %constant.36.clone.forward_s, ...), custom_call_target="tpu_custom_call" | custom-call | flops 2500000000 | bytes 10000000 | tf_op jit(solution)/shard_map/input_rows/pallas_call | solution.py:353
  60.1 1.9 %all-to-all-done.1 = f32[16,8,8,128]{3,2,1,0:T(8,128)S(1)} async-done(((f32[16,8,8,128]{3,2,1,0:T(8,128)}), f32[16,8,8,128]{3,2,1,0:T(8,128)S(1)}, u32[]{:S(2)}, u32[]{:S(2)}) %all-to-all-start.1) | async-done | bytes 524320 | tf_op jit(solution)/shard_map/all_to_all | solution.py:417
  62.0 5.8 %all-to-all-start.2 = ((f32[16,2,8,8,128]{4,3,2,1,0:T(8,128)}), f32[16,2,8,8,128]{4,3,2,1,0:T(8,128)S(1)}, u32[]{:S(2)}, u32[]{:S(2)}) async-start(f32[16,2,8,8,128]{4,3,2,1,0:T(8,128)} %input_rows.1), calls=%async_computation.2 | async-start | bytes 2097152 | tf_op jit(solution)/shard_map/all_to_all | solution.py:421
  67.8 0.0 collective-permute-start.1
  67.8 1.2 %collective-permute-done.1 = f32[2,8,8,128]{3,2,1,0:T(8,128)S(1)} collective-permute-done((f32[2,8,8,128]{3,2,1,0:T(8,128)S(1)}, f32[2,8,8,128]{3,2,1,0:T(8,128)S(1)}, u32[]{:S(2)}, u32[]{:S(2)}) %collective-permute-start.1) | collective-permute-done | bytes 65568 | tf_op jit(solution)/shard_map/ppermute | solution.py:390
  69.1 2.0 %collective-permute-start.2 = (f32[2,8,8,128]{3,2,1,0:T(8,128)S(1)}, f32[2,8,8,128]{3,2,1,0:T(8,128)S(1)}, u32[]{:S(2)}, u32[]{:S(2)}) collective-permute-start(f32[2,8,8,128]{3,2,1,0:T(8,128)S(1)} %add.17), channel_id=1, source_target_pairs={{0,32},{16,240},{32,64},{48,16},{64,96},{80,48},{96,128},{112,80},... | collective-permute-start | bytes 196616 | tf_op jit(solution)/shard_map/ppermute | solution.py:390
  71.1 6.2 %collective-permute-done.2 = f32[2,8,8,128]{3,2,1,0:T(8,128)S(1)} collective-permute-done((f32[2,8,8,128]{3,2,1,0:T(8,128)S(1)}, f32[2,8,8,128]{3,2,1,0:T(8,128)S(1)}, u32[]{:S(2)}, u32[]{:S(2)}) %collective-permute-start.2) | collective-permute-done | bytes 65568 | tf_op jit(solution)/shard_map/ppermute | solution.py:390
  77.2 0.1 collective-permute-start.3
  77.3 6.9 %collective-permute-done.3 = f32[2,8,8,128]{3,2,1,0:T(8,128)S(1)} collective-permute-done((f32[2,8,8,128]{3,2,1,0:T(8,128)S(1)}, f32[2,8,8,128]{3,2,1,0:T(8,128)S(1)}, u32[]{:S(2)}, u32[]{:S(2)}) %collective-permute-start.3) | collective-permute-done | bytes 65568 | tf_op jit(solution)/shard_map/ppermute | solution.py:390
  84.3 0.1 collective-permute-start.4
  84.4 0.0 all-to-all-done.2
  84.4 0.1 fusion
  84.5 0.1 copy.13
  84.6 1.0 %convert_element_type.11 = bf16[2,16,8192]{2,1,0:T(8,128)(2,1)} reshape(bf16[2,16,8,8,128]{4,3,2,1,0:T(8,128)(2,1)S(1)} %copy.13) | data formatting | bytes 1048576 | tf_op jit(solution)/shard_map/convert_element_type | solution.py:423
  85.6 2.4 %collective-permute-done.4 = f32[2,8,8,128]{3,2,1,0:T(8,128)S(1)} collective-permute-done((f32[2,8,8,128]{3,2,1,0:T(8,128)S(1)}, f32[2,8,8,128]{3,2,1,0:T(8,128)S(1)}, u32[]{:S(2)}, u32[]{:S(2)}) %collective-permute-start.4) | collective-permute-done | bytes 65568 | tf_op jit(solution)/shard_map/ppermute | solution.py:390
  88.1 0.7 copy.18
  (6 shorter events, 0.1 us)
Async XLA Ops:
  2.9 37.2 %copy-start.1 = (f32[8,2,128,128]{3,2,1,0:T(8,128)S(1)}, f32[8,2,128,128]{3,2,1,0:T(8,128)}, u32[]{:S(2)}) copy-start(f32[8,2,128,128]{3,2,1,0:T(8,128)} %constant.41.clone.over_l) | copy-start | bytes 3145732
  2.9 37.2 %copy-start.2 = (bf16[8,512,128]{2,1,0:T(8,128)(2,1)S(1)}, bf16[8,512,128]{2,1,0:T(8,128)(2,1)}, u32[]{:S(2)}) copy-start(bf16[8,512,128]{2,1,0:T(8,128)(2,1)} %constant.36.clone.forward_s) | copy-start | bytes 3145732
  3.0 37.2 %copy-start.3 = (f32[8,2,128,128]{3,2,1,0:T(8,128)S(1)}, f32[8,2,128,128]{3,2,1,0:T(8,128)}, u32[]{:S(2)}) copy-start(f32[8,2,128,128]{3,2,1,0:T(8,128)} %constant.40.clone.over_r) | copy-start | bytes 3145732
  3.0 37.2 %copy-start.4 = (bf16[2,256,256]{2,1,0:T(8,128)(2,1)S(1)}, bf16[2,256,256]{2,1,0:T(8,128)(2,1)}, u32[]{:S(2)}) copy-start(bf16[2,256,256]{2,1,0:T(8,128)(2,1)} %constant.39.clone.inverse_l) | copy-start | bytes 786436
  3.0 37.2 %copy-start.5 = (bf16[2,256,256]{2,1,0:T(8,128)(2,1)S(1)}, bf16[2,256,256]{2,1,0:T(8,128)(2,1)}, u32[]{:S(2)}) copy-start(bf16[2,256,256]{2,1,0:T(8,128)(2,1)} %constant.38.clone.forward_l) | copy-start | bytes 786436
  3.0 37.2 %copy-start.6 = (bf16[256,256]{1,0:T(8,128)(2,1)S(1)}, bf16[256,256]{1,0:T(8,128)(2,1)}, u32[]{:S(2)}) copy-start(bf16[256,256]{1,0:T(8,128)(2,1)} %constant.43.inverse_s) | copy-start | bytes 393220
  46.6 5.5 %copy-start = (f32[16,4,8,128]{3,2,1,0:T(8,128)}, f32[16,4,8,128]{3,2,1,0:T(8,128)S(1)}, u32[]{:S(2)}) copy-start(f32[16,4,8,128]{3,2,1,0:T(8,128)S(1)} %get-tuple-element.9.mine) | copy-start | bytes 786436
  46.6 5.5 %collective-permute-start = (f32[16,4,8,128]{3,2,1,0:T(8,128)S(1)}, f32[16,4,8,128]{3,2,1,0:T(8,128)S(1)}, u32[]{:S(2)}, u32[]{:S(2)}) collective-permute-start(f32[16,4,8,128]{3,2,1,0:T(8,128)S(1)} %get-tuple-element.9.mine), channel_id=1, source_target_pairs={{0,16},{16,0},{32,48},{48,32},{64,80},{80,64},{96,112},{112,96},{1... | collective-permute-start | bytes 786440 | tf_op jit(solution)/shard_map/ppermute | solution.py:416
  46.7 15.2 %all-to-all-start.1 = ((f32[16,8,8,128]{3,2,1,0:T(8,128)}), f32[16,8,8,128]{3,2,1,0:T(8,128)S(1)}, u32[]{:S(2)}, u32[]{:S(2)}) async-start(f32[16,8,8,128]{3,2,1,0:T(8,128)} %get-tuple-element.11), calls=%async_computation.1 | async-start | bytes 1048576 | tf_op jit(solution)/shard_map/all_to_all | solution.py:417
  52.1 0.7 copy-start.7
  62.0 22.4 %all-to-all-start.2 = ((f32[16,2,8,8,128]{4,3,2,1,0:T(8,128)}), f32[16,2,8,8,128]{4,3,2,1,0:T(8,128)S(1)}, u32[]{:S(2)}, u32[]{:S(2)}) async-start(f32[16,2,8,8,128]{4,3,2,1,0:T(8,128)} %input_rows.1), calls=%async_computation.2 | async-start | bytes 2097152 | tf_op jit(solution)/shard_map/all_to_all | solution.py:421
  67.8 1.3 %collective-permute-start.1 = (f32[2,8,8,128]{3,2,1,0:T(8,128)S(1)}, f32[2,8,8,128]{3,2,1,0:T(8,128)S(1)}, u32[]{:S(2)}, u32[]{:S(2)}) collective-permute-start(f32[2,8,8,128]{3,2,1,0:T(8,128)S(1)} %reduce_sum.9), channel_id=1, source_target_pairs={{0,16},{16,0},{32,48},{48,32},{64,80},{80,64},{96,112},{112,96},{1... | collective-permute-start | bytes 196616 | tf_op jit(solution)/shard_map/ppermute | solution.py:390
  69.1 8.2 %collective-permute-start.2 = (f32[2,8,8,128]{3,2,1,0:T(8,128)S(1)}, f32[2,8,8,128]{3,2,1,0:T(8,128)S(1)}, u32[]{:S(2)}, u32[]{:S(2)}) collective-permute-start(f32[2,8,8,128]{3,2,1,0:T(8,128)S(1)} %add.17), channel_id=1, source_target_pairs={{0,32},{16,240},{32,64},{48,16},{64,96},{80,48},{96,128},{112,80},... | collective-permute-start | bytes 196616 | tf_op jit(solution)/shard_map/ppermute | solution.py:390
  77.2 7.0 %collective-permute-start.3 = (f32[2,8,8,128]{3,2,1,0:T(8,128)S(1)}, f32[2,8,8,128]{3,2,1,0:T(8,128)S(1)}, u32[]{:S(2)}, u32[]{:S(2)}) collective-permute-start(f32[2,8,8,128]{3,2,1,0:T(8,128)S(1)} %add.18), channel_id=1, source_target_pairs={{0,64},{16,208},{32,96},{48,240},{64,128},{80,16},{96,160},{112,48... | collective-permute-start | bytes 196616 | tf_op jit(solution)/shard_map/ppermute | solution.py:390
  84.3 3.8 %collective-permute-start.4 = (f32[2,8,8,128]{3,2,1,0:T(8,128)S(1)}, f32[2,8,8,128]{3,2,1,0:T(8,128)S(1)}, u32[]{:S(2)}, u32[]{:S(2)}) collective-permute-start(f32[2,8,8,128]{3,2,1,0:T(8,128)S(1)} %add.19), channel_id=1, source_target_pairs={{0,48},{16,224},{32,80},{48,0},{64,112},{80,32},{96,144},{112,64},... | collective-permute-start | bytes 196616 | tf_op jit(solution)/shard_map/ppermute | solution.py:390
